TPU v7x, 32 devices: a whole 2x2x4 slice. The times are simulated.
32 devices in a mesh: feat: 8 (over y, x, core), rep: 4 (over z).
Axes of the slice: x: 2, y: 2, z: 4, core: 2. Of those that a mesh axis runs over, the one named last changes fastest.
Arguments:
- feats: bfloat16 [4, 2048, 1024], P('rep', None, 'feat'), may hold values from -6 to 6
- w_self: bfloat16 [1024, 256], P('feat'), may hold values from -0.1875 to 0.1875
- w_neigh: bfloat16 [1024, 256], P('feat'), may hold values from -0.1875 to 0.1875
- bias: float32 [256], replicated, may hold values from -3 to 3
- tile_weight: bfloat16 [4, 8, 3, 128, 128], P('rep'), may hold values from -0.375 to 0.375
- tile_src: int32 [4, 8, 3], P('rep'), may hold values from 0 to 15
- tile_count: int32 [4, 8], P('rep'), may hold values from 1 to 3
- owner_order: int32 [4, 8], P('rep'), may hold values from 0 to 7, each once within a row
- cotangent: bfloat16 [4, 1024, 256], P('rep', 'feat'), may hold values from -6 to 6
Outputs:
- hidden: bfloat16 [4, 1024, 256], P('rep', 'feat')
- grad_self: float32 [1024, 256], P('feat')
- grad_neigh: float32 [1024, 256], P('feat')
All inputs are finite; a program needn't handle non-finite values.
Results may differ from a plain program's by a relative error of at most 0.0055.
Values may be sent and summed in bfloat16 or wider, within the bound.
No kernel may reach another device: no remote copies, remote signals or barrier semaphores. Data moves between devices by JAX's collectives and lax.ppermute only.
A program may use at most 64 MiB of HBM per device.

v0:
```python
import jax
import jax.numpy as jnp
from jax import lax
from jax.sharding import PartitionSpec as P


def transposed_product(left, right):
    return lax.dot_general(
        left, right, (((0,), (0,)), ((), ())), preferred_element_type=jnp.float32
    )


def body(feats, w_self, w_neigh, bias, tile_weight, tile_src, tile_count, owner_order, cotangent):
    block_rows = tile_weight.shape[3]
    tile_slots = tile_weight.shape[2]
    columns = feats.shape[2]
    by_block = feats[0].reshape(-1, block_rows, columns)
    in_use = jnp.arange(tile_slots)[None, :] < tile_count[0][:, None]
    masked = jnp.where(in_use[:, :, None, None], tile_weight[0], jnp.zeros((), jnp.bfloat16))
    sources = by_block[tile_src[0]]
    aggregate = jnp.einsum(
        "bkij,bkjc->bic", masked, sources, preferred_element_type=jnp.float32
    ).astype(jnp.bfloat16)
    target_rows = by_block[owner_order[0]].reshape(-1, columns)
    target_mean = aggregate[owner_order[0]].reshape(-1, columns)
    partial_sums = jnp.dot(target_rows, w_self, preferred_element_type=jnp.float32)
    partial_sums = partial_sums + jnp.dot(target_mean, w_neigh, preferred_element_type=jnp.float32)
    preact = lax.psum_scatter(partial_sums, "feat", scatter_dimension=0, tiled=True) + bias
    hidden = jax.nn.silu(preact).astype(jnp.bfloat16)
    squash = jax.nn.sigmoid(preact)
    output_grad = (
        cotangent[0].astype(jnp.float32) * squash * (1.0 + preact * (1.0 - squash))
    ).astype(jnp.bfloat16)
    pieces = lax.all_gather(output_grad, "feat", axis=0, tiled=True)
    grad_self = transposed_product(target_rows, pieces)
    grad_neigh = transposed_product(target_mean, pieces)
    grad_self, grad_neigh = lax.psum((grad_self, grad_neigh), "rep")
    return (hidden[None], grad_self, grad_neigh)


def solution(mesh):
    in_specs = (
        P("rep", None, "feat"),
        P("feat", None),
        P("feat", None),
        P(),
        P("rep", None, None, None, None),
        P("rep", None, None),
        P("rep", None),
        P("rep", None),
        P("rep", "feat", None),
    )
    out_specs = (P("rep", "feat", None), P("feat", None), P("feat", None))
    return jax.shard_map(body, mesh=mesh, in_specs=in_specs, out_specs=out_specs, check_vma=False)
```

profile of v0, /device:TPU:0, one launch (start us, length us, event | category | flops | bytes accessed | tf_op | source)
XLA Modules:
  0.0 110.9 jit_solution(8174284367922403643)
XLA Ops:
  7.2 0.0 reduce-scatter.2.cloned.1.call-start
  7.2 0.6 copy-done.8
  7.9 0.1 iota_compare_fusion
  8.0 0.6 copy-done.5
  8.6 0.1 copy.13
  8.7 0.1 reshape.130
  8.8 0.6 gather_fusion
  9.4 0.7 gather_fusion.1
  10.1 0.4 copy-done.7
  10.5 0.4 fusion
  11.0 0.6 gather_fusion.2
  11.6 0.2 copy-done.4
  11.8 0.3 fusion.9
  12.1 0.6 copy-done.2
  12.6 1.3 %convolution_add_fusion = f32[1024,256]{1,0:T(8,128)} fusion(f32[1024,256]{1,0:T(8,128)S(1)} %fusion.9, bf16[1024,128]{1,0:T(8,128)(2,1)S(1)} %bitcast.40, bf16[128,256]{1,0:T(8,128)(2,1)S(1)} %copy-done.2), kind=kOutput, calls=%fused_computation.3 | convolution fusion | flops 67371008 | bytes 2424832 | tf_op jit(solution)/shard_map/dot_general | solution.py:27
  13.9 0.0 all-reduce.3.cloned.1.call-start
  14.0 38.8 %reduce-scatter.2.cloned.1.call-done = f32[128,256]{1,0:T(8,128)} async-done(((f32[1024,256]{1,0:T(8,128)}), f32[128,256]{1,0:T(8,128)}) %reduce-scatter.2.cloned.1.call-update) | async-done | bytes 131088 | tf_op jit(solution)/shard_map/reduce_scatter | solution.py:28
  52.8 1.6 %fusion.4 = (bf16[128,256]{1,0:T(8,128)(2,1)S(1)}, bf16[1,128,256]{2,1,0:T(8,128)(2,1)}) fusion(f32[128,256]{1,0:T(8,128)} %reduce-scatter.2.cloned.1.call-done, bf16[1,128,256]{2,1,0:T(8,128)(2,1)S(1)} %copy-done.3, f32[256]{0:T(256)S(1)} %copy-done.6), kind=kLoop, calls=%fused_computation.11 | loop fusion | flops 425984 | bytes 328704 | tf_op jit(solution)/shard_map/convert_element_type | solution.py:33
  54.4 9.8 %all_gather.3 = bf16[1024,256]{1,0:T(8,128)(2,1)S(1)} all-gather(bf16[128,256]{1,0:T(8,128)(2,1)S(1)} %get-tuple-element.5), channel_id=1, replica_groups=mesh['feat'=8,'rep'=4] {'feat'}, dimensions={0}, use_global_device_ids=true | all-gather | bytes 589824 | tf_op jit(solution)/shard_map/all_gather | solution.py:34
  64.1 0.9 fusion.11
  65.1 0.9 fusion.10
  66.0 35.7 %all-reduce.3.cloned.1.call-done = (f32[128,256]{1,0:T(8,128)}, f32[128,256]{1,0:T(8,128)}) async-done(((f32[128,256]{1,0:T(8,128)}, f32[128,256]{1,0:T(8,128)}), (f32[128,256]{1,0:T(8,128)}, f32[128,256]{1,0:T(8,128)})) %all-reduce.3.cloned.1.call-update) | async-done | bytes 262160 | tf_op jit(solution)/shard_map/psum | solution.py:37
  101.8 1.6 %copy.17 = f32[128,256]{1,0:T(8,128)} copy(f32[128,256]{1,0:T(8,128)} %get-tuple-element.12) | data formatting | bytes 262144
  103.4 0.7 copy.18
  (21 shorter events, 0.1 us)
Async XLA Ops:
  7.2 1.6 %copy-start = (bf16[1,2048,128]{2,1,0:T(8,128)(2,1)S(1)}, bf16[1,2048,128]{2,1,0:T(8,128)(2,1)}, u32[]{:S(2)}) copy-start(bf16[1,2048,128]{2,1,0:T(8,128)(2,1)} %param.9) | copy-start | bytes 1572868
  7.2 0.7 copy-start.8
  7.2 45.6 %reduce-scatter.2.cloned.1.call-start = ((), (), s32[]{:S(2)}) async-start(), calls=%async_computation.1 | async-start | bytes 1179648 | tf_op jit(solution)/shard_map/reduce_scatter | solution.py:28
  7.2 0.7 copy-start.9
  7.9 0.7 copy-start.5
  9.4 1.1 %copy-start.7 = (bf16[1,8,3,128,128]{4,3,2,1,0:T(8,128)(2,1)S(1)}, bf16[1,8,3,128,128]{4,3,2,1,0:T(8,128)(2,1)}, u32[]{:S(2)}) copy-start(bf16[1,8,3,128,128]{4,3,2,1,0:T(8,128)(2,1)} %param.13) | copy-start | bytes 2359300
  10.9 0.8 copy-start.4
  11.8 0.8 copy-start.2
  13.9 38.9 %copy-start.3 = (bf16[1,128,256]{2,1,0:T(8,128)(2,1)S(1)}, bf16[1,128,256]{2,1,0:T(8,128)(2,1)}, u32[]{:S(2)}) copy-start(bf16[1,128,256]{2,1,0:T(8,128)(2,1)} %param.17) | copy-start | bytes 196612
  13.9 38.9 %copy-start.6 = (f32[256]{0:T(256)S(1)}, f32[256]{0:T(256)}, u32[]{:S(2)}) copy-start(f32[256]{0:T(256)} %param.12) | copy-start | bytes 3076
  13.9 87.9 %all-reduce.3.cloned.1.call-start = ((), (), s32[]{:S(2)}) async-start(), calls=%async_computation.2 | async-start | bytes 524288 | tf_op jit(solution)/shard_map/psum | solution.py:37
  101.8 1.6 %copy-start.1 = (f32[128,256]{1,0:T(8,128)S(1)}, f32[128,256]{1,0:T(8,128)}, u32[]{:S(2)}) copy-start(f32[128,256]{1,0:T(8,128)} %get-tuple-element.13) | copy-start | bytes 393220
Sparse Core Ops, SparseCore 0:
  14.0 38.7 reduce-scatter.1
  66.2 35.5 all-reduce.2
where the time goes:
time: 111 us
  waiting for transfers between devices  74.6 us (67%)
  between operations  14.1 us (13%)
  blocking collectives  9.76 us (9%)
  local copies, waits for them, and re-layouts  6.81 us (6%)
  matrix products  3.81 us (3%)
  other arithmetic  1.69 us (2%)
    reduce_scatter x1, waiting for transfers between devices, body(): lax.psum_scatter(partial_sums, 'feat', scatter_dimension=0, tiled=True)  38.8 us
    psum x1, waiting for transfers between devices, body(): grad_self, grad_neigh = lax.psum((grad_self, grad_neigh), 'rep')  35.7 us
    all_gather x1, blocking collectives, body(): pieces = lax.all_gather(output_grad, 'feat', axis=0, tiled=True)  9.76 us
    unnamed x22, local copies, waits for them, and re-layouts  4.75 us
  transfers between devices with their start and end apart: 2, of which 2 were waited for; matrix products, arithmetic and copies ran while one was open for 0% of the time, Pallas kernels for 0%

commit v1 on v0

v1 whole, which is shorter than its diff:
```python
import jax
import jax.numpy as jnp
from jax import lax
from jax.sharding import PartitionSpec as P


def transposed_product(left, right):
    return lax.dot_general(
        left, right, (((0,), (0,)), ((), ())), preferred_element_type=jnp.float32
    )


def exchange(value, axis, size, flip):
    return lax.ppermute(value, axis, [(i, i ^ flip) for i in range(size)])


def body(n_feat, n_rep, feats, w_self, w_neigh, bias, tile_weight, tile_src, tile_count, owner_order, cotangent):
    block_rows = tile_weight.shape[3]
    tile_slots = tile_weight.shape[2]
    columns = feats.shape[2]
    hidden_units = w_self.shape[1]
    n_chip = n_feat // 2
    me = lax.axis_index("feat")
    core, chip = me % 2, me // 2
    flips = jnp.arange(n_chip, dtype=jnp.int32)
    places = 2 * (chip ^ flips)
    order = owner_order[0]
    kept, given = order[places + core], order[places + 1 - core]
    blocks = jnp.concatenate([given, kept])

    by_block = feats[0].reshape(-1, block_rows, columns)
    in_use = jnp.arange(tile_slots)[None, :] < tile_count[0][blocks][:, None]
    masked = jnp.where(in_use[:, :, None, None], tile_weight[0][blocks], jnp.zeros((), jnp.bfloat16))
    sources = by_block[tile_src[0][blocks]]
    target_mean = jnp.einsum(
        "bkij,bkjc->bic", masked, sources, preferred_element_type=jnp.float32
    ).astype(jnp.bfloat16)
    target_rows = by_block[blocks]
    both = jnp.concatenate([target_rows, target_mean], axis=2).reshape(-1, 2 * columns)
    weights = jnp.concatenate([w_self, w_neigh], axis=0)
    half = n_chip * block_rows
    partial_sums = jnp.dot(both, weights, preferred_element_type=jnp.float32)

    from_core = exchange(partial_sums[:half].astype(jnp.bfloat16), "feat", n_feat, 1)
    chip_sums = (partial_sums[half:] + from_core.astype(jnp.float32)).reshape(n_chip, block_rows, hidden_units)
    preact = chip_sums[0] + bias
    for j in reversed(range(1, n_chip)):
        got = exchange(chip_sums[j].astype(jnp.bfloat16), "feat", n_feat, 2 * j)
        preact = preact + got.astype(jnp.float32)
    squash = jax.nn.sigmoid(preact)
    hidden = (preact * squash).astype(jnp.bfloat16)
    output_grad = (
        cotangent[0].astype(jnp.float32) * squash * (1.0 + preact * (1.0 - squash))
    ).astype(jnp.bfloat16)

    own = [output_grad] + [exchange(output_grad, "feat", n_feat, 2 * j) for j in range(1, n_chip)]
    own = jnp.concatenate(own, axis=0)
    other = exchange(own, "feat", n_feat, 1)
    grads = transposed_product(both[half:], own) + transposed_product(both[:half], other)

    flip = 1
    while flip < n_rep:
        sent = lax.optimization_barrier(grads.astype(jnp.bfloat16))
        got = exchange(sent, "rep", n_rep, flip)
        grads = sent.astype(jnp.float32) + got.astype(jnp.float32)
        flip *= 2
    return (hidden[None], grads[:columns], grads[columns:])


def solution(mesh):
    n_feat, n_rep = mesh.shape["feat"], mesh.shape["rep"]

    def local(*args):
        return body(n_feat, n_rep, *args)

    in_specs = (
        P("rep", None, "feat"),
        P("feat", None),
        P("feat", None),
        P(),
        P("rep", None, None, None, None),
        P("rep", None, None),
        P("rep", None),
        P("rep", None),
        P("rep", "feat", None),
    )
    out_specs = (P("rep", "feat", None), P("feat", None), P("feat", None))
    return jax.shard_map(local, mesh=mesh, in_specs=in_specs, out_specs=out_specs, check_vma=False)
```

time: 111 us -> 45.4 us (0.41)
  waiting for transfers between devices: 74.6 us -> 20 us
  between operations: 14.1 us -> 0.89 us
  starting transfers between devices: 0.08 us -> 12.9 us
  blocking collectives: 9.76 us -> 0 us
  matrix products: 3.81 us -> 1.34 us
  local copies, waits for them, and re-layouts: 6.81 us -> 8.87 us
    reduce_scatter x1 -> x0, waiting for transfers between devices: 38.8 us -> none  [body(): lax.psum_scatter(partial_sums, 'feat', scatter_dimension=0, tiled=True)]
    psum x1 -> x0, waiting for transfers between devices: 35.7 us -> none  [body(): grad_self, grad_neigh = lax.psum((grad_self, grad_neigh), 'rep')]
    ppermute x0 -> x10, waiting for transfers between devices: none -> 20 us  [exchange(): return lax.ppermute(value, axis, [(i, i ^ flip) for i in range(size)])]
    ppermute x0 -> x10, starting transfers between devices: none -> 12.9 us  [exchange(): return lax.ppermute(value, axis, [(i, i ^ flip) for i in range(size)])]
    all_gather x1 -> x0, blocking collectives: 9.76 us -> none  [body(): pieces = lax.all_gather(output_grad, 'feat', axis=0, tiled=True)]
    gather x3 -> x9, local copies, waits for them, and re-layouts: 1.89 us -> 4.73 us  [the longest x3 1.34 us: body(): sources = by_block[tile_src[0][blocks]]]
    unnamed x22 -> x18, local copies, waits for them, and re-layouts: 4.75 us -> 2.63 us
    dot_general x2, matrix products: 1.87 us -> 0.53 us  [transposed_product(): lax.dot_general(left, right, (((0,), (0,)), ((), ())), preferred_element_...]
  transfers between devices with their start and end apart: 2 -> 10, of which waited for: 2 -> 10; matrix products, arithmetic and copies ran while one was open for 0% -> 1% of each run, Pallas kernels for 0% -> 0%
where the time goes in v1:
time: 45.4 us; the launch traced here: 45.2 us
  waiting for transfers between devices  20 us (44%)
  starting transfers between devices  12.9 us (28%)
  local copies, waits for them, and re-layouts  8.87 us (20%)
  matrix products  1.34 us (3%)
  other arithmetic  1.15 us (3%)
  between operations  0.89 us (2%)
    ppermute x10, waiting for transfers between devices, exchange(): return lax.ppermute(value, axis, [(i, i ^ flip) for i in range(size)])  20 us
    ppermute x10, starting transfers between devices, exchange(): return lax.ppermute(value, axis, [(i, i ^ flip) for i in range(size)])  12.9 us
    unnamed x18, local copies, waits for them, and re-layouts  2.63 us
    gather x3, local copies, waits for them, and re-layouts, body(): sources = by_block[tile_src[0][blocks]]  1.34 us
    gather x2, local copies, waits for them, and re-layouts, body(): kept, given = (order[places + core], order[places + 1 - core])  1.28 us
  transfers between devices with their start and end apart: 10, of which 10 were waited for; matrix products, arithmetic and copies ran while one was open for 1% of the time, Pallas kernels for 0%

profile of v1, /device:TPU:0, one launch (start us, length us, event | category | flops | bytes accessed | tf_op | source)
XLA Modules:
  0.0 45.2 jit_solution(5721688185107814077)
XLA Ops:
  0.7 0.7 %copy-done.1 = s32[1,8]{1,0:T(1,128)S(1)} copy-done((s32[1,8]{1,0:T(1,128)S(1)}, s32[1,8]{1,0:T(1,128)}, u32[]{:S(2)}) %copy-start.1) | copy-done | bytes 56
  1.4 0.6 %gather_fusion = s32[4]{0:T(128)S(1)} fusion(s32[8]{0:T(128)S(1)} %bitcast.39, s32[1024]{0:T(1024)S(1)} %pad_clamp_fusion.4), kind=kCustom, calls=%fused_computation | custom fusion | bytes 48 | tf_op jit(solution)/shard_map/gather | solution.py:28
  2.1 0.6 %gather_fusion.1 = s32[4]{0:T(128)S(1)} fusion(s32[8]{0:T(128)S(1)} %bitcast.40, s32[1024]{0:T(1024)S(1)} %pad_clamp_fusion.3), kind=kCustom, calls=%fused_computation.1 | custom fusion | bytes 48 | tf_op jit(solution)/shard_map/gather | solution.py:28
  2.8 0.6 %copy-done.2 = s32[1,8]{1,0:T(1,128)S(1)} copy-done((s32[1,8]{1,0:T(1,128)S(1)}, s32[1,8]{1,0:T(1,128)}, u32[]{:S(2)}) %copy-start.2) | copy-done | bytes 56
  3.5 0.6 %gather_fusion.3 = s32[8]{0:T(128)S(1)} fusion(s32[8]{0:T(128)S(1)} %bitcast.41, s32[1024]{0:T(1024)S(1)} %pad_clamp_fusion.1), kind=kCustom, calls=%fused_computation.3 | custom fusion | bytes 96 | tf_op jit(solution)/shard_map/gather | solution.py:32
  4.2 0.6 %copy-done.7 = s32[1,8,3]{1,0,2:T(1,128)S(1)} copy-done((s32[1,8,3]{1,0,2:T(1,128)S(1)}, s32[1,8,3]{1,0,2:T(1,128)}, u32[]{:S(2)}) %copy-start.7) | copy-done | bytes 120
  6.5 0.7 %gather_fusion.6 = bf16[24,128,128]{2,1,0:T(8,128)(2,1)S(1)} fusion(bf16[16,128,128]{2,1,0:T(8,128)(2,1)S(1)} %bitcast.43, s32[1024]{0:T(1024)S(1)} %pad_clamp_fusion), kind=kCustom, calls=%fused_computation.6 | custom fusion | bytes 1572960 | tf_op jit(solution)/shard_map/gather | solution.py:34
  7.2 0.7 %gather_fusion.4 = bf16[8,3,128,128]{3,2,1,0:T(8,128)(2,1)S(1)} fusion(bf16[8,3,128,128]{3,2,1,0:T(8,128)(2,1)S(1)} %bitcast.38, s32[1024]{0:T(1024)S(1)} %pad_clamp_fusion.1), kind=kCustom, calls=%fused_computation.4 | custom fusion | bytes 1572896 | tf_op jit(solution)/shard_map/gather | solution.py:33
  8.7 0.6 %copy-done.5 = bf16[128,256]{1,0:T(8,128)(2,1)S(1)} copy-done((bf16[128,256]{1,0:T(8,128)(2,1)S(1)}, bf16[128,256]{1,0:T(8,128)(2,1)}, u32[]{:S(2)}) %copy-start.5) | copy-done | bytes 65560
  10.2 1.2 %collective-permute-done = bf16[512,256]{1,0:T(8,128)(2,1)S(1)} collective-permute-done((bf16[512,256]{1,0:T(8,128)(2,1)S(1)}, bf16[512,256]{1,0:T(8,128)(2,1)S(1)}, u32[]{:S(2)}, u32[]{:S(2)}) %collective-permute-start) | collective-permute-done | bytes 262176 | tf_op jit(solution)/shard_map/ppermute | solution.py:14
  11.5 3.9 %collective-permute-start.1 = (bf16[128,256]{1,0:T(8,128)(2,1)S(1)}, bf16[128,256]{1,0:T(8,128)(2,1)S(1)}, u32[]{:S(2)}, u32[]{:S(2)}) collective-permute-start(bf16[128,256]{1,0:T(8,128)(2,1)S(1)} %get-tuple-element.11), channel_id=1, source_target_pairs={{0,24},{4,28},{8,16},{12,20},{16,8},{20,12},{24,0},{28,4},{1,25},{... | collective-permute-start | bytes 196616 | tf_op jit(solution)/shard_map/ppermute | solution.py:14
  16.0 1.7 %collective-permute-done.1 = bf16[128,256]{1,0:T(8,128)(2,1)S(1)} collective-permute-done((bf16[128,256]{1,0:T(8,128)(2,1)S(1)}, bf16[128,256]{1,0:T(8,128)(2,1)S(1)}, u32[]{:S(2)}, u32[]{:S(2)}) %collective-permute-start.1) | collective-permute-done | bytes 65568 | tf_op jit(solution)/shard_map/ppermute | solution.py:14
  17.8 1.9 %collective-permute-done.3 = bf16[128,256]{1,0:T(8,128)(2,1)S(1)} collective-permute-done((bf16[128,256]{1,0:T(8,128)(2,1)S(1)}, bf16[128,256]{1,0:T(8,128)(2,1)S(1)}, u32[]{:S(2)}, u32[]{:S(2)}) %collective-permute-start.3) | collective-permute-done | bytes 65568 | tf_op jit(solution)/shard_map/ppermute | solution.py:14
  20.2 0.7 %fusion.15 = (bf16[128,256]{1,0:T(8,128)(2,1)S(1)}, bf16[1,128,256]{2,1,0:T(8,128)(2,1)}) fusion(bf16[1,128,256]{2,1,0:T(8,128)(2,1)S(1)} %copy-done.4, bf16[128,256]{1,0:T(8,128)(2,1)S(1)} %collective-permute-done.3, bf16[128,256]{1,0:T(8,128)(2,1)S(1)} %collective-permute-done.2, bf16[128,256]{1,0:T(8,128)(2,1)S(1)} %collective-permute-done.1, ...), kind=kLoop, calls=%fused_computation.36 | loop fusion | flops 622592 | bytes 525312 | tf_op jit(solution)/shard_map/convert_element_type | solution.py:54
  20.9 1.6 %collective-permute-start.6 = (bf16[128,256]{1,0:T(8,128)(2,1)S(1)}, bf16[128,256]{1,0:T(8,128)(2,1)S(1)}, u32[]{:S(2)}, u32[]{:S(2)}) collective-permute-start(bf16[128,256]{1,0:T(8,128)(2,1)S(1)} %get-tuple-element.5), channel_id=1, source_target_pairs={{0,24},{4,28},{8,16},{12,20},{16,8},{20,12},{24,0},{28,4},{1,25},{... | collective-permute-start | bytes 196616 | tf_op jit(solution)/shard_map/ppermute | solution.py:14
  22.5 1.3 %collective-permute-start.5 = (bf16[128,256]{1,0:T(8,128)(2,1)S(1)}, bf16[128,256]{1,0:T(8,128)(2,1)S(1)}, u32[]{:S(2)}, u32[]{:S(2)}) collective-permute-start(bf16[128,256]{1,0:T(8,128)(2,1)S(1)} %get-tuple-element.5), channel_id=1, source_target_pairs={{0,16},{4,20},{8,24},{12,28},{16,0},{20,4},{24,8},{28,12},{1,17},{... | collective-permute-start | bytes 196616 | tf_op jit(solution)/shard_map/ppermute | solution.py:14
  24.4 2.4 %collective-permute-done.6 = bf16[128,256]{1,0:T(8,128)(2,1)S(1)} collective-permute-done((bf16[128,256]{1,0:T(8,128)(2,1)S(1)}, bf16[128,256]{1,0:T(8,128)(2,1)S(1)}, u32[]{:S(2)}, u32[]{:S(2)}) %collective-permute-start.6) | collective-permute-done | bytes 65568 | tf_op jit(solution)/shard_map/ppermute | solution.py:14
  27.1 1.0 %collective-permute-done.4 = bf16[128,256]{1,0:T(8,128)(2,1)S(1)} collective-permute-done((bf16[128,256]{1,0:T(8,128)(2,1)S(1)}, bf16[128,256]{1,0:T(8,128)(2,1)S(1)}, u32[]{:S(2)}, u32[]{:S(2)}) %collective-permute-start.4) | collective-permute-done | bytes 65568 | tf_op jit(solution)/shard_map/ppermute | solution.py:14
  28.6 1.2 %collective-permute-done.7 = bf16[512,256]{1,0:T(8,128)(2,1)S(1)} collective-permute-done((bf16[512,256]{1,0:T(8,128)(2,1)S(1)}, bf16[512,256]{1,0:T(8,128)(2,1)S(1)}, u32[]{:S(2)}, u32[]{:S(2)}) %collective-permute-start.7) | collective-permute-done | bytes 262176 | tf_op jit(solution)/shard_map/ppermute | solution.py:14
  30.3 1.6 %collective-permute-start.8 = (bf16[256,256]{1,0:T(8,128)(2,1)S(1)}, bf16[256,256]{1,0:T(8,128)(2,1)S(1)}, u32[]{:S(2)}, u32[]{:S(2)}) collective-permute-start(bf16[256,256]{1,0:T(8,128)(2,1)S(1)} %fusion.1), channel_id=1, source_target_pairs={{0,1},{1,0},{2,3},{3,2},{4,5},{5,4},{6,7},{7,6},{8,9},{9,8},{10,11... | collective-permute-start | bytes 393224 | tf_op jit(solution)/shard_map/ppermute | solution.py:14
  31.9 4.0 %collective-permute-done.8 = bf16[256,256]{1,0:T(8,128)(2,1)S(1)} collective-permute-done((bf16[256,256]{1,0:T(8,128)(2,1)S(1)}, bf16[256,256]{1,0:T(8,128)(2,1)S(1)}, u32[]{:S(2)}, u32[]{:S(2)}) %collective-permute-start.8) | collective-permute-done | bytes 131104 | tf_op jit(solution)/shard_map/ppermute | solution.py:14
  35.9 2.7 %collective-permute-start.9 = (bf16[256,256]{1,0:T(8,128)(2,1)S(1)}, bf16[256,256]{1,0:T(8,128)(2,1)S(1)}, u32[]{:S(2)}, u32[]{:S(2)}) collective-permute-start(bf16[256,256]{1,0:T(8,128)(2,1)S(1)} %add_convert_fusion), channel_id=1, source_target_pairs={{0,2},{1,3},{2,0},{3,1},{4,6},{5,7},{6,4},{7,5},{8,10},{9,11},{10,... | collective-permute-start | bytes 393224 | tf_op jit(solution)/shard_map/ppermute | solution.py:14
  38.6 5.8 %collective-permute-done.9 = bf16[256,256]{1,0:T(8,128)(2,1)S(1)} collective-permute-done((bf16[256,256]{1,0:T(8,128)(2,1)S(1)}, bf16[256,256]{1,0:T(8,128)(2,1)S(1)}, u32[]{:S(2)}, u32[]{:S(2)}) %collective-permute-start.9) | collective-permute-done | bytes 131104 | tf_op jit(solution)/shard_map/ppermute | solution.py:14
  44.4 0.7 %fusion.24 = (f32[128,256]{1,0:T(8,128)}, f32[128,256]{1,0:T(8,128)}) fusion(f32[256,256]{1,0:T(8,128)S(1)} %convert_add_fusion), kind=kLoop, calls=%fused_computation.60 | loop fusion | bytes 524288 | tf_op jit(solution)/shard_map/slice | solution.py:67
  (52 shorter events, 6.7 us)
Async XLA Ops:
  0.6 6.6 %copy-start = (bf16[1,8,3,128,128]{4,3,2,1,0:T(8,128)(2,1)S(1)}, bf16[1,8,3,128,128]{4,3,2,1,0:T(8,128)(2,1)}, u32[]{:S(2)}) copy-start(bf16[1,8,3,128,128]{4,3,2,1,0:T(8,128)(2,1)} %param.13) | copy-start | bytes 2359300
  0.7 0.7 %copy-start.1 = (s32[1,8]{1,0:T(1,128)S(1)}, s32[1,8]{1,0:T(1,128)}, u32[]{:S(2)}) copy-start(s32[1,8]{1,0:T(1,128)} %param.16) | copy-start | bytes 100
  2.1 3.6 %copy-start.3 = (bf16[1,2048,128]{2,1,0:T(8,128)(2,1)S(1)}, bf16[1,2048,128]{2,1,0:T(8,128)(2,1)}, u32[]{:S(2)}) copy-start(bf16[1,2048,128]{2,1,0:T(8,128)(2,1)} %param.9) | copy-start | bytes 1572868
  2.8 0.7 %copy-start.2 = (s32[1,8]{1,0:T(1,128)S(1)}, s32[1,8]{1,0:T(1,128)}, u32[]{:S(2)}) copy-start(s32[1,8]{1,0:T(1,128)} %param.15) | copy-start | bytes 100
  4.1 0.7 %copy-start.7 = (s32[1,8,3]{1,0,2:T(1,128)S(1)}, s32[1,8,3]{1,0,2:T(1,128)}, u32[]{:S(2)}) copy-start(s32[1,8,3]{1,0,2:T(1,128)} %param.14) | copy-start | bytes 292
  8.5 0.8 %copy-start.5 = (bf16[128,256]{1,0:T(8,128)(2,1)S(1)}, bf16[128,256]{1,0:T(8,128)(2,1)}, u32[]{:S(2)}) copy-start(bf16[128,256]{1,0:T(8,128)(2,1)} %param.11) | copy-start | bytes 196612
  8.5 0.9 %copy-start.6 = (bf16[128,256]{1,0:T(8,128)(2,1)S(1)}, bf16[128,256]{1,0:T(8,128)(2,1)}, u32[]{:S(2)}) copy-start(bf16[128,256]{1,0:T(8,128)(2,1)} %param.10) | copy-start | bytes 196612
  9.7 1.7 %collective-permute-start = (bf16[512,256]{1,0:T(8,128)(2,1)S(1)}, bf16[512,256]{1,0:T(8,128)(2,1)S(1)}, u32[]{:S(2)}, u32[]{:S(2)}) collective-permute-start(bf16[512,256]{1,0:T(8,128)(2,1)S(1)} %slice.107), channel_id=1, source_target_pairs={{0,4},{4,0},{8,12},{12,8},{16,20},{20,16},{24,28},{28,24},{1,5},{5... | collective-permute-start | bytes 786440 | tf_op jit(solution)/shard_map/ppermute | solution.py:14
  11.4 8.7 %copy-start.4 = (bf16[1,128,256]{2,1,0:T(8,128)(2,1)S(1)}, bf16[1,128,256]{2,1,0:T(8,128)(2,1)}, u32[]{:S(2)}) copy-start(bf16[1,128,256]{2,1,0:T(8,128)(2,1)} %param.17) | copy-start | bytes 196612
  11.5 6.3 %collective-permute-start.1 = (bf16[128,256]{1,0:T(8,128)(2,1)S(1)}, bf16[128,256]{1,0:T(8,128)(2,1)S(1)}, u32[]{:S(2)}, u32[]{:S(2)}) collective-permute-start(bf16[128,256]{1,0:T(8,128)(2,1)S(1)} %get-tuple-element.11), channel_id=1, source_target_pairs={{0,24},{4,28},{8,16},{12,20},{16,8},{20,12},{24,0},{28,4},{1,25},{... | collective-permute-start | bytes 196616 | tf_op jit(solution)/shard_map/ppermute | solution.py:14
  15.4 4.3 %collective-permute-start.3 = (bf16[128,256]{1,0:T(8,128)(2,1)S(1)}, bf16[128,256]{1,0:T(8,128)(2,1)S(1)}, u32[]{:S(2)}, u32[]{:S(2)}) collective-permute-start(bf16[128,256]{1,0:T(8,128)(2,1)S(1)} %get-tuple-element.12), channel_id=1, source_target_pairs={{0,8},{4,12},{8,0},{12,4},{16,24},{20,28},{24,16},{28,20},{1,9},{5... | collective-permute-start | bytes 196616 | tf_op jit(solution)/shard_map/ppermute | solution.py:14
  15.9 4.3 %copy-start.8 = (f32[256]{0:T(256)S(1)}, f32[256]{0:T(256)}, u32[]{:S(2)}) copy-start(f32[256]{0:T(256)} %param.12) | copy-start | bytes 3076
  15.9 4.3 %collective-permute-start.2 = (bf16[128,256]{1,0:T(8,128)(2,1)S(1)}, bf16[128,256]{1,0:T(8,128)(2,1)S(1)}, u32[]{:S(2)}, u32[]{:S(2)}) collective-permute-start(bf16[128,256]{1,0:T(8,128)(2,1)S(1)} %get-tuple-element.13), channel_id=1, source_target_pairs={{0,16},{4,20},{8,24},{12,28},{16,0},{20,4},{24,8},{28,12},{1,17},{... | collective-permute-start | bytes 196616 | tf_op jit(solution)/shard_map/ppermute | solution.py:14
  20.9 5.9 %collective-permute-start.6 = (bf16[128,256]{1,0:T(8,128)(2,1)S(1)}, bf16[128,256]{1,0:T(8,128)(2,1)S(1)}, u32[]{:S(2)}, u32[]{:S(2)}) collective-permute-start(bf16[128,256]{1,0:T(8,128)(2,1)S(1)} %get-tuple-element.5), channel_id=1, source_target_pairs={{0,24},{4,28},{8,16},{12,20},{16,8},{20,12},{24,0},{28,4},{1,25},{... | collective-permute-start | bytes 196616 | tf_op jit(solution)/shard_map/ppermute | solution.py:14
  22.5 4.6 %collective-permute-start.5 = (bf16[128,256]{1,0:T(8,128)(2,1)S(1)}, bf16[128,256]{1,0:T(8,128)(2,1)S(1)}, u32[]{:S(2)}, u32[]{:S(2)}) collective-permute-start(bf16[128,256]{1,0:T(8,128)(2,1)S(1)} %get-tuple-element.5), channel_id=1, source_target_pairs={{0,16},{4,20},{8,24},{12,28},{16,0},{20,4},{24,8},{28,12},{1,17},{... | collective-permute-start | bytes 196616 | tf_op jit(solution)/shard_map/ppermute | solution.py:14
  23.8 4.3 %collective-permute-start.4 = (bf16[128,256]{1,0:T(8,128)(2,1)S(1)}, bf16[128,256]{1,0:T(8,128)(2,1)S(1)}, u32[]{:S(2)}, u32[]{:S(2)}) collective-permute-start(bf16[128,256]{1,0:T(8,128)(2,1)S(1)} %get-tuple-element.5), channel_id=1, source_target_pairs={{0,8},{4,12},{8,0},{12,4},{16,24},{20,28},{24,16},{28,20},{1,9},{5... | collective-permute-start | bytes 196616 | tf_op jit(solution)/shard_map/ppermute | solution.py:14
  28.1 1.6 %collective-permute-start.7 = (bf16[512,256]{1,0:T(8,128)(2,1)S(1)}, bf16[512,256]{1,0:T(8,128)(2,1)S(1)}, u32[]{:S(2)}, u32[]{:S(2)}) collective-permute-start(bf16[512,256]{1,0:T(8,128)(2,1)S(1)} %pad_maximum_fusion.1), channel_id=1, source_target_pairs={{0,4},{4,0},{8,12},{12,8},{16,20},{20,16},{24,28},{28,24},{1,5},{5... | collective-permute-start | bytes 786440 | tf_op jit(solution)/shard_map/ppermute | solution.py:14
  30.3 5.6 %collective-permute-start.8 = (bf16[256,256]{1,0:T(8,128)(2,1)S(1)}, bf16[256,256]{1,0:T(8,128)(2,1)S(1)}, u32[]{:S(2)}, u32[]{:S(2)}) collective-permute-start(bf16[256,256]{1,0:T(8,128)(2,1)S(1)} %fusion.1), channel_id=1, source_target_pairs={{0,1},{1,0},{2,3},{3,2},{4,5},{5,4},{6,7},{7,6},{8,9},{9,8},{10,11... | collective-permute-start | bytes 393224 | tf_op jit(solution)/shard_map/ppermute | solution.py:14
  35.9 8.5 %collective-permute-start.9 = (bf16[256,256]{1,0:T(8,128)(2,1)S(1)}, bf16[256,256]{1,0:T(8,128)(2,1)S(1)}, u32[]{:S(2)}, u32[]{:S(2)}) collective-permute-start(bf16[256,256]{1,0:T(8,128)(2,1)S(1)} %add_convert_fusion), channel_id=1, source_target_pairs={{0,2},{1,3},{2,0},{3,1},{4,6},{5,7},{6,4},{7,5},{8,10},{9,11},{10,... | collective-permute-start | bytes 393224 | tf_op jit(solution)/shard_map/ppermute | solution.py:14

commit v2 on v1

v2 whole, which is shorter than its diff:
```python
import functools

import jax
import jax.numpy as jnp
from jax import lax
from jax.experimental import pallas as pl
from jax.experimental.pallas import tpu as pltpu
from jax.sharding import PartitionSpec as P


def transposed_product(left, right):
    return lax.dot_general(
        left, right, (((0,), (0,)), ((), ())), preferred_element_type=jnp.float32
    )


def exchange(value, axis, size, flip):
    return lax.ppermute(value, axis, [(i, i ^ flip) for i in range(size)])


def project_blocks(core_flip, order, tile_src, tile_count, feats, tiles, w_self, w_neigh, rows_out, sums_out):
    block_rows = tiles.shape[2]
    tile_slots = tiles.shape[1]
    n_chip = rows_out.shape[0] // block_rows
    me = lax.axis_index("feat")
    weights = jnp.concatenate([w_self[...], w_neigh[...]], axis=0)

    def block_of(index):
        return feats[pl.ds(pl.multiple_of(index * block_rows, block_rows), block_rows), :]

    for j in range(n_chip):
        block = order[0, me ^ (2 * j + core_flip)]
        here = pl.ds(j * block_rows, block_rows)
        used = []
        sources = []
        for k in range(tile_slots):
            tile = tiles[block, k]
            used.append(jnp.where(k < tile_count[0, block], tile, jnp.zeros_like(tile)))
            sources.append(block_of(tile_src[k, 0, block]))
        mean = jnp.dot(
            jnp.concatenate(used, axis=1), jnp.concatenate(sources, axis=0), preferred_element_type=jnp.float32
        ).astype(jnp.bfloat16)
        rows = jnp.concatenate([block_of(block), mean], axis=1)
        rows_out[here, :] = rows
        sums_out[here, :] = jnp.dot(rows, weights, preferred_element_type=jnp.float32).astype(sums_out.dtype)


def load_and_project(*refs):
    loaded_from, rows_out, sums_out, loaded, sems = refs[:7], refs[7], refs[8], refs[9:16], refs[16]
    copies = []
    for i, (source, target) in enumerate(zip(loaded_from, loaded)):
        source = source.at[0] if len(source.shape) > len(target.shape) else source
        copies.append(pltpu.make_async_copy(source, target, sems.at[i]))
        copies[-1].start()
    for copy in copies:
        copy.wait()
    project_blocks(1, *loaded, rows_out, sums_out)


def body(n_feat, n_rep, feats, w_self, w_neigh, bias, tile_weight, tile_src, tile_count, owner_order, cotangent):
    block_rows = tile_weight.shape[3]
    tile_slots = tile_weight.shape[2]
    columns = feats.shape[2]
    hidden_units = w_self.shape[1]
    n_chip = n_feat // 2
    rows = n_chip * block_rows
    tiles_of_slot = jnp.transpose(tile_src, (2, 0, 1))

    operands = (owner_order, tiles_of_slot, tile_count, feats, tile_weight, w_self, w_neigh)
    smem, vmem = pl.BlockSpec(memory_space=pltpu.SMEM), pl.BlockSpec(memory_space=pltpu.VMEM)
    loaded_specs = (smem,) * 3 + (vmem,) * 4
    loaded_shapes = tuple(
        jax.ShapeDtypeStruct(a.shape if i < 3 or i > 4 else a.shape[1:], a.dtype) for i, a in enumerate(operands)
    )
    params = dict(
        compiler_params=pltpu.CompilerParams(vmem_limit_bytes=32 * 1024 * 1024),
        cost_estimate=pl.CostEstimate(
            flops=2 * rows * (tile_slots * block_rows * columns + 2 * columns * hidden_units),
            bytes_accessed=feats.size * 2 + tile_weight.size + rows * 8 * columns,
            transcendentals=0,
        ),
    )

    def results(dtype):
        return (
            jax.ShapeDtypeStruct((rows, 2 * columns), jnp.bfloat16),
            jax.ShapeDtypeStruct((rows, hidden_units), dtype),
        )

    operands = tuple(pltpu.with_memory_space_constraint(a, pltpu.HBM) for a in operands)
    given_rows, given, *loaded = pl.pallas_call(
        load_and_project,
        out_shape=results(jnp.bfloat16) + loaded_shapes,
        in_specs=[pl.BlockSpec(memory_space=pltpu.HBM)] * 7,
        out_specs=(vmem,) * 2 + loaded_specs,
        scratch_shapes=[pltpu.SemaphoreType.DMA((7,))],
        **params,
    )(*operands)
    kept_rows, kept = pl.pallas_call(
        functools.partial(project_blocks, 0),
        out_shape=results(jnp.float32),
        in_specs=loaded_specs,
        out_specs=(vmem,) * 2,
        **params,
    )(*loaded)

    from_core = exchange(given, "feat", n_feat, 1)
    chip_sums = (kept + from_core.astype(jnp.float32)).reshape(n_chip, block_rows, hidden_units)
    preact = chip_sums[0] + bias
    for j in reversed(range(1, n_chip)):
        got = exchange(chip_sums[j].astype(jnp.bfloat16), "feat", n_feat, 2 * j)
        preact = preact + got.astype(jnp.float32)
    squash = jax.nn.sigmoid(preact)
    output_grad = (
        cotangent[0].astype(jnp.float32) * squash * (1.0 + preact * (1.0 - squash))
    ).astype(jnp.bfloat16)
    preact, output_grad = lax.optimization_barrier((preact, output_grad))
    hidden = jax.nn.silu(preact).astype(jnp.bfloat16)

    own = [output_grad] + [exchange(output_grad, "feat", n_feat, 2 * j) for j in range(1, n_chip)]
    own = jnp.concatenate(own, axis=0)
    other = exchange(own, "feat", n_feat, 1)
    grads = transposed_product(kept_rows, own) + transposed_product(given_rows, other)

    flip = 1
    while flip < n_rep:
        sent = lax.optimization_barrier(grads.astype(jnp.bfloat16))
        got = exchange(sent, "rep", n_rep, flip)
        grads = sent.astype(jnp.float32) + got.astype(jnp.float32)
        flip = 2 * flip + 1
    return (hidden[None], grads[:columns], grads[columns:])


def solution(mesh):
    n_feat, n_rep = mesh.shape["feat"], mesh.shape["rep"]

    def local(*args):
        return body(n_feat, n_rep, *args)

    in_specs = (
        P("rep", None, "feat"),
        P("feat", None),
        P("feat", None),
        P(),
        P("rep", None, None, None, None),
        P("rep", None, None),
        P("rep", None),
        P("rep", None),
        P("rep", "feat", None),
    )
    out_specs = (P("rep", "feat", None), P("feat", None), P("feat", None))
    return jax.shard_map(local, mesh=mesh, in_specs=in_specs, out_specs=out_specs, check_vma=False)
```

time: 45.4 us -> 36.7 us (0.81)
  local copies, waits for them, and re-layouts: 8.87 us -> 0.77 us
  waiting for transfers between devices: 20 us -> 15.9 us
  Pallas kernels: 0 us -> 3.73 us
  starting transfers between devices: 12.9 us -> 13.9 us
  matrix products: 1.34 us -> 0.54 us
    gather x9 -> x0, local copies, waits for them, and re-layouts: 4.73 us -> none  [the longest x3 1.34 us: body(): sources = by_block[tile_src[0][blocks]]]
    ppermute x10, waiting for transfers between devices: 20 us -> 15.9 us  [exchange(): return lax.ppermute(value, axis, [(i, i ^ flip) for i in range(size)])]
    pallas_call x0 -> x2, Pallas kernels: none -> 3.73 us  [the longest x1 2.51 us: body(): pl.pallas_call(load_and_project, out_shape=results(jnp.bfloat16) + loaded...]
    unnamed x18 -> x7, local copies, waits for them, and re-layouts: 2.63 us -> 0.03 us
    ppermute x10, starting transfers between devices: 12.9 us -> 13.9 us  [exchange(): return lax.ppermute(value, axis, [(i, i ^ flip) for i in range(size)])]
    dot_general x2 -> x0, matrix products: 0.81 us -> none  [the longest x1 0.51 us: body(): jnp.einsum('bkij,bkjc->bic', masked, sources, preferred_element_type=jnp....]
    broadcast_in_dim x0 -> x1, other arithmetic: none -> 0.67 us  [body(): return (hidden[None], grads[:columns], grads[columns:])]
    convert_element_type x1, other arithmetic: 0.72 us -> 0.09 us  [body(): output_grad = (cotangent[0].astype(jnp.float32) * squash * (1.0 + preact...]
  transfers between devices with their start and end apart: 10 -> 10, of which waited for: 10 -> 7; matrix products, arithmetic and copies ran while one was open for 1% -> 2% of each run, Pallas kernels for 0% -> 3%
where the time goes in v2:
time: 36.7 us; the launch traced here: 36.5 us
  waiting for transfers between devices  15.9 us (43%)
  starting transfers between devices  13.9 us (38%)
  Pallas kernels  3.73 us (10%)
  other arithmetic  0.89 us (2%)
  local copies, waits for them, and re-layouts  0.77 us (2%)
  between operations  0.75 us (2%)
  matrix products  0.54 us (1%)
    ppermute x10, waiting for transfers between devices, exchange(): return lax.ppermute(value, axis, [(i, i ^ flip) for i in range(size)])  15.9 us
    ppermute x10, starting transfers between devices, exchange(): return lax.ppermute(value, axis, [(i, i ^ flip) for i in range(size)])  13.9 us
    pallas_call x1, Pallas kernels, body(): pl.pallas_call(load_and_project, out_shape=results(jnp.bfloat16) + loaded...  2.51 us
    pallas_call x1, Pallas kernels, body(): pl.pallas_call(functools.partial(project_blocks, 0), out_shape=results(jn...  1.23 us
  transfers between devices with their start and end apart: 10, of which 7 were waited for; matrix products, arithmetic and copies ran while one was open for 2% of the time, Pallas kernels for 3%

profile of v2, /device:TPU:0, one launch (start us, length us, event | category | flops | bytes accessed | tf_op | source)
XLA Modules:
  0.0 36.5 jit_solution(3281066465208014371)
XLA Ops:
  0.6 2.5 %shard_map.112 = (bf16[512,256]{1,0:T(8,128)(2,1)S(1)}, bf16[512,256]{1,0:T(8,128)(2,1)S(1)}, s32[1,8]{1,0:T(1,128)S(1)}, s32[3,1,8]{2,1,0:T(1,128)S(1)}, s32[1,...) custom-call(s32[1,8]{1,0:T(1,128)} %refs_0_.1, ...), custom_call_target="tpu_custom_call" | custom-call | flops 117440512 | bytes 1441792 | tf_op jit(solution)/shard_map/pallas_call | solution.py:91
  3.1 0.5 %collective-permute-start = (bf16[512,256]{1,0:T(8,128)(2,1)S(1)}, bf16[512,256]{1,0:T(8,128)(2,1)S(1)}, u32[]{:S(2)}, u32[]{:S(2)}) collective-permute-start(bf16[512,256]{1,0:T(8,128)(2,1)S(1)} %get-tuple-element.24), channel_id=1, source_target_pairs={{0,4},{4,0},{8,12},{12,8},{16,20},{20,16},{24,28},{28,24},{1,5},{5... | collective-permute-start | bytes 786440 | tf_op jit(solution)/shard_map/ppermute | solution.py:18
  3.7 1.2 %shard_map.113 = (bf16[512,256]{1,0:T(8,128)(2,1)S(1)}, f32[512,256]{1,0:T(8,128)S(1)}) custom-call(s32[1,8]{1,0:T(1,128)S(1)} %get-tuple-element.16.order, s32[3,1,8]{2,1,0:T(1,128)S(1)} %get-tuple-element.17.tile_src, s32[1,8]{1,0:T(1,128)S(1)} %get-tuple-element.18.tile_count, bf16[2048,128]{1,0:T(8,128)(2,1)S(1)} %get-tuple-element.19.feats, ...), custom_call_target="tpu_custom_call" | custom-call | flops 117440512 | bytes 1441792 | tf_op jit(solution)/shard_map/pallas_call | solution.py:99
  5.0 3.8 %collective-permute-start.1 = (bf16[128,256]{1,0:T(8,128)(2,1)S(1)}, bf16[128,256]{1,0:T(8,128)(2,1)S(1)}, u32[]{:S(2)}, u32[]{:S(2)}) collective-permute-start(bf16[128,256]{1,0:T(8,128)(2,1)S(1)} %get-tuple-element.35), channel_id=1, source_target_pairs={{0,24},{4,28},{8,16},{12,20},{16,8},{20,12},{24,0},{28,4},{1,25},{... | collective-permute-start | bytes 196616 | tf_op jit(solution)/shard_map/ppermute | solution.py:18
  8.8 0.5 %collective-permute-start.3 = (bf16[128,256]{1,0:T(8,128)(2,1)S(1)}, bf16[128,256]{1,0:T(8,128)(2,1)S(1)}, u32[]{:S(2)}, u32[]{:S(2)}) collective-permute-start(bf16[128,256]{1,0:T(8,128)(2,1)S(1)} %get-tuple-element.36), channel_id=1, source_target_pairs={{0,8},{4,12},{8,0},{12,4},{16,24},{20,28},{24,16},{28,20},{1,9},{5... | collective-permute-start | bytes 196616 | tf_op jit(solution)/shard_map/ppermute | solution.py:18
  9.4 0.1 collective-permute-start.2
  9.5 1.8 %collective-permute-done.1 = bf16[128,256]{1,0:T(8,128)(2,1)S(1)} collective-permute-done((bf16[128,256]{1,0:T(8,128)(2,1)S(1)}, bf16[128,256]{1,0:T(8,128)(2,1)S(1)}, u32[]{:S(2)}, u32[]{:S(2)}) %collective-permute-start.1) | collective-permute-done | bytes 65568 | tf_op jit(solution)/shard_map/ppermute | solution.py:18
  11.3 1.8 %collective-permute-done.3 = bf16[128,256]{1,0:T(8,128)(2,1)S(1)} collective-permute-done((bf16[128,256]{1,0:T(8,128)(2,1)S(1)}, bf16[128,256]{1,0:T(8,128)(2,1)S(1)}, u32[]{:S(2)}, u32[]{:S(2)}) %collective-permute-start.3) | collective-permute-done | bytes 65568 | tf_op jit(solution)/shard_map/ppermute | solution.py:18
  13.1 0.5 %collective-permute-done.2 = bf16[128,256]{1,0:T(8,128)(2,1)S(1)} collective-permute-done((bf16[128,256]{1,0:T(8,128)(2,1)S(1)}, bf16[128,256]{1,0:T(8,128)(2,1)S(1)}, u32[]{:S(2)}, u32[]{:S(2)}) %collective-permute-start.2) | collective-permute-done | bytes 65568 | tf_op jit(solution)/shard_map/ppermute | solution.py:18
  13.6 0.1 fusion.5
  13.7 1.8 %collective-permute-start.6 = (bf16[128,256]{1,0:T(8,128)(2,1)S(1)}, bf16[128,256]{1,0:T(8,128)(2,1)S(1)}, u32[]{:S(2)}, u32[]{:S(2)}) collective-permute-start(bf16[128,256]{1,0:T(8,128)(2,1)S(1)} %get-tuple-element.27), channel_id=1, source_target_pairs={{0,24},{4,28},{8,16},{12,20},{16,8},{20,12},{24,0},{28,4},{1,25},{... | collective-permute-start | bytes 196616 | tf_op jit(solution)/shard_map/ppermute | solution.py:18
  15.5 1.2 %collective-permute-start.5 = (bf16[128,256]{1,0:T(8,128)(2,1)S(1)}, bf16[128,256]{1,0:T(8,128)(2,1)S(1)}, u32[]{:S(2)}, u32[]{:S(2)}) collective-permute-start(bf16[128,256]{1,0:T(8,128)(2,1)S(1)} %get-tuple-element.27), channel_id=1, source_target_pairs={{0,16},{4,20},{8,24},{12,28},{16,0},{20,4},{24,8},{28,12},{1,17},{... | collective-permute-start | bytes 196616 | tf_op jit(solution)/shard_map/ppermute | solution.py:18
  16.7 0.5 %collective-permute-start.4 = (bf16[128,256]{1,0:T(8,128)(2,1)S(1)}, bf16[128,256]{1,0:T(8,128)(2,1)S(1)}, u32[]{:S(2)}, u32[]{:S(2)}) collective-permute-start(bf16[128,256]{1,0:T(8,128)(2,1)S(1)} %get-tuple-element.27), channel_id=1, source_target_pairs={{0,8},{4,12},{8,0},{12,4},{16,24},{20,28},{24,16},{28,20},{1,9},{5... | collective-permute-start | bytes 196616 | tf_op jit(solution)/shard_map/ppermute | solution.py:18
  17.3 3.7 %collective-permute-done.4 = bf16[128,256]{1,0:T(8,128)(2,1)S(1)} collective-permute-done((bf16[128,256]{1,0:T(8,128)(2,1)S(1)}, bf16[128,256]{1,0:T(8,128)(2,1)S(1)}, u32[]{:S(2)}, u32[]{:S(2)}) %collective-permute-start.4) | collective-permute-done | bytes 65568 | tf_op jit(solution)/shard_map/ppermute | solution.py:18
  21.1 0.1 collective-permute-start.7
  21.1 1.5 %collective-permute-done.7 = bf16[512,256]{1,0:T(8,128)(2,1)S(1)} collective-permute-done((bf16[512,256]{1,0:T(8,128)(2,1)S(1)}, bf16[512,256]{1,0:T(8,128)(2,1)S(1)}, u32[]{:S(2)}, u32[]{:S(2)}) %collective-permute-start.7) | collective-permute-done | bytes 262176 | tf_op jit(solution)/shard_map/ppermute | solution.py:18
  22.7 0.3 fusion.11
  22.9 0.3 fusion
  23.2 1.6 %collective-permute-start.8 = (bf16[256,256]{1,0:T(8,128)(2,1)S(1)}, bf16[256,256]{1,0:T(8,128)(2,1)S(1)}, u32[]{:S(2)}, u32[]{:S(2)}) collective-permute-start(bf16[256,256]{1,0:T(8,128)(2,1)S(1)} %fusion), channel_id=1, source_target_pairs={{0,1},{1,0},{2,3},{3,2},{4,5},{5,4},{6,7},{7,6},{8,9},{9,8},{10,11... | collective-permute-start | bytes 393224 | tf_op jit(solution)/shard_map/ppermute | solution.py:18
  24.9 4.0 %collective-permute-done.8 = bf16[256,256]{1,0:T(8,128)(2,1)S(1)} collective-permute-done((bf16[256,256]{1,0:T(8,128)(2,1)S(1)}, bf16[256,256]{1,0:T(8,128)(2,1)S(1)}, u32[]{:S(2)}, u32[]{:S(2)}) %collective-permute-start.8) | collective-permute-done | bytes 131104 | tf_op jit(solution)/shard_map/ppermute | solution.py:18
  28.9 3.7 %collective-permute-start.9 = (bf16[256,256]{1,0:T(8,128)(2,1)S(1)}, bf16[256,256]{1,0:T(8,128)(2,1)S(1)}, u32[]{:S(2)}, u32[]{:S(2)}) collective-permute-start(bf16[256,256]{1,0:T(8,128)(2,1)S(1)} %add_convert_fusion), channel_id=1, source_target_pairs={{0,3},{1,2},{2,1},{3,0},{4,7},{5,6},{6,5},{7,4},{8,11},{9,10},{10,... | collective-permute-start | bytes 393224 | tf_op jit(solution)/shard_map/ppermute | solution.py:18
  32.5 0.7 %fusion.6 = bf16[1,128,256]{2,1,0:T(8,128)(2,1)} fusion(f32[128,256]{1,0:T(8,128)S(1)} %get-tuple-element.25), kind=kLoop, calls=%fused_computation.13 | loop fusion | flops 163840 | bytes 196608 | tf_op jit(solution)/shard_map/broadcast_in_dim | solution.py:131
  33.2 2.5 %collective-permute-done.9 = bf16[256,256]{1,0:T(8,128)(2,1)S(1)} collective-permute-done((bf16[256,256]{1,0:T(8,128)(2,1)S(1)}, bf16[256,256]{1,0:T(8,128)(2,1)S(1)}, u32[]{:S(2)}, u32[]{:S(2)}) %collective-permute-start.9) | collective-permute-done | bytes 131104 | tf_op jit(solution)/shard_map/ppermute | solution.py:18
  35.8 0.7 %fusion.9 = (f32[128,256]{1,0:T(8,128)}, f32[128,256]{1,0:T(8,128)}) fusion(f32[256,256]{1,0:T(8,128)S(1)} %convert_add_fusion.1), kind=kLoop, calls=%fused_computation.19 | loop fusion | bytes 524288 | tf_op jit(solution)/shard_map/slice | solution.py:131
  (15 shorter events, 0.2 us)
Async XLA Ops:
  3.1 1.8 %collective-permute-start = (bf16[512,256]{1,0:T(8,128)(2,1)S(1)}, bf16[512,256]{1,0:T(8,128)(2,1)S(1)}, u32[]{:S(2)}, u32[]{:S(2)}) collective-permute-start(bf16[512,256]{1,0:T(8,128)(2,1)S(1)} %get-tuple-element.24), channel_id=1, source_target_pairs={{0,4},{4,0},{8,12},{12,8},{16,20},{20,16},{24,28},{28,24},{1,5},{5... | collective-permute-start | bytes 786440 | tf_op jit(solution)/shard_map/ppermute | solution.py:18
  5.0 8.6 %copy-start = (bf16[1,128,256]{2,1,0:T(8,128)(2,1)S(1)}, bf16[1,128,256]{2,1,0:T(8,128)(2,1)}, u32[]{:S(2)}) copy-start(bf16[1,128,256]{2,1,0:T(8,128)(2,1)} %param.17) | copy-start | bytes 196612
  5.0 6.3 %collective-permute-start.1 = (bf16[128,256]{1,0:T(8,128)(2,1)S(1)}, bf16[128,256]{1,0:T(8,128)(2,1)S(1)}, u32[]{:S(2)}, u32[]{:S(2)}) collective-permute-start(bf16[128,256]{1,0:T(8,128)(2,1)S(1)} %get-tuple-element.35), channel_id=1, source_target_pairs={{0,24},{4,28},{8,16},{12,20},{16,8},{20,12},{24,0},{28,4},{1,25},{... | collective-permute-start | bytes 196616 | tf_op jit(solution)/shard_map/ppermute | solution.py:18
  8.8 4.3 %collective-permute-start.3 = (bf16[128,256]{1,0:T(8,128)(2,1)S(1)}, bf16[128,256]{1,0:T(8,128)(2,1)S(1)}, u32[]{:S(2)}, u32[]{:S(2)}) collective-permute-start(bf16[128,256]{1,0:T(8,128)(2,1)S(1)} %get-tuple-element.36), channel_id=1, source_target_pairs={{0,8},{4,12},{8,0},{12,4},{16,24},{20,28},{24,16},{28,20},{1,9},{5... | collective-permute-start | bytes 196616 | tf_op jit(solution)/shard_map/ppermute | solution.py:18
  9.4 4.3 %copy-start.1 = (f32[256]{0:T(256)S(1)}, f32[256]{0:T(256)}, u32[]{:S(2)}) copy-start(f32[256]{0:T(256)} %param.12) | copy-start | bytes 3076
  9.4 4.3 %collective-permute-start.2 = (bf16[128,256]{1,0:T(8,128)(2,1)S(1)}, bf16[128,256]{1,0:T(8,128)(2,1)S(1)}, u32[]{:S(2)}, u32[]{:S(2)}) collective-permute-start(bf16[128,256]{1,0:T(8,128)(2,1)S(1)} %get-tuple-element.37), channel_id=1, source_target_pairs={{0,16},{4,20},{8,24},{12,28},{16,0},{20,4},{24,8},{28,12},{1,17},{... | collective-permute-start | bytes 196616 | tf_op jit(solution)/shard_map/ppermute | solution.py:18
  13.7 7.3 %collective-permute-start.6 = (bf16[128,256]{1,0:T(8,128)(2,1)S(1)}, bf16[128,256]{1,0:T(8,128)(2,1)S(1)}, u32[]{:S(2)}, u32[]{:S(2)}) collective-permute-start(bf16[128,256]{1,0:T(8,128)(2,1)S(1)} %get-tuple-element.27), channel_id=1, source_target_pairs={{0,24},{4,28},{8,16},{12,20},{16,8},{20,12},{24,0},{28,4},{1,25},{... | collective-permute-start | bytes 196616 | tf_op jit(solution)/shard_map/ppermute | solution.py:18
  15.5 5.5 %collective-permute-start.5 = (bf16[128,256]{1,0:T(8,128)(2,1)S(1)}, bf16[128,256]{1,0:T(8,128)(2,1)S(1)}, u32[]{:S(2)}, u32[]{:S(2)}) collective-permute-start(bf16[128,256]{1,0:T(8,128)(2,1)S(1)} %get-tuple-element.27), channel_id=1, source_target_pairs={{0,16},{4,20},{8,24},{12,28},{16,0},{20,4},{24,8},{28,12},{1,17},{... | collective-permute-start | bytes 196616 | tf_op jit(solution)/shard_map/ppermute | solution.py:18
  16.7 4.3 %collective-permute-start.4 = (bf16[128,256]{1,0:T(8,128)(2,1)S(1)}, bf16[128,256]{1,0:T(8,128)(2,1)S(1)}, u32[]{:S(2)}, u32[]{:S(2)}) collective-permute-start(bf16[128,256]{1,0:T(8,128)(2,1)S(1)} %get-tuple-element.27), channel_id=1, source_target_pairs={{0,8},{4,12},{8,0},{12,4},{16,24},{20,28},{24,16},{28,20},{1,9},{5... | collective-permute-start | bytes 196616 | tf_op jit(solution)/shard_map/ppermute | solution.py:18
  21.1 1.6 %collective-permute-start.7 = (bf16[512,256]{1,0:T(8,128)(2,1)S(1)}, bf16[512,256]{1,0:T(8,128)(2,1)S(1)}, u32[]{:S(2)}, u32[]{:S(2)}) collective-permute-start(bf16[512,256]{1,0:T(8,128)(2,1)S(1)} %constant_dynamic-update-slice_fusion), channel_id=1, source_target_pairs={{0,4},{4,0},{8,12},{12,8},{16,20},{20,16},{24,28},{28,24},{1,5},{5... | collective-permute-start | bytes 786440 | tf_op jit(solution)/shard_map/ppermute | solution.py:18
  23.2 5.6 %collective-permute-start.8 = (bf16[256,256]{1,0:T(8,128)(2,1)S(1)}, bf16[256,256]{1,0:T(8,128)(2,1)S(1)}, u32[]{:S(2)}, u32[]{:S(2)}) collective-permute-start(bf16[256,256]{1,0:T(8,128)(2,1)S(1)} %fusion), channel_id=1, source_target_pairs={{0,1},{1,0},{2,3},{3,2},{4,5},{5,4},{6,7},{7,6},{8,9},{9,8},{10,11... | collective-permute-start | bytes 393224 | tf_op jit(solution)/shard_map/ppermute | solution.py:18
  28.9 6.9 %collective-permute-start.9 = (bf16[256,256]{1,0:T(8,128)(2,1)S(1)}, bf16[256,256]{1,0:T(8,128)(2,1)S(1)}, u32[]{:S(2)}, u32[]{:S(2)}) collective-permute-start(bf16[256,256]{1,0:T(8,128)(2,1)S(1)} %add_convert_fusion), channel_id=1, source_target_pairs={{0,3},{1,2},{2,1},{3,0},{4,7},{5,6},{6,5},{7,4},{8,11},{9,10},{10,... | collective-permute-start | bytes 393224 | tf_op jit(solution)/shard_map/ppermute | solution.py:18

commit v3 on v2

--- a/solution.py
+++ b/solution.py
@@ -18,34 +18,29 @@
     return lax.ppermute(value, axis, [(i, i ^ flip) for i in range(size)])
 
 
-def project_blocks(core_flip, order, tile_src, tile_count, feats, tiles, w_self, w_neigh, rows_out, sums_out):
+def project_blocks(flips, order, tile_src, tile_count, feats, tiles, w_self, w_neigh, rows_out, sums_out):
     block_rows = tiles.shape[2]
     tile_slots = tiles.shape[1]
-    n_chip = rows_out.shape[0] // block_rows
     me = lax.axis_index("feat")
-    weights = jnp.concatenate([w_self[...], w_neigh[...]], axis=0)
 
     def block_of(index):
         return feats[pl.ds(pl.multiple_of(index * block_rows, block_rows), block_rows), :]
 
-    for j in range(n_chip):
-        block = order[0, me ^ (2 * j + core_flip)]
-        here = pl.ds(j * block_rows, block_rows)
-        used = []
-        sources = []
+    for j, (even, odd) in enumerate(flips):
+        block = order[0, me ^ jnp.where(me % 2 == 0, even, odd)]
+        mean = jnp.zeros((block_rows, feats.shape[1]), jnp.float32)
         for k in range(tile_slots):
             tile = tiles[block, k]
-            used.append(jnp.where(k < tile_count[0, block], tile, jnp.zeros_like(tile)))
-            sources.append(block_of(tile_src[k, 0, block]))
-        mean = jnp.dot(
-            jnp.concatenate(used, axis=1), jnp.concatenate(sources, axis=0), preferred_element_type=jnp.float32
-        ).astype(jnp.bfloat16)
-        rows = jnp.concatenate([block_of(block), mean], axis=1)
-        rows_out[here, :] = rows
-        sums_out[here, :] = jnp.dot(rows, weights, preferred_element_type=jnp.float32).astype(sums_out.dtype)
+            used = jnp.where(k < tile_count[0, block], tile, jnp.zeros_like(tile))
+            mean += jnp.dot(used, block_of(tile_src[k, 0, block]), preferred_element_type=jnp.float32)
+        rows_out[pl.ds(j * block_rows, block_rows), :] = jnp.concatenate(
+            [block_of(block), mean.astype(jnp.bfloat16)], axis=1
+        )
+    weights = jnp.concatenate([w_self[...], w_neigh[...]], axis=0)
+    sums_out[...] = jnp.dot(rows_out[...], weights, preferred_element_type=jnp.float32).astype(sums_out.dtype)
 
 
-def load_and_project(*refs):
+def load_and_project(flips, *refs):
     loaded_from, rows_out, sums_out, loaded, sems = refs[:7], refs[7], refs[8], refs[9:16], refs[16]
     copies = []
     for i, (source, target) in enumerate(zip(loaded_from, loaded)):
@@ -54,7 +49,22 @@
         copies[-1].start()
     for copy in copies:
         copy.wait()
-    project_blocks(1, *loaded, rows_out, sums_out)
+    project_blocks(flips, *loaded, rows_out, sums_out)
+
+
+def first_products(kept_rows, given_rows, own, partner, early, total_out):
+    n = own.shape[0]
+    total = transposed_product(kept_rows[pl.ds(0, n), :], own[...])
+    total += transposed_product(given_rows[pl.ds(0, n), :], partner[...])
+    total_out[...] = total + transposed_product(kept_rows[pl.ds(2 * n, early.shape[0]), :], early[...])
+
+
+def last_products(total, kept_rows, given_rows, late, others_late, others_early, total_out):
+    n = late.shape[0]
+    last = transposed_product(kept_rows[pl.ds(n, n), :], late[...])
+    last += transposed_product(given_rows[pl.ds(2 * n, others_early.shape[0]), :], others_early[...])
+    last += transposed_product(given_rows[pl.ds(n, n), :], others_late[...])
+    total_out[...] = (total[...] + last).astype(jnp.bfloat16)
 
 
 def body(n_feat, n_rep, feats, w_self, w_neigh, bias, tile_weight, tile_src, tile_count, owner_order, cotangent):
@@ -64,6 +74,12 @@
     hidden_units = w_self.shape[1]
     n_chip = n_feat // 2
     rows = n_chip * block_rows
+
+    def swap_cores(value):
+        return exchange(value, "feat", n_feat, 1)
+
+    kept_flips = tuple((2 * j + (j > 0), 2 * j + (j > 0)) for j in range(n_chip))
+    given_flips = tuple((odd ^ 1, even ^ 1) for even, odd in kept_flips)
     tiles_of_slot = jnp.transpose(tile_src, (2, 0, 1))
 
     operands = (owner_order, tiles_of_slot, tile_count, feats, tile_weight, w_self, w_neigh)
@@ -89,7 +105,7 @@
 
     operands = tuple(pltpu.with_memory_space_constraint(a, pltpu.HBM) for a in operands)
     given_rows, given, *loaded = pl.pallas_call(
-        load_and_project,
+        functools.partial(load_and_project, given_flips),
         out_shape=results(jnp.bfloat16) + loaded_shapes,
         in_specs=[pl.BlockSpec(memory_space=pltpu.HBM)] * 7,
         out_specs=(vmem,) * 2 + loaded_specs,
@@ -97,18 +113,21 @@
         **params,
     )(*operands)
     kept_rows, kept = pl.pallas_call(
-        functools.partial(project_blocks, 0),
+        functools.partial(project_blocks, kept_flips),
         out_shape=results(jnp.float32),
         in_specs=loaded_specs,
         out_specs=(vmem,) * 2,
         **params,
     )(*loaded)
 
-    from_core = exchange(given, "feat", n_feat, 1)
-    chip_sums = (kept + from_core.astype(jnp.float32)).reshape(n_chip, block_rows, hidden_units)
-    preact = chip_sums[0] + bias
-    for j in reversed(range(1, n_chip)):
-        got = exchange(chip_sums[j].astype(jnp.bfloat16), "feat", n_feat, 2 * j)
+    from_core = swap_cores(given)
+    chip_sums = kept + from_core.astype(jnp.float32)
+    arrived = [
+        exchange(chip_sums[j * block_rows : (j + 1) * block_rows].astype(jnp.bfloat16), "feat", n_feat, 2 * j + 1)
+        for j in reversed(range(1, n_chip))
+    ]
+    preact = chip_sums[:block_rows] + bias
+    for got in arrived:
         preact = preact + got.astype(jnp.float32)
     squash = jax.nn.sigmoid(preact)
     output_grad = (
@@ -117,10 +136,29 @@
     preact, output_grad = lax.optimization_barrier((preact, output_grad))
     hidden = jax.nn.silu(preact).astype(jnp.bfloat16)
 
-    own = [output_grad] + [exchange(output_grad, "feat", n_feat, 2 * j) for j in range(1, n_chip)]
-    own = jnp.concatenate(own, axis=0)
-    other = exchange(own, "feat", n_feat, 1)
-    grads = transposed_product(kept_rows, own) + transposed_product(given_rows, other)
+    received = [exchange(output_grad, "feat", n_feat, 2 * j + 1) for j in range(1, n_chip)]
+    partner = swap_cores(output_grad)
+    early = jnp.concatenate(received[1:], axis=0)
+    early, partner = lax.optimization_barrier((early, partner))
+    others_early = swap_cores(early)
+    others_late = swap_cores(received[0])
+    products = pl.CostEstimate(flops=2 * rows * 2 * columns * hidden_units, bytes_accessed=0, transcendentals=0)
+    total = pl.pallas_call(
+        first_products,
+        out_shape=jax.ShapeDtypeStruct((2 * columns, hidden_units), jnp.float32),
+        in_specs=(vmem,) * 5,
+        out_specs=vmem,
+        compiler_params=params["compiler_params"],
+        cost_estimate=products,
+    )(kept_rows, given_rows, output_grad, partner, early)
+    grads = pl.pallas_call(
+        last_products,
+        out_shape=jax.ShapeDtypeStruct((2 * columns, hidden_units), jnp.bfloat16),
+        in_specs=(vmem,) * 6,
+        out_specs=vmem,
+        compiler_params=params["compiler_params"],
+        cost_estimate=products,
+    )(total, kept_rows, given_rows, received[0], others_late, others_early)
 
     flip = 1
     while flip < n_rep:

time: 36.7 us -> 34.9 us (0.951)
  waiting for transfers between devices: 15.9 us -> 14.5 us
  matrix products: 0.54 us -> 0 us
    ppermute x10 -> x12, waiting for transfers between devices: 15.9 us -> 14.5 us  [exchange(): return lax.ppermute(value, axis, [(i, i ^ flip) for i in range(size)])]
    dot_general x2 -> x0, matrix products: 0.54 us -> none  [transposed_product(): lax.dot_general(left, right, (((0,), (0,)), ((), ())), preferred_element_...]
    ppermute x10 -> x12, starting transfers between devices: 13.9 us -> 14.1 us  [exchange(): return lax.ppermute(value, axis, [(i, i ^ flip) for i in range(size)])]
    pallas_call x2 -> x4, Pallas kernels: 3.73 us -> 3.71 us  [the longest x1 2.11 us: body(): pl.pallas_call(functools.partial(load_and_project, given_flips), out_shap...]
  transfers between devices with their start and end apart: 10 -> 12, of which waited for: 7 -> 9; matrix products, arithmetic and copies ran while one was open for 2% -> 2% of each run, Pallas kernels for 3% -> 4%
where the time goes in v3:
time: 34.9 us; the launch traced here: 34.7 us
  waiting for transfers between devices  14.5 us (42%)
  starting transfers between devices  14.1 us (40%)
  Pallas kernels  3.71 us (11%)
  other arithmetic  0.9 us (3%)
  local copies, waits for them, and re-layouts  0.74 us (2%)
  between operations  0.71 us (2%)
    ppermute x12, waiting for transfers between devices, exchange(): return lax.ppermute(value, axis, [(i, i ^ flip) for i in range(size)])  14.5 us
    ppermute x12, starting transfers between devices, exchange(): return lax.ppermute(value, axis, [(i, i ^ flip) for i in range(size)])  14.1 us
    pallas_call x1, Pallas kernels, body(): pl.pallas_call(functools.partial(load_and_project, given_flips), out_shap...  2.11 us
    pallas_call x1, Pallas kernels, body(): pl.pallas_call(functools.partial(project_blocks, kept_flips), out_shape=r...  1.01 us
    slice x1, local copies, waits for them, and re-layouts, body(): return (hidden[None], grads[:columns], grads[columns:])  0.72 us
  transfers between devices with their start and end apart: 12, of which 9 were waited for; matrix products, arithmetic and copies ran while one was open for 2% of the time, Pallas kernels for 4%

profile of v3, /device:TPU:0, one launch (start us, length us, event | category | flops | bytes accessed | tf_op | source)
XLA Modules:
  0.0 34.7 jit_solution(4679947535884461603)
XLA Ops:
  0.6 2.1 %shard_map.112 = (bf16[512,256]{1,0:T(8,128)(2,1)S(1)}, bf16[512,256]{1,0:T(8,128)(2,1)S(1)}, s32[1,8]{1,0:T(1,128)S(1)}, s32[3,1,8]{2,1,0:T(1,128)S(1)}, s32[1,...) custom-call(s32[1,8]{1,0:T(1,128)} %refs_0_.1, ...), custom_call_target="tpu_custom_call" | custom-call | flops 117440512 | bytes 1441792 | tf_op jit(solution)/shard_map/pallas_call | solution.py:107
  2.8 0.5 %collective-permute-start = (bf16[512,256]{1,0:T(8,128)(2,1)S(1)}, bf16[512,256]{1,0:T(8,128)(2,1)S(1)}, u32[]{:S(2)}, u32[]{:S(2)}) collective-permute-start(bf16[512,256]{1,0:T(8,128)(2,1)S(1)} %get-tuple-element.26), channel_id=1, source_target_pairs={{0,4},{4,0},{8,12},{12,8},{16,20},{20,16},{24,28},{28,24},{1,5},{5... | collective-permute-start | bytes 786440 | tf_op jit(solution)/shard_map/ppermute | solution.py:18
  3.3 1.0 %shard_map.113 = (bf16[512,256]{1,0:T(8,128)(2,1)S(1)}, f32[512,256]{1,0:T(8,128)S(1)}) custom-call(s32[1,8]{1,0:T(1,128)S(1)} %get-tuple-element.18.order, s32[3,1,8]{2,1,0:T(1,128)S(1)} %get-tuple-element.19.tile_src, s32[1,8]{1,0:T(1,128)S(1)} %get-tuple-element.20.tile_count, bf16[2048,128]{1,0:T(8,128)(2,1)S(1)} %get-tuple-element.21.feats, ...), custom_call_target="tpu_custom_call" | custom-call | flops 117440512 | bytes 1441792 | tf_op jit(solution)/shard_map/pallas_call | solution.py:115
  4.5 3.6 %collective-permute-start.1 = (bf16[128,256]{1,0:T(8,128)(2,1)S(1)}, bf16[128,256]{1,0:T(8,128)(2,1)S(1)}, u32[]{:S(2)}, u32[]{:S(2)}) collective-permute-start(bf16[128,256]{1,0:T(8,128)(2,1)S(1)} %get-tuple-element.39), channel_id=1, source_target_pairs={{0,28},{4,24},{8,20},{12,16},{16,12},{20,8},{24,4},{28,0},{1,29},{... | collective-permute-start | bytes 196616 | tf_op jit(solution)/shard_map/ppermute | solution.py:18
  8.2 0.5 %collective-permute-start.3 = (bf16[128,256]{1,0:T(8,128)(2,1)S(1)}, bf16[128,256]{1,0:T(8,128)(2,1)S(1)}, u32[]{:S(2)}, u32[]{:S(2)}) collective-permute-start(bf16[128,256]{1,0:T(8,128)(2,1)S(1)} %get-tuple-element.40), channel_id=1, source_target_pairs={{0,12},{4,8},{8,4},{12,0},{16,28},{20,24},{24,20},{28,16},{1,13},{... | collective-permute-start | bytes 196616 | tf_op jit(solution)/shard_map/ppermute | solution.py:18
  8.8 1.9 %collective-permute-done.1 = bf16[128,256]{1,0:T(8,128)(2,1)S(1)} collective-permute-done((bf16[128,256]{1,0:T(8,128)(2,1)S(1)}, bf16[128,256]{1,0:T(8,128)(2,1)S(1)}, u32[]{:S(2)}, u32[]{:S(2)}) %collective-permute-start.1) | collective-permute-done | bytes 65568 | tf_op jit(solution)/shard_map/ppermute | solution.py:18
  10.7 1.7 %collective-permute-done.3 = bf16[128,256]{1,0:T(8,128)(2,1)S(1)} collective-permute-done((bf16[128,256]{1,0:T(8,128)(2,1)S(1)}, bf16[128,256]{1,0:T(8,128)(2,1)S(1)}, u32[]{:S(2)}, u32[]{:S(2)}) %collective-permute-start.3) | collective-permute-done | bytes 65568 | tf_op jit(solution)/shard_map/ppermute | solution.py:18
  12.4 0.3 collective-permute-done.2
  12.8 2.1 %collective-permute-start.5 = (bf16[128,256]{1,0:T(8,128)(2,1)S(1)}, bf16[128,256]{1,0:T(8,128)(2,1)S(1)}, u32[]{:S(2)}, u32[]{:S(2)}) collective-permute-start(bf16[128,256]{1,0:T(8,128)(2,1)S(1)} %get-tuple-element.30.own), channel_id=1, source_target_pairs={{0,28},{4,24},{8,20},{12,16},{16,12},{20,8},{24,4},{28,0},{1,29},{... | collective-permute-start | bytes 196616 | tf_op jit(solution)/shard_map/ppermute | solution.py:18
  15.0 0.6 %collective-permute-start.4 = (bf16[128,256]{1,0:T(8,128)(2,1)S(1)}, bf16[128,256]{1,0:T(8,128)(2,1)S(1)}, u32[]{:S(2)}, u32[]{:S(2)}) collective-permute-start(bf16[128,256]{1,0:T(8,128)(2,1)S(1)} %get-tuple-element.30.own), channel_id=1, source_target_pairs={{0,20},{4,16},{8,28},{12,24},{16,4},{20,0},{24,12},{28,8},{1,21},{... | collective-permute-start | bytes 196616 | tf_op jit(solution)/shard_map/ppermute | solution.py:18
  15.6 0.3 collective-permute-start.7
  15.9 0.4 %collective-permute-start.6 = (bf16[128,256]{1,0:T(8,128)(2,1)S(1)}, bf16[128,256]{1,0:T(8,128)(2,1)S(1)}, u32[]{:S(2)}, u32[]{:S(2)}) collective-permute-start(bf16[128,256]{1,0:T(8,128)(2,1)S(1)} %get-tuple-element.30.own), channel_id=1, source_target_pairs={{0,4},{4,0},{8,12},{12,8},{16,20},{20,16},{24,28},{28,24},{1,5},{5... | collective-permute-start | bytes 196616 | tf_op jit(solution)/shard_map/ppermute | solution.py:18
  16.2 1.6 %collective-permute-done.5 = bf16[128,256]{1,0:T(8,128)(2,1)S(1)} collective-permute-done((bf16[128,256]{1,0:T(8,128)(2,1)S(1)}, bf16[128,256]{1,0:T(8,128)(2,1)S(1)}, u32[]{:S(2)}, u32[]{:S(2)}) %collective-permute-start.5) | collective-permute-done | bytes 65568 | tf_op jit(solution)/shard_map/ppermute | solution.py:18
  17.8 1.4 %collective-permute-done.4 = bf16[128,256]{1,0:T(8,128)(2,1)S(1)} collective-permute-done((bf16[128,256]{1,0:T(8,128)(2,1)S(1)}, bf16[128,256]{1,0:T(8,128)(2,1)S(1)}, u32[]{:S(2)}, u32[]{:S(2)}) %collective-permute-start.4) | collective-permute-done | bytes 65568 | tf_op jit(solution)/shard_map/ppermute | solution.py:18
  19.3 0.5 %collective-permute-start.9 = (bf16[256,256]{1,0:T(8,128)(2,1)S(1)}, bf16[256,256]{1,0:T(8,128)(2,1)S(1)}, u32[]{:S(2)}, u32[]{:S(2)}) collective-permute-start(bf16[256,256]{1,0:T(8,128)(2,1)S(1)} %pad_maximum_fusion.early), channel_id=1, source_target_pairs={{0,4},{4,0},{8,12},{12,8},{16,20},{20,16},{24,28},{28,24},{1,5},{5... | collective-permute-start | bytes 393224 | tf_op jit(solution)/shard_map/ppermute | solution.py:18
  19.9 0.3 shard_map.114.total
  20.2 0.9 %collective-permute-done.8.others_late = bf16[128,256]{1,0:T(8,128)(2,1)S(1)} collective-permute-done((bf16[128,256]{1,0:T(8,128)(2,1)S(1)}, bf16[128,256]{1,0:T(8,128)(2,1)S(1)}, u32[]{:S(2)}, u32[]{:S(2)}) %collective-permute-start.8) | collective-permute-done | bytes 65568 | tf_op jit(solution)/shard_map/ppermute | solution.py:18
  21.1 0.3 shard_map.115
  21.4 1.6 %collective-permute-start.10 = (bf16[256,256]{1,0:T(8,128)(2,1)S(1)}, bf16[256,256]{1,0:T(8,128)(2,1)S(1)}, u32[]{:S(2)}, u32[]{:S(2)}) collective-permute-start(bf16[256,256]{1,0:T(8,128)(2,1)S(1)} %shard_map.115), channel_id=1, source_target_pairs={{0,1},{1,0},{2,3},{3,2},{4,5},{5,4},{6,7},{7,6},{8,9},{9,8},{10,11... | collective-permute-start | bytes 393224 | tf_op jit(solution)/shard_map/ppermute | solution.py:18
  23.0 4.0 %collective-permute-done.10 = bf16[256,256]{1,0:T(8,128)(2,1)S(1)} collective-permute-done((bf16[256,256]{1,0:T(8,128)(2,1)S(1)}, bf16[256,256]{1,0:T(8,128)(2,1)S(1)}, u32[]{:S(2)}, u32[]{:S(2)}) %collective-permute-start.10) | collective-permute-done | bytes 131104 | tf_op jit(solution)/shard_map/ppermute | solution.py:18
  27.1 3.7 %collective-permute-start.11 = (bf16[256,256]{1,0:T(8,128)(2,1)S(1)}, bf16[256,256]{1,0:T(8,128)(2,1)S(1)}, u32[]{:S(2)}, u32[]{:S(2)}) collective-permute-start(bf16[256,256]{1,0:T(8,128)(2,1)S(1)} %add_convert_fusion), channel_id=1, source_target_pairs={{0,3},{1,2},{2,1},{3,0},{4,7},{5,6},{6,5},{7,4},{8,11},{9,10},{10,... | collective-permute-start | bytes 393224 | tf_op jit(solution)/shard_map/ppermute | solution.py:18
  30.7 0.7 %fusion.5 = bf16[1,128,256]{2,1,0:T(8,128)(2,1)} fusion(f32[128,256]{1,0:T(8,128)S(1)} %get-tuple-element.27), kind=kLoop, calls=%fused_computation.12 | loop fusion | flops 163840 | bytes 196608 | tf_op jit(solution)/shard_map/broadcast_in_dim | solution.py:169
  31.4 2.5 %collective-permute-done.11 = bf16[256,256]{1,0:T(8,128)(2,1)S(1)} collective-permute-done((bf16[256,256]{1,0:T(8,128)(2,1)S(1)}, bf16[256,256]{1,0:T(8,128)(2,1)S(1)}, u32[]{:S(2)}, u32[]{:S(2)}) %collective-permute-start.11) | collective-permute-done | bytes 131104 | tf_op jit(solution)/shard_map/ppermute | solution.py:18
  34.0 0.7 %fusion.8 = (f32[128,256]{1,0:T(8,128)}, f32[128,256]{1,0:T(8,128)}) fusion(f32[256,256]{1,0:T(8,128)S(1)} %convert_add_fusion.1), kind=kLoop, calls=%fused_computation.14 | loop fusion | bytes 524288 | tf_op jit(solution)/shard_map/slice | solution.py:169
  (16 shorter events, 0.6 us)
Async XLA Ops:
  2.8 1.7 %collective-permute-start = (bf16[512,256]{1,0:T(8,128)(2,1)S(1)}, bf16[512,256]{1,0:T(8,128)(2,1)S(1)}, u32[]{:S(2)}, u32[]{:S(2)}) collective-permute-start(bf16[512,256]{1,0:T(8,128)(2,1)S(1)} %get-tuple-element.26), channel_id=1, source_target_pairs={{0,4},{4,0},{8,12},{12,8},{16,20},{20,16},{24,28},{28,24},{1,5},{5... | collective-permute-start | bytes 786440 | tf_op jit(solution)/shard_map/ppermute | solution.py:18
  4.5 8.2 %copy-start = (bf16[1,128,256]{2,1,0:T(8,128)(2,1)S(1)}, bf16[1,128,256]{2,1,0:T(8,128)(2,1)}, u32[]{:S(2)}) copy-start(bf16[1,128,256]{2,1,0:T(8,128)(2,1)} %param.17) | copy-start | bytes 196612
  4.5 6.1 %collective-permute-start.1 = (bf16[128,256]{1,0:T(8,128)(2,1)S(1)}, bf16[128,256]{1,0:T(8,128)(2,1)S(1)}, u32[]{:S(2)}, u32[]{:S(2)}) collective-permute-start(bf16[128,256]{1,0:T(8,128)(2,1)S(1)} %get-tuple-element.39), channel_id=1, source_target_pairs={{0,28},{4,24},{8,20},{12,16},{16,12},{20,8},{24,4},{28,0},{1,29},{... | collective-permute-start | bytes 196616 | tf_op jit(solution)/shard_map/ppermute | solution.py:18
  8.2 4.2 %collective-permute-start.3 = (bf16[128,256]{1,0:T(8,128)(2,1)S(1)}, bf16[128,256]{1,0:T(8,128)(2,1)S(1)}, u32[]{:S(2)}, u32[]{:S(2)}) collective-permute-start(bf16[128,256]{1,0:T(8,128)(2,1)S(1)} %get-tuple-element.40), channel_id=1, source_target_pairs={{0,12},{4,8},{8,4},{12,0},{16,28},{20,24},{24,20},{28,16},{1,13},{... | collective-permute-start | bytes 196616 | tf_op jit(solution)/shard_map/ppermute | solution.py:18
  8.7 4.1 %copy-start.1 = (f32[256]{0:T(256)S(1)}, f32[256]{0:T(256)}, u32[]{:S(2)}) copy-start(f32[256]{0:T(256)} %param.12) | copy-start | bytes 3076
  8.7 4.1 %collective-permute-start.2 = (bf16[128,256]{1,0:T(8,128)(2,1)S(1)}, bf16[128,256]{1,0:T(8,128)(2,1)S(1)}, u32[]{:S(2)}, u32[]{:S(2)}) collective-permute-start(bf16[128,256]{1,0:T(8,128)(2,1)S(1)} %get-tuple-element.41), channel_id=1, source_target_pairs={{0,20},{4,16},{8,28},{12,24},{16,4},{20,0},{24,12},{28,8},{1,21},{... | collective-permute-start | bytes 196616 | tf_op jit(solution)/shard_map/ppermute | solution.py:18
  12.8 5.0 %collective-permute-start.5 = (bf16[128,256]{1,0:T(8,128)(2,1)S(1)}, bf16[128,256]{1,0:T(8,128)(2,1)S(1)}, u32[]{:S(2)}, u32[]{:S(2)}) collective-permute-start(bf16[128,256]{1,0:T(8,128)(2,1)S(1)} %get-tuple-element.30.own), channel_id=1, source_target_pairs={{0,28},{4,24},{8,20},{12,16},{16,12},{20,8},{24,4},{28,0},{1,29},{... | collective-permute-start | bytes 196616 | tf_op jit(solution)/shard_map/ppermute | solution.py:18
  15.0 4.3 %collective-permute-start.4 = (bf16[128,256]{1,0:T(8,128)(2,1)S(1)}, bf16[128,256]{1,0:T(8,128)(2,1)S(1)}, u32[]{:S(2)}, u32[]{:S(2)}) collective-permute-start(bf16[128,256]{1,0:T(8,128)(2,1)S(1)} %get-tuple-element.30.own), channel_id=1, source_target_pairs={{0,20},{4,16},{8,28},{12,24},{16,4},{20,0},{24,12},{28,8},{1,21},{... | collective-permute-start | bytes 196616 | tf_op jit(solution)/shard_map/ppermute | solution.py:18
  15.6 4.2 %collective-permute-start.7 = (bf16[128,256]{1,0:T(8,128)(2,1)S(1)}, bf16[128,256]{1,0:T(8,128)(2,1)S(1)}, u32[]{:S(2)}, u32[]{:S(2)}) collective-permute-start(bf16[128,256]{1,0:T(8,128)(2,1)S(1)} %get-tuple-element.30.own), channel_id=1, source_target_pairs={{0,12},{4,8},{8,4},{12,0},{16,28},{20,24},{24,20},{28,16},{1,13},{... | collective-permute-start | bytes 196616 | tf_op jit(solution)/shard_map/ppermute | solution.py:18
  15.9 3.4 %collective-permute-start.6 = (bf16[128,256]{1,0:T(8,128)(2,1)S(1)}, bf16[128,256]{1,0:T(8,128)(2,1)S(1)}, u32[]{:S(2)}, u32[]{:S(2)}) collective-permute-start(bf16[128,256]{1,0:T(8,128)(2,1)S(1)} %get-tuple-element.30.own), channel_id=1, source_target_pairs={{0,4},{4,0},{8,12},{12,8},{16,20},{20,16},{24,28},{28,24},{1,5},{5... | collective-permute-start | bytes 196616 | tf_op jit(solution)/shard_map/ppermute | solution.py:18
  19.3 1.8 %collective-permute-start.9 = (bf16[256,256]{1,0:T(8,128)(2,1)S(1)}, bf16[256,256]{1,0:T(8,128)(2,1)S(1)}, u32[]{:S(2)}, u32[]{:S(2)}) collective-permute-start(bf16[256,256]{1,0:T(8,128)(2,1)S(1)} %pad_maximum_fusion.early), channel_id=1, source_target_pairs={{0,4},{4,0},{8,12},{12,8},{16,20},{20,16},{24,28},{28,24},{1,5},{5... | collective-permute-start | bytes 393224 | tf_op jit(solution)/shard_map/ppermute | solution.py:18
  19.8 1.3 %collective-permute-start.8 = (bf16[128,256]{1,0:T(8,128)(2,1)S(1)}, bf16[128,256]{1,0:T(8,128)(2,1)S(1)}, u32[]{:S(2)}, u32[]{:S(2)}) collective-permute-start(bf16[128,256]{1,0:T(8,128)(2,1)S(1)} %collective-permute-done.7.late), channel_id=1, source_target_pairs={{0,4},{4,0},{8,12},{12,8},{16,20},{20,16},{24,28},{28,24},{1,5},{5... | collective-permute-start | bytes 196616 | tf_op jit(solution)/shard_map/ppermute | solution.py:18
  21.4 5.7 %collective-permute-start.10 = (bf16[256,256]{1,0:T(8,128)(2,1)S(1)}, bf16[256,256]{1,0:T(8,128)(2,1)S(1)}, u32[]{:S(2)}, u32[]{:S(2)}) collective-permute-start(bf16[256,256]{1,0:T(8,128)(2,1)S(1)} %shard_map.115), channel_id=1, source_target_pairs={{0,1},{1,0},{2,3},{3,2},{4,5},{5,4},{6,7},{7,6},{8,9},{9,8},{10,11... | collective-permute-start | bytes 393224 | tf_op jit(solution)/shard_map/ppermute | solution.py:18
  27.1 6.9 %collective-permute-start.11 = (bf16[256,256]{1,0:T(8,128)(2,1)S(1)}, bf16[256,256]{1,0:T(8,128)(2,1)S(1)}, u32[]{:S(2)}, u32[]{:S(2)}) collective-permute-start(bf16[256,256]{1,0:T(8,128)(2,1)S(1)} %add_convert_fusion), channel_id=1, source_target_pairs={{0,3},{1,2},{2,1},{3,0},{4,7},{5,6},{6,5},{7,4},{8,11},{9,10},{10,... | collective-permute-start | bytes 393224 | tf_op jit(solution)/shard_map/ppermute | solution.py:18

commit v4 on v3

--- a/solution.py
+++ b/solution.py
@@ -18,7 +18,15 @@
     return lax.ppermute(value, axis, [(i, i ^ flip) for i in range(size)])
 
 
-def project_blocks(flips, order, tile_src, tile_count, feats, tiles, w_self, w_neigh, rows_out, sums_out):
+def copy_all(pairs, sems):
+    copies = [pltpu.make_async_copy(source, target, sems.at[i]) for i, (source, target) in enumerate(pairs)]
+    for copy in copies:
+        copy.start()
+    for copy in copies:
+        copy.wait()
+
+
+def project_blocks(flips, order, tile_src, tile_count, feats, tiles, weights, rows_out, sums_out):
     block_rows = tiles.shape[2]
     tile_slots = tiles.shape[1]
     me = lax.axis_index("feat")
@@ -26,8 +34,8 @@
     def block_of(index):
         return feats[pl.ds(pl.multiple_of(index * block_rows, block_rows), block_rows), :]
 
-    for j, (even, odd) in enumerate(flips):
-        block = order[0, me ^ jnp.where(me % 2 == 0, even, odd)]
+    for j, flip in enumerate(flips):
+        block = order[0, me ^ flip]
         mean = jnp.zeros((block_rows, feats.shape[1]), jnp.float32)
         for k in range(tile_slots):
             tile = tiles[block, k]
@@ -36,20 +44,35 @@
         rows_out[pl.ds(j * block_rows, block_rows), :] = jnp.concatenate(
             [block_of(block), mean.astype(jnp.bfloat16)], axis=1
         )
-    weights = jnp.concatenate([w_self[...], w_neigh[...]], axis=0)
-    sums_out[...] = jnp.dot(rows_out[...], weights, preferred_element_type=jnp.float32).astype(sums_out.dtype)
-
-
-def load_and_project(flips, *refs):
-    loaded_from, rows_out, sums_out, loaded, sems = refs[:7], refs[7], refs[8], refs[9:16], refs[16]
-    copies = []
-    for i, (source, target) in enumerate(zip(loaded_from, loaded)):
-        source = source.at[0] if len(source.shape) > len(target.shape) else source
-        copies.append(pltpu.make_async_copy(source, target, sems.at[i]))
-        copies[-1].start()
-    for copy in copies:
-        copy.wait()
-    project_blocks(flips, *loaded, rows_out, sums_out)
+    sums_out[...] = jnp.dot(rows_out[...], weights[...], preferred_element_type=jnp.float32).astype(sums_out.dtype)
+
+
+def load_and_project(
+    flips, order_hbm, tile_src_hbm, tile_count_hbm, feats_hbm, tiles_hbm, w_self, w_neigh,
+    rows_out, sums_out, feats, tiles, weights, order, tile_src, tile_count, sems,
+):
+    columns = feats.shape[1]
+    copy_all(
+        (
+            (order_hbm, order),
+            (tile_src_hbm, tile_src),
+            (tile_count_hbm, tile_count),
+            (feats_hbm.at[0], feats),
+            (tiles_hbm.at[0], tiles),
+            (w_self, weights.at[pl.ds(0, columns)]),
+            (w_neigh, weights.at[pl.ds(columns, columns)]),
+        ),
+        sems,
+    )
+    project_blocks(flips, order, tile_src, tile_count, feats, tiles, weights, rows_out, sums_out)
+
+
+def project_loaded(
+    flips, order_hbm, tile_src_hbm, tile_count_hbm, feats, tiles, weights,
+    rows_out, sums_out, order, tile_src, tile_count, sems,
+):
+    copy_all(((order_hbm, order), (tile_src_hbm, tile_src), (tile_count_hbm, tile_count)), sems)
+    project_blocks(flips, order, tile_src, tile_count, feats, tiles, weights, rows_out, sums_out)
 
 
 def first_products(kept_rows, given_rows, own, partner, early, total_out):
@@ -78,24 +101,16 @@
     def swap_cores(value):
         return exchange(value, "feat", n_feat, 1)
 
-    kept_flips = tuple((2 * j + (j > 0), 2 * j + (j > 0)) for j in range(n_chip))
-    given_flips = tuple((odd ^ 1, even ^ 1) for even, odd in kept_flips)
+    kept_flips = (0,) + tuple(2 * j + 1 for j in range(1, n_chip))
+    given_flips = tuple(flip ^ 1 for flip in kept_flips)
     tiles_of_slot = jnp.transpose(tile_src, (2, 0, 1))
 
     operands = (owner_order, tiles_of_slot, tile_count, feats, tile_weight, w_self, w_neigh)
-    smem, vmem = pl.BlockSpec(memory_space=pltpu.SMEM), pl.BlockSpec(memory_space=pltpu.VMEM)
-    loaded_specs = (smem,) * 3 + (vmem,) * 4
-    loaded_shapes = tuple(
-        jax.ShapeDtypeStruct(a.shape if i < 3 or i > 4 else a.shape[1:], a.dtype) for i, a in enumerate(operands)
-    )
-    params = dict(
-        compiler_params=pltpu.CompilerParams(vmem_limit_bytes=32 * 1024 * 1024),
-        cost_estimate=pl.CostEstimate(
-            flops=2 * rows * (tile_slots * block_rows * columns + 2 * columns * hidden_units),
-            bytes_accessed=feats.size * 2 + tile_weight.size + rows * 8 * columns,
-            transcendentals=0,
-        ),
-    )
+    operands = tuple(pltpu.with_memory_space_constraint(a, pltpu.HBM) for a in operands)
+    vmem = pl.BlockSpec(memory_space=pltpu.VMEM)
+    params = pltpu.CompilerParams(vmem_limit_bytes=32 * 1024 * 1024)
+    hbm = pl.BlockSpec(memory_space=pltpu.HBM)
+    indices = [pltpu.SMEM(a.shape, jnp.int32) for a in operands[:3]]
 
     def results(dtype):
         return (
@@ -103,22 +118,34 @@
             jax.ShapeDtypeStruct((rows, hidden_units), dtype),
         )
 
-    operands = tuple(pltpu.with_memory_space_constraint(a, pltpu.HBM) for a in operands)
+    estimate = pl.CostEstimate(
+        flops=2 * rows * (tile_slots * block_rows * columns + 2 * columns * hidden_units),
+        bytes_accessed=feats.size * 2 + tile_weight.size,
+        transcendentals=0,
+    )
     given_rows, given, *loaded = pl.pallas_call(
         functools.partial(load_and_project, given_flips),
-        out_shape=results(jnp.bfloat16) + loaded_shapes,
-        in_specs=[pl.BlockSpec(memory_space=pltpu.HBM)] * 7,
-        out_specs=(vmem,) * 2 + loaded_specs,
-        scratch_shapes=[pltpu.SemaphoreType.DMA((7,))],
-        **params,
+        out_shape=results(jnp.bfloat16)
+        + (
+            jax.ShapeDtypeStruct(feats.shape[1:], jnp.bfloat16),
+            jax.ShapeDtypeStruct(tile_weight.shape[1:], jnp.bfloat16),
+            jax.ShapeDtypeStruct((2 * columns, hidden_units), jnp.bfloat16),
+        ),
+        in_specs=[hbm] * 7,
+        out_specs=(vmem,) * 5,
+        scratch_shapes=indices + [pltpu.SemaphoreType.DMA((7,))],
+        compiler_params=params,
+        cost_estimate=estimate,
     )(*operands)
     kept_rows, kept = pl.pallas_call(
-        functools.partial(project_blocks, kept_flips),
+        functools.partial(project_loaded, kept_flips),
         out_shape=results(jnp.float32),
-        in_specs=loaded_specs,
+        in_specs=[hbm] * 3 + [vmem] * 3,
         out_specs=(vmem,) * 2,
-        **params,
-    )(*loaded)
+        scratch_shapes=indices + [pltpu.SemaphoreType.DMA((3,))],
+        compiler_params=params,
+        cost_estimate=estimate,
+    )(*operands[:3], *loaded)
 
     from_core = swap_cores(given)
     chip_sums = kept + from_core.astype(jnp.float32)
@@ -148,7 +175,7 @@
         out_shape=jax.ShapeDtypeStruct((2 * columns, hidden_units), jnp.float32),
         in_specs=(vmem,) * 5,
         out_specs=vmem,
-        compiler_params=params["compiler_params"],
+        compiler_params=params,
         cost_estimate=products,
     )(kept_rows, given_rows, output_grad, partner, early)
     grads = pl.pallas_call(
@@ -156,7 +183,7 @@
         out_shape=jax.ShapeDtypeStruct((2 * columns, hidden_units), jnp.bfloat16),
         in_specs=(vmem,) * 6,
         out_specs=vmem,
-        compiler_params=params["compiler_params"],
+        compiler_params=params,
         cost_estimate=products,
     )(total, kept_rows, given_rows, received[0], others_late, others_early)
 

time: 34.9 us -> 34.6 us (level)
  transfers between devices with their start and end apart: 12 -> 12, of which waited for: 9 -> 8; matrix products, arithmetic and copies ran while one was open for 2% -> 2% of each run, Pallas kernels for 4% -> 4%
where the time goes in v4:
time: 34.6 us; the launch traced here: 34.4 us
  waiting for transfers between devices  14.4 us (42%)
  starting transfers between devices  14.1 us (41%)
  Pallas kernels  3.55 us (10%)
  other arithmetic  0.9 us (3%)
  local copies, waits for them, and re-layouts  0.74 us (2%)
  between operations  0.73 us (2%)
    ppermute x12, waiting for transfers between devices, exchange(): return lax.ppermute(value, axis, [(i, i ^ flip) for i in range(size)])  14.4 us
    ppermute x12, starting transfers between devices, exchange(): return lax.ppermute(value, axis, [(i, i ^ flip) for i in range(size)])  14.1 us
    pallas_call x1, Pallas kernels, body(): pl.pallas_call(functools.partial(load_and_project, given_flips), out_shap...  1.79 us
    pallas_call x1, Pallas kernels, body(): pl.pallas_call(functools.partial(project_loaded, kept_flips), out_shape=r...  1.18 us
    slice x1, local copies, waits for them, and re-layouts, body(): return (hidden[None], grads[:columns], grads[columns:])  0.72 us
  transfers between devices with their start and end apart: 12, of which 8 were waited for; matrix products, arithmetic and copies ran while one was open for 2% of the time, Pallas kernels for 4%

profile of v4, /device:TPU:0, one launch (start us, length us, event | category | flops | bytes accessed | tf_op | source)
XLA Modules:
  0.0 34.4 jit_solution(6198754616405669455)
XLA Ops:
  0.6 1.8 %shard_map.112 = (bf16[512,256]{1,0:T(8,128)(2,1)S(1)}, bf16[512,256]{1,0:T(8,128)(2,1)S(1)}, bf16[2048,128]{1,0:T(8,128)(2,1)S(1)}, bf16[8,3,128,128]{3,2,1,0:T(8,128)(2,1)S(1)}, bf16[256,256]{1,0:T(8,128)(2,1)S(1)}) custom-call(s32[1,8]{1,0:T(1,128)} %order_hbm.3, s32[3,1,8]{2,1,0:T(1,128)} %bitcast.6, s32[1,8]{1,0:T(1,128)} %tile_count_hbm.3, ...), custom_call_target="tpu_custom_call" | custom-call | flops 117440512 | bytes 917504 | tf_op jit(solution)/shard_map/pallas_call | solution.py:126
  2.4 0.5 %collective-permute-start = (bf16[512,256]{1,0:T(8,128)(2,1)S(1)}, bf16[512,256]{1,0:T(8,128)(2,1)S(1)}, u32[]{:S(2)}, u32[]{:S(2)}) collective-permute-start(bf16[512,256]{1,0:T(8,128)(2,1)S(1)} %get-tuple-element.18), channel_id=1, source_target_pairs={{0,4},{4,0},{8,12},{12,8},{16,20},{20,16},{24,28},{28,24},{1,5},{5... | collective-permute-start | bytes 786440 | tf_op jit(solution)/shard_map/ppermute | solution.py:18
  3.0 1.2 %shard_map.113 = (bf16[512,256]{1,0:T(8,128)(2,1)S(1)}, f32[512,256]{1,0:T(8,128)S(1)}) custom-call(s32[1,8]{1,0:T(1,128)} %order_hbm.3, s32[3,1,8]{2,1,0:T(1,128)} %bitcast.7, s32[1,8]{1,0:T(1,128)} %tile_count_hbm.3, bf16[2048,128]{1,0:T(8,128)(2,1)S(1)} %get-tuple-element.14.feats, bf16[8,3,128,128]{3,2,1,0:T(8,128)(2,1)S(1)} %get-tuple-element.15.tiles, ...), custom_call_target="tpu_custom_call" | custom-call | flops 117440512 | bytes 917504 | tf_op jit(solution)/shard_map/pallas_call | solution.py:140
  4.3 3.6 %collective-permute-start.1 = (bf16[128,256]{1,0:T(8,128)(2,1)S(1)}, bf16[128,256]{1,0:T(8,128)(2,1)S(1)}, u32[]{:S(2)}, u32[]{:S(2)}) collective-permute-start(bf16[128,256]{1,0:T(8,128)(2,1)S(1)} %get-tuple-element.31), channel_id=1, source_target_pairs={{0,28},{4,24},{8,20},{12,16},{16,12},{20,8},{24,4},{28,0},{1,29},{... | collective-permute-start | bytes 196616 | tf_op jit(solution)/shard_map/ppermute | solution.py:18
  7.9 0.5 %collective-permute-start.3 = (bf16[128,256]{1,0:T(8,128)(2,1)S(1)}, bf16[128,256]{1,0:T(8,128)(2,1)S(1)}, u32[]{:S(2)}, u32[]{:S(2)}) collective-permute-start(bf16[128,256]{1,0:T(8,128)(2,1)S(1)} %get-tuple-element.32), channel_id=1, source_target_pairs={{0,12},{4,8},{8,4},{12,0},{16,28},{20,24},{24,20},{28,16},{1,13},{... | collective-permute-start | bytes 196616 | tf_op jit(solution)/shard_map/ppermute | solution.py:18
  8.5 1.8 %collective-permute-done.1 = bf16[128,256]{1,0:T(8,128)(2,1)S(1)} collective-permute-done((bf16[128,256]{1,0:T(8,128)(2,1)S(1)}, bf16[128,256]{1,0:T(8,128)(2,1)S(1)}, u32[]{:S(2)}, u32[]{:S(2)}) %collective-permute-start.1) | collective-permute-done | bytes 65568 | tf_op jit(solution)/shard_map/ppermute | solution.py:18
  10.3 1.8 %collective-permute-done.3 = bf16[128,256]{1,0:T(8,128)(2,1)S(1)} collective-permute-done((bf16[128,256]{1,0:T(8,128)(2,1)S(1)}, bf16[128,256]{1,0:T(8,128)(2,1)S(1)}, u32[]{:S(2)}, u32[]{:S(2)}) %collective-permute-start.3) | collective-permute-done | bytes 65568 | tf_op jit(solution)/shard_map/ppermute | solution.py:18
  12.1 0.4 %collective-permute-done.2 = bf16[128,256]{1,0:T(8,128)(2,1)S(1)} collective-permute-done((bf16[128,256]{1,0:T(8,128)(2,1)S(1)}, bf16[128,256]{1,0:T(8,128)(2,1)S(1)}, u32[]{:S(2)}, u32[]{:S(2)}) %collective-permute-start.2) | collective-permute-done | bytes 65568 | tf_op jit(solution)/shard_map/ppermute | solution.py:18
  12.6 2.1 %collective-permute-start.5 = (bf16[128,256]{1,0:T(8,128)(2,1)S(1)}, bf16[128,256]{1,0:T(8,128)(2,1)S(1)}, u32[]{:S(2)}, u32[]{:S(2)}) collective-permute-start(bf16[128,256]{1,0:T(8,128)(2,1)S(1)} %get-tuple-element.22.own), channel_id=1, source_target_pairs={{0,28},{4,24},{8,20},{12,16},{16,12},{20,8},{24,4},{28,0},{1,29},{... | collective-permute-start | bytes 196616 | tf_op jit(solution)/shard_map/ppermute | solution.py:18
  14.6 0.7 %collective-permute-start.4 = (bf16[128,256]{1,0:T(8,128)(2,1)S(1)}, bf16[128,256]{1,0:T(8,128)(2,1)S(1)}, u32[]{:S(2)}, u32[]{:S(2)}) collective-permute-start(bf16[128,256]{1,0:T(8,128)(2,1)S(1)} %get-tuple-element.22.own), channel_id=1, source_target_pairs={{0,20},{4,16},{8,28},{12,24},{16,4},{20,0},{24,12},{28,8},{1,21},{... | collective-permute-start | bytes 196616 | tf_op jit(solution)/shard_map/ppermute | solution.py:18
  15.4 0.2 collective-permute-start.7
  15.6 0.4 %collective-permute-start.6 = (bf16[128,256]{1,0:T(8,128)(2,1)S(1)}, bf16[128,256]{1,0:T(8,128)(2,1)S(1)}, u32[]{:S(2)}, u32[]{:S(2)}) collective-permute-start(bf16[128,256]{1,0:T(8,128)(2,1)S(1)} %get-tuple-element.22.own), channel_id=1, source_target_pairs={{0,4},{4,0},{8,12},{12,8},{16,20},{20,16},{24,28},{28,24},{1,5},{5... | collective-permute-start | bytes 196616 | tf_op jit(solution)/shard_map/ppermute | solution.py:18
  16.0 1.6 %collective-permute-done.5 = bf16[128,256]{1,0:T(8,128)(2,1)S(1)} collective-permute-done((bf16[128,256]{1,0:T(8,128)(2,1)S(1)}, bf16[128,256]{1,0:T(8,128)(2,1)S(1)}, u32[]{:S(2)}, u32[]{:S(2)}) %collective-permute-start.5) | collective-permute-done | bytes 65568 | tf_op jit(solution)/shard_map/ppermute | solution.py:18
  17.6 1.4 %collective-permute-done.4 = bf16[128,256]{1,0:T(8,128)(2,1)S(1)} collective-permute-done((bf16[128,256]{1,0:T(8,128)(2,1)S(1)}, bf16[128,256]{1,0:T(8,128)(2,1)S(1)}, u32[]{:S(2)}, u32[]{:S(2)}) %collective-permute-start.4) | collective-permute-done | bytes 65568 | tf_op jit(solution)/shard_map/ppermute | solution.py:18
  19.0 0.5 %collective-permute-start.9 = (bf16[256,256]{1,0:T(8,128)(2,1)S(1)}, bf16[256,256]{1,0:T(8,128)(2,1)S(1)}, u32[]{:S(2)}, u32[]{:S(2)}) collective-permute-start(bf16[256,256]{1,0:T(8,128)(2,1)S(1)} %pad_maximum_fusion.early), channel_id=1, source_target_pairs={{0,4},{4,0},{8,12},{12,8},{16,20},{20,16},{24,28},{28,24},{1,5},{5... | collective-permute-start | bytes 393224 | tf_op jit(solution)/shard_map/ppermute | solution.py:18
  19.6 0.3 shard_map.114.total
  19.9 0.9 %collective-permute-done.8.others_late = bf16[128,256]{1,0:T(8,128)(2,1)S(1)} collective-permute-done((bf16[128,256]{1,0:T(8,128)(2,1)S(1)}, bf16[128,256]{1,0:T(8,128)(2,1)S(1)}, u32[]{:S(2)}, u32[]{:S(2)}) %collective-permute-start.8) | collective-permute-done | bytes 65568 | tf_op jit(solution)/shard_map/ppermute | solution.py:18
  20.8 0.3 shard_map.115
  21.1 1.7 %collective-permute-start.10 = (bf16[256,256]{1,0:T(8,128)(2,1)S(1)}, bf16[256,256]{1,0:T(8,128)(2,1)S(1)}, u32[]{:S(2)}, u32[]{:S(2)}) collective-permute-start(bf16[256,256]{1,0:T(8,128)(2,1)S(1)} %shard_map.115), channel_id=1, source_target_pairs={{0,1},{1,0},{2,3},{3,2},{4,5},{5,4},{6,7},{7,6},{8,9},{9,8},{10,11... | collective-permute-start | bytes 393224 | tf_op jit(solution)/shard_map/ppermute | solution.py:18
  22.8 4.0 %collective-permute-done.10 = bf16[256,256]{1,0:T(8,128)(2,1)S(1)} collective-permute-done((bf16[256,256]{1,0:T(8,128)(2,1)S(1)}, bf16[256,256]{1,0:T(8,128)(2,1)S(1)}, u32[]{:S(2)}, u32[]{:S(2)}) %collective-permute-start.10) | collective-permute-done | bytes 131104 | tf_op jit(solution)/shard_map/ppermute | solution.py:18
  26.8 3.7 %collective-permute-start.11 = (bf16[256,256]{1,0:T(8,128)(2,1)S(1)}, bf16[256,256]{1,0:T(8,128)(2,1)S(1)}, u32[]{:S(2)}, u32[]{:S(2)}) collective-permute-start(bf16[256,256]{1,0:T(8,128)(2,1)S(1)} %add_convert_fusion), channel_id=1, source_target_pairs={{0,3},{1,2},{2,1},{3,0},{4,7},{5,6},{6,5},{7,4},{8,11},{9,10},{10,... | collective-permute-start | bytes 393224 | tf_op jit(solution)/shard_map/ppermute | solution.py:18
  30.5 0.7 %fusion.5 = bf16[1,128,256]{2,1,0:T(8,128)(2,1)} fusion(f32[128,256]{1,0:T(8,128)S(1)} %get-tuple-element.19), kind=kLoop, calls=%fused_computation.12 | loop fusion | flops 163840 | bytes 196608 | tf_op jit(solution)/shard_map/broadcast_in_dim | solution.py:196
  31.1 2.5 %collective-permute-done.11 = bf16[256,256]{1,0:T(8,128)(2,1)S(1)} collective-permute-done((bf16[256,256]{1,0:T(8,128)(2,1)S(1)}, bf16[256,256]{1,0:T(8,128)(2,1)S(1)}, u32[]{:S(2)}, u32[]{:S(2)}) %collective-permute-start.11) | collective-permute-done | bytes 131104 | tf_op jit(solution)/shard_map/ppermute | solution.py:18
  33.7 0.7 %fusion.8 = (f32[128,256]{1,0:T(8,128)}, f32[128,256]{1,0:T(8,128)}) fusion(f32[256,256]{1,0:T(8,128)S(1)} %convert_add_fusion.1), kind=kLoop, calls=%fused_computation.14 | loop fusion | bytes 524288 | tf_op jit(solution)/shard_map/slice | solution.py:196
  (16 shorter events, 0.5 us)
Async XLA Ops:
  2.4 1.7 %collective-permute-start = (bf16[512,256]{1,0:T(8,128)(2,1)S(1)}, bf16[512,256]{1,0:T(8,128)(2,1)S(1)}, u32[]{:S(2)}, u32[]{:S(2)}) collective-permute-start(bf16[512,256]{1,0:T(8,128)(2,1)S(1)} %get-tuple-element.18), channel_id=1, source_target_pairs={{0,4},{4,0},{8,12},{12,8},{16,20},{20,16},{24,28},{28,24},{1,5},{5... | collective-permute-start | bytes 786440 | tf_op jit(solution)/shard_map/ppermute | solution.py:18
  4.2 8.3 %copy-start = (bf16[1,128,256]{2,1,0:T(8,128)(2,1)S(1)}, bf16[1,128,256]{2,1,0:T(8,128)(2,1)}, u32[]{:S(2)}) copy-start(bf16[1,128,256]{2,1,0:T(8,128)(2,1)} %param.17) | copy-start | bytes 196612
  4.3 6.0 %collective-permute-start.1 = (bf16[128,256]{1,0:T(8,128)(2,1)S(1)}, bf16[128,256]{1,0:T(8,128)(2,1)S(1)}, u32[]{:S(2)}, u32[]{:S(2)}) collective-permute-start(bf16[128,256]{1,0:T(8,128)(2,1)S(1)} %get-tuple-element.31), channel_id=1, source_target_pairs={{0,28},{4,24},{8,20},{12,16},{16,12},{20,8},{24,4},{28,0},{1,29},{... | collective-permute-start | bytes 196616 | tf_op jit(solution)/shard_map/ppermute | solution.py:18
  7.9 4.2 %collective-permute-start.3 = (bf16[128,256]{1,0:T(8,128)(2,1)S(1)}, bf16[128,256]{1,0:T(8,128)(2,1)S(1)}, u32[]{:S(2)}, u32[]{:S(2)}) collective-permute-start(bf16[128,256]{1,0:T(8,128)(2,1)S(1)} %get-tuple-element.32), channel_id=1, source_target_pairs={{0,12},{4,8},{8,4},{12,0},{16,28},{20,24},{24,20},{28,16},{1,13},{... | collective-permute-start | bytes 196616 | tf_op jit(solution)/shard_map/ppermute | solution.py:18
  8.3 4.1 %copy-start.1 = (f32[256]{0:T(256)S(1)}, f32[256]{0:T(256)}, u32[]{:S(2)}) copy-start(f32[256]{0:T(256)} %param.12) | copy-start | bytes 3076
  8.4 4.1 %collective-permute-start.2 = (bf16[128,256]{1,0:T(8,128)(2,1)S(1)}, bf16[128,256]{1,0:T(8,128)(2,1)S(1)}, u32[]{:S(2)}, u32[]{:S(2)}) collective-permute-start(bf16[128,256]{1,0:T(8,128)(2,1)S(1)} %get-tuple-element.33), channel_id=1, source_target_pairs={{0,20},{4,16},{8,28},{12,24},{16,4},{20,0},{24,12},{28,8},{1,21},{... | collective-permute-start | bytes 196616 | tf_op jit(solution)/shard_map/ppermute | solution.py:18
  12.6 5.1 %collective-permute-start.5 = (bf16[128,256]{1,0:T(8,128)(2,1)S(1)}, bf16[128,256]{1,0:T(8,128)(2,1)S(1)}, u32[]{:S(2)}, u32[]{:S(2)}) collective-permute-start(bf16[128,256]{1,0:T(8,128)(2,1)S(1)} %get-tuple-element.22.own), channel_id=1, source_target_pairs={{0,28},{4,24},{8,20},{12,16},{16,12},{20,8},{24,4},{28,0},{1,29},{... | collective-permute-start | bytes 196616 | tf_op jit(solution)/shard_map/ppermute | solution.py:18
  14.6 4.4 %collective-permute-start.4 = (bf16[128,256]{1,0:T(8,128)(2,1)S(1)}, bf16[128,256]{1,0:T(8,128)(2,1)S(1)}, u32[]{:S(2)}, u32[]{:S(2)}) collective-permute-start(bf16[128,256]{1,0:T(8,128)(2,1)S(1)} %get-tuple-element.22.own), channel_id=1, source_target_pairs={{0,20},{4,16},{8,28},{12,24},{16,4},{20,0},{24,12},{28,8},{1,21},{... | collective-permute-start | bytes 196616 | tf_op jit(solution)/shard_map/ppermute | solution.py:18
  15.4 4.2 %collective-permute-start.7 = (bf16[128,256]{1,0:T(8,128)(2,1)S(1)}, bf16[128,256]{1,0:T(8,128)(2,1)S(1)}, u32[]{:S(2)}, u32[]{:S(2)}) collective-permute-start(bf16[128,256]{1,0:T(8,128)(2,1)S(1)} %get-tuple-element.22.own), channel_id=1, source_target_pairs={{0,12},{4,8},{8,4},{12,0},{16,28},{20,24},{24,20},{28,16},{1,13},{... | collective-permute-start | bytes 196616 | tf_op jit(solution)/shard_map/ppermute | solution.py:18
  15.6 3.5 %collective-permute-start.6 = (bf16[128,256]{1,0:T(8,128)(2,1)S(1)}, bf16[128,256]{1,0:T(8,128)(2,1)S(1)}, u32[]{:S(2)}, u32[]{:S(2)}) collective-permute-start(bf16[128,256]{1,0:T(8,128)(2,1)S(1)} %get-tuple-element.22.own), channel_id=1, source_target_pairs={{0,4},{4,0},{8,12},{12,8},{16,20},{20,16},{24,28},{28,24},{1,5},{5... | collective-permute-start | bytes 196616 | tf_op jit(solution)/shard_map/ppermute | solution.py:18
  19.0 1.8 %collective-permute-start.9 = (bf16[256,256]{1,0:T(8,128)(2,1)S(1)}, bf16[256,256]{1,0:T(8,128)(2,1)S(1)}, u32[]{:S(2)}, u32[]{:S(2)}) collective-permute-start(bf16[256,256]{1,0:T(8,128)(2,1)S(1)} %pad_maximum_fusion.early), channel_id=1, source_target_pairs={{0,4},{4,0},{8,12},{12,8},{16,20},{20,16},{24,28},{28,24},{1,5},{5... | collective-permute-start | bytes 393224 | tf_op jit(solution)/shard_map/ppermute | solution.py:18
  19.5 1.3 %collective-permute-start.8 = (bf16[128,256]{1,0:T(8,128)(2,1)S(1)}, bf16[128,256]{1,0:T(8,128)(2,1)S(1)}, u32[]{:S(2)}, u32[]{:S(2)}) collective-permute-start(bf16[128,256]{1,0:T(8,128)(2,1)S(1)} %collective-permute-done.7.late), channel_id=1, source_target_pairs={{0,4},{4,0},{8,12},{12,8},{16,20},{20,16},{24,28},{28,24},{1,5},{5... | collective-permute-start | bytes 196616 | tf_op jit(solution)/shard_map/ppermute | solution.py:18
  21.1 5.7 %collective-permute-start.10 = (bf16[256,256]{1,0:T(8,128)(2,1)S(1)}, bf16[256,256]{1,0:T(8,128)(2,1)S(1)}, u32[]{:S(2)}, u32[]{:S(2)}) collective-permute-start(bf16[256,256]{1,0:T(8,128)(2,1)S(1)} %shard_map.115), channel_id=1, source_target_pairs={{0,1},{1,0},{2,3},{3,2},{4,5},{5,4},{6,7},{7,6},{8,9},{9,8},{10,11... | collective-permute-start | bytes 393224 | tf_op jit(solution)/shard_map/ppermute | solution.py:18
  26.8 6.9 %collective-permute-start.11 = (bf16[256,256]{1,0:T(8,128)(2,1)S(1)}, bf16[256,256]{1,0:T(8,128)(2,1)S(1)}, u32[]{:S(2)}, u32[]{:S(2)}) collective-permute-start(bf16[256,256]{1,0:T(8,128)(2,1)S(1)} %add_convert_fusion), channel_id=1, source_target_pairs={{0,3},{1,2},{2,1},{3,0},{4,7},{5,6},{6,5},{7,4},{8,11},{9,10},{10,... | collective-permute-start | bytes 393224 | tf_op jit(solution)/shard_map/ppermute | solution.py:18

commit v5 on v4

--- a/solution.py
+++ b/solution.py
@@ -187,12 +187,13 @@
         cost_estimate=products,
     )(total, kept_rows, given_rows, received[0], others_late, others_early)
 
-    flip = 1
-    while flip < n_rep:
+    n_flips = n_rep.bit_length() - 1
+    for step in range(n_flips):
+        flips = (2 ** (n_flips - 1 - step), 2 ** (step + 1) - 1)
         sent = lax.optimization_barrier(grads.astype(jnp.bfloat16))
-        got = exchange(sent, "rep", n_rep, flip)
+        pairs = [(f * n_rep + r, f * n_rep + (r ^ flips[f % 2])) for f in range(n_feat) for r in range(n_rep)]
+        got = lax.ppermute(sent, ("feat", "rep"), pairs)
         grads = sent.astype(jnp.float32) + got.astype(jnp.float32)
-        flip = 2 * flip + 1
     return (hidden[None], grads[:columns], grads[columns:])
 
 

time: 34.6 us -> 33.6 us (0.971)
  starting transfers between devices: 14.1 us -> 13.3 us
    ppermute x12 -> x10, waiting for transfers between devices: 14.4 us -> 7.9 us  [exchange(): return lax.ppermute(value, axis, [(i, i ^ flip) for i in range(size)])]
    ppermute x0 -> x2, waiting for transfers between devices: none -> 6.23 us  [body(): got = lax.ppermute(sent, ('feat', 'rep'), pairs)]
    ppermute x12 -> x10, starting transfers between devices: 14.1 us -> 8.74 us  [exchange(): return lax.ppermute(value, axis, [(i, i ^ flip) for i in range(size)])]
    ppermute x0 -> x2, starting transfers between devices: none -> 4.61 us  [body(): got = lax.ppermute(sent, ('feat', 'rep'), pairs)]
where the time goes in v5:
time: 33.6 us; the launch traced here: 33.4 us
  waiting for transfers between devices  14.1 us (42%)
  starting transfers between devices  13.3 us (40%)
  Pallas kernels  3.55 us (11%)
  other arithmetic  0.9 us (3%)
  local copies, waits for them, and re-layouts  0.74 us (2%)
  between operations  0.73 us (2%)
    ppermute x10, starting transfers between devices, exchange(): return lax.ppermute(value, axis, [(i, i ^ flip) for i in range(size)])  8.74 us
    ppermute x10, waiting for transfers between devices, exchange(): return lax.ppermute(value, axis, [(i, i ^ flip) for i in range(size)])  7.9 us
    ppermute x2, waiting for transfers between devices, body(): got = lax.ppermute(sent, ('feat', 'rep'), pairs)  6.23 us
    ppermute x2, starting transfers between devices, body(): got = lax.ppermute(sent, ('feat', 'rep'), pairs)  4.61 us
    pallas_call x1, Pallas kernels, body(): pl.pallas_call(functools.partial(load_and_project, given_flips), out_shap...  1.79 us
    pallas_call x1, Pallas kernels, body(): pl.pallas_call(functools.partial(project_loaded, kept_flips), out_shape=r...  1.18 us
    slice x1, local copies, waits for them, and re-layouts, body(): return (hidden[None], grads[:columns], grads[columns:])  0.72 us
    broadcast_in_dim x1, other arithmetic, body(): return (hidden[None], grads[:columns], grads[columns:])  0.67 us
  transfers between devices with their start and end apart: 12, of which 8 were waited for; matrix products, arithmetic and copies ran while one was open for 2% of the time, Pallas kernels for 4%

profile of v5, /device:TPU:0, one launch (start us, length us, event | category | flops | bytes accessed | tf_op | source)
XLA Modules:
  0.0 33.4 jit_solution(12491562305202228062)
XLA Ops:
  0.6 1.8 %shard_map.112 = (bf16[512,256]{1,0:T(8,128)(2,1)S(1)}, bf16[512,256]{1,0:T(8,128)(2,1)S(1)}, bf16[2048,128]{1,0:T(8,128)(2,1)S(1)}, bf16[8,3,128,128]{3,2,1,0:T(8,128)(2,1)S(1)}, bf16[256,256]{1,0:T(8,128)(2,1)S(1)}) custom-call(s32[1,8]{1,0:T(1,128)} %order_hbm.3, s32[3,1,8]{2,1,0:T(1,128)} %bitcast.6, s32[1,8]{1,0:T(1,128)} %tile_count_hbm.3, ...), custom_call_target="tpu_custom_call" | custom-call | flops 117440512 | bytes 917504 | tf_op jit(solution)/shard_map/pallas_call | solution.py:126
  2.4 0.5 %collective-permute-start = (bf16[512,256]{1,0:T(8,128)(2,1)S(1)}, bf16[512,256]{1,0:T(8,128)(2,1)S(1)}, u32[]{:S(2)}, u32[]{:S(2)}) collective-permute-start(bf16[512,256]{1,0:T(8,128)(2,1)S(1)} %get-tuple-element.18), channel_id=1, source_target_pairs={{0,4},{4,0},{8,12},{12,8},{16,20},{20,16},{24,28},{28,24},{1,5},{5... | collective-permute-start | bytes 786440 | tf_op jit(solution)/shard_map/ppermute | solution.py:18
  3.0 1.2 %shard_map.113 = (bf16[512,256]{1,0:T(8,128)(2,1)S(1)}, f32[512,256]{1,0:T(8,128)S(1)}) custom-call(s32[1,8]{1,0:T(1,128)} %order_hbm.3, s32[3,1,8]{2,1,0:T(1,128)} %bitcast.7, s32[1,8]{1,0:T(1,128)} %tile_count_hbm.3, bf16[2048,128]{1,0:T(8,128)(2,1)S(1)} %get-tuple-element.14.feats, bf16[8,3,128,128]{3,2,1,0:T(8,128)(2,1)S(1)} %get-tuple-element.15.tiles, ...), custom_call_target="tpu_custom_call" | custom-call | flops 117440512 | bytes 917504 | tf_op jit(solution)/shard_map/pallas_call | solution.py:140
  4.3 3.6 %collective-permute-start.1 = (bf16[128,256]{1,0:T(8,128)(2,1)S(1)}, bf16[128,256]{1,0:T(8,128)(2,1)S(1)}, u32[]{:S(2)}, u32[]{:S(2)}) collective-permute-start(bf16[128,256]{1,0:T(8,128)(2,1)S(1)} %get-tuple-element.31), channel_id=1, source_target_pairs={{0,28},{4,24},{8,20},{12,16},{16,12},{20,8},{24,4},{28,0},{1,29},{... | collective-permute-start | bytes 196616 | tf_op jit(solution)/shard_map/ppermute | solution.py:18
  7.9 0.5 %collective-permute-start.3 = (bf16[128,256]{1,0:T(8,128)(2,1)S(1)}, bf16[128,256]{1,0:T(8,128)(2,1)S(1)}, u32[]{:S(2)}, u32[]{:S(2)}) collective-permute-start(bf16[128,256]{1,0:T(8,128)(2,1)S(1)} %get-tuple-element.32), channel_id=1, source_target_pairs={{0,12},{4,8},{8,4},{12,0},{16,28},{20,24},{24,20},{28,16},{1,13},{... | collective-permute-start | bytes 196616 | tf_op jit(solution)/shard_map/ppermute | solution.py:18
  8.5 1.8 %collective-permute-done.1 = bf16[128,256]{1,0:T(8,128)(2,1)S(1)} collective-permute-done((bf16[128,256]{1,0:T(8,128)(2,1)S(1)}, bf16[128,256]{1,0:T(8,128)(2,1)S(1)}, u32[]{:S(2)}, u32[]{:S(2)}) %collective-permute-start.1) | collective-permute-done | bytes 65568 | tf_op jit(solution)/shard_map/ppermute | solution.py:18
  10.3 1.8 %collective-permute-done.3 = bf16[128,256]{1,0:T(8,128)(2,1)S(1)} collective-permute-done((bf16[128,256]{1,0:T(8,128)(2,1)S(1)}, bf16[128,256]{1,0:T(8,128)(2,1)S(1)}, u32[]{:S(2)}, u32[]{:S(2)}) %collective-permute-start.3) | collective-permute-done | bytes 65568 | tf_op jit(solution)/shard_map/ppermute | solution.py:18
  12.1 0.4 %collective-permute-done.2 = bf16[128,256]{1,0:T(8,128)(2,1)S(1)} collective-permute-done((bf16[128,256]{1,0:T(8,128)(2,1)S(1)}, bf16[128,256]{1,0:T(8,128)(2,1)S(1)}, u32[]{:S(2)}, u32[]{:S(2)}) %collective-permute-start.2) | collective-permute-done | bytes 65568 | tf_op jit(solution)/shard_map/ppermute | solution.py:18
  12.6 2.1 %collective-permute-start.5 = (bf16[128,256]{1,0:T(8,128)(2,1)S(1)}, bf16[128,256]{1,0:T(8,128)(2,1)S(1)}, u32[]{:S(2)}, u32[]{:S(2)}) collective-permute-start(bf16[128,256]{1,0:T(8,128)(2,1)S(1)} %get-tuple-element.22.own), channel_id=1, source_target_pairs={{0,28},{4,24},{8,20},{12,16},{16,12},{20,8},{24,4},{28,0},{1,29},{... | collective-permute-start | bytes 196616 | tf_op jit(solution)/shard_map/ppermute | solution.py:18
  14.6 0.7 %collective-permute-start.4 = (bf16[128,256]{1,0:T(8,128)(2,1)S(1)}, bf16[128,256]{1,0:T(8,128)(2,1)S(1)}, u32[]{:S(2)}, u32[]{:S(2)}) collective-permute-start(bf16[128,256]{1,0:T(8,128)(2,1)S(1)} %get-tuple-element.22.own), channel_id=1, source_target_pairs={{0,20},{4,16},{8,28},{12,24},{16,4},{20,0},{24,12},{28,8},{1,21},{... | collective-permute-start | bytes 196616 | tf_op jit(solution)/shard_map/ppermute | solution.py:18
  15.4 0.2 collective-permute-start.7
  15.6 0.4 %collective-permute-start.6 = (bf16[128,256]{1,0:T(8,128)(2,1)S(1)}, bf16[128,256]{1,0:T(8,128)(2,1)S(1)}, u32[]{:S(2)}, u32[]{:S(2)}) collective-permute-start(bf16[128,256]{1,0:T(8,128)(2,1)S(1)} %get-tuple-element.22.own), channel_id=1, source_target_pairs={{0,4},{4,0},{8,12},{12,8},{16,20},{20,16},{24,28},{28,24},{1,5},{5... | collective-permute-start | bytes 196616 | tf_op jit(solution)/shard_map/ppermute | solution.py:18
  16.0 1.6 %collective-permute-done.5 = bf16[128,256]{1,0:T(8,128)(2,1)S(1)} collective-permute-done((bf16[128,256]{1,0:T(8,128)(2,1)S(1)}, bf16[128,256]{1,0:T(8,128)(2,1)S(1)}, u32[]{:S(2)}, u32[]{:S(2)}) %collective-permute-start.5) | collective-permute-done | bytes 65568 | tf_op jit(solution)/shard_map/ppermute | solution.py:18
  17.6 1.4 %collective-permute-done.4 = bf16[128,256]{1,0:T(8,128)(2,1)S(1)} collective-permute-done((bf16[128,256]{1,0:T(8,128)(2,1)S(1)}, bf16[128,256]{1,0:T(8,128)(2,1)S(1)}, u32[]{:S(2)}, u32[]{:S(2)}) %collective-permute-start.4) | collective-permute-done | bytes 65568 | tf_op jit(solution)/shard_map/ppermute | solution.py:18
  19.0 0.5 %collective-permute-start.9 = (bf16[256,256]{1,0:T(8,128)(2,1)S(1)}, bf16[256,256]{1,0:T(8,128)(2,1)S(1)}, u32[]{:S(2)}, u32[]{:S(2)}) collective-permute-start(bf16[256,256]{1,0:T(8,128)(2,1)S(1)} %pad_maximum_fusion.early), channel_id=1, source_target_pairs={{0,4},{4,0},{8,12},{12,8},{16,20},{20,16},{24,28},{28,24},{1,5},{5... | collective-permute-start | bytes 393224 | tf_op jit(solution)/shard_map/ppermute | solution.py:18
  19.6 0.3 shard_map.114.total
  19.9 0.9 %collective-permute-done.8.others_late = bf16[128,256]{1,0:T(8,128)(2,1)S(1)} collective-permute-done((bf16[128,256]{1,0:T(8,128)(2,1)S(1)}, bf16[128,256]{1,0:T(8,128)(2,1)S(1)}, u32[]{:S(2)}, u32[]{:S(2)}) %collective-permute-start.8) | collective-permute-done | bytes 65568 | tf_op jit(solution)/shard_map/ppermute | solution.py:18
  20.8 0.3 shard_map.115
  21.1 2.7 %collective-permute-start.10 = (bf16[256,256]{1,0:T(8,128)(2,1)S(1)}, bf16[256,256]{1,0:T(8,128)(2,1)S(1)}, u32[]{:S(2)}, u32[]{:S(2)}) collective-permute-start(bf16[256,256]{1,0:T(8,128)(2,1)S(1)} %shard_map.115), channel_id=1, source_target_pairs={{0,2},{1,3},{2,0},{3,1},{4,5},{5,4},{6,7},{7,6},{8,10},{9,11},{10,... | collective-permute-start | bytes 393224 | tf_op jit(solution)/shard_map/ppermute | solution.py:195
  23.8 3.7 %collective-permute-done.10 = bf16[256,256]{1,0:T(8,128)(2,1)S(1)} collective-permute-done((bf16[256,256]{1,0:T(8,128)(2,1)S(1)}, bf16[256,256]{1,0:T(8,128)(2,1)S(1)}, u32[]{:S(2)}, u32[]{:S(2)}) %collective-permute-start.10) | collective-permute-done | bytes 131104 | tf_op jit(solution)/shard_map/ppermute | solution.py:195
  27.5 1.9 %collective-permute-start.11 = (bf16[256,256]{1,0:T(8,128)(2,1)S(1)}, bf16[256,256]{1,0:T(8,128)(2,1)S(1)}, u32[]{:S(2)}, u32[]{:S(2)}) collective-permute-start(bf16[256,256]{1,0:T(8,128)(2,1)S(1)} %add_convert_fusion), channel_id=1, source_target_pairs={{0,1},{1,0},{2,3},{3,2},{4,7},{5,6},{6,5},{7,4},{8,9},{9,8},{10,11... | collective-permute-start | bytes 393224 | tf_op jit(solution)/shard_map/ppermute | solution.py:195
  29.4 0.7 %fusion.5 = bf16[1,128,256]{2,1,0:T(8,128)(2,1)} fusion(f32[128,256]{1,0:T(8,128)S(1)} %get-tuple-element.19), kind=kLoop, calls=%fused_computation.12 | loop fusion | flops 163840 | bytes 196608 | tf_op jit(solution)/shard_map/broadcast_in_dim | solution.py:197
  30.1 2.5 %collective-permute-done.11 = bf16[256,256]{1,0:T(8,128)(2,1)S(1)} collective-permute-done((bf16[256,256]{1,0:T(8,128)(2,1)S(1)}, bf16[256,256]{1,0:T(8,128)(2,1)S(1)}, u32[]{:S(2)}, u32[]{:S(2)}) %collective-permute-start.11) | collective-permute-done | bytes 131104 | tf_op jit(solution)/shard_map/ppermute | solution.py:195
  32.7 0.7 %fusion.8 = (f32[128,256]{1,0:T(8,128)}, f32[128,256]{1,0:T(8,128)}) fusion(f32[256,256]{1,0:T(8,128)S(1)} %convert_add_fusion.1), kind=kLoop, calls=%fused_computation.14 | loop fusion | bytes 524288 | tf_op jit(solution)/shard_map/slice | solution.py:197
  (16 shorter events, 0.5 us)
Async XLA Ops:
  2.4 1.7 %collective-permute-start = (bf16[512,256]{1,0:T(8,128)(2,1)S(1)}, bf16[512,256]{1,0:T(8,128)(2,1)S(1)}, u32[]{:S(2)}, u32[]{:S(2)}) collective-permute-start(bf16[512,256]{1,0:T(8,128)(2,1)S(1)} %get-tuple-element.18), channel_id=1, source_target_pairs={{0,4},{4,0},{8,12},{12,8},{16,20},{20,16},{24,28},{28,24},{1,5},{5... | collective-permute-start | bytes 786440 | tf_op jit(solution)/shard_map/ppermute | solution.py:18
  4.2 8.3 %copy-start = (bf16[1,128,256]{2,1,0:T(8,128)(2,1)S(1)}, bf16[1,128,256]{2,1,0:T(8,128)(2,1)}, u32[]{:S(2)}) copy-start(bf16[1,128,256]{2,1,0:T(8,128)(2,1)} %param.17) | copy-start | bytes 196612
  4.3 6.0 %collective-permute-start.1 = (bf16[128,256]{1,0:T(8,128)(2,1)S(1)}, bf16[128,256]{1,0:T(8,128)(2,1)S(1)}, u32[]{:S(2)}, u32[]{:S(2)}) collective-permute-start(bf16[128,256]{1,0:T(8,128)(2,1)S(1)} %get-tuple-element.31), channel_id=1, source_target_pairs={{0,28},{4,24},{8,20},{12,16},{16,12},{20,8},{24,4},{28,0},{1,29},{... | collective-permute-start | bytes 196616 | tf_op jit(solution)/shard_map/ppermute | solution.py:18
  7.9 4.2 %collective-permute-start.3 = (bf16[128,256]{1,0:T(8,128)(2,1)S(1)}, bf16[128,256]{1,0:T(8,128)(2,1)S(1)}, u32[]{:S(2)}, u32[]{:S(2)}) collective-permute-start(bf16[128,256]{1,0:T(8,128)(2,1)S(1)} %get-tuple-element.32), channel_id=1, source_target_pairs={{0,12},{4,8},{8,4},{12,0},{16,28},{20,24},{24,20},{28,16},{1,13},{... | collective-permute-start | bytes 196616 | tf_op jit(solution)/shard_map/ppermute | solution.py:18
  8.3 4.1 %copy-start.1 = (f32[256]{0:T(256)S(1)}, f32[256]{0:T(256)}, u32[]{:S(2)}) copy-start(f32[256]{0:T(256)} %param.12) | copy-start | bytes 3076
  8.4 4.1 %collective-permute-start.2 = (bf16[128,256]{1,0:T(8,128)(2,1)S(1)}, bf16[128,256]{1,0:T(8,128)(2,1)S(1)}, u32[]{:S(2)}, u32[]{:S(2)}) collective-permute-start(bf16[128,256]{1,0:T(8,128)(2,1)S(1)} %get-tuple-element.33), channel_id=1, source_target_pairs={{0,20},{4,16},{8,28},{12,24},{16,4},{20,0},{24,12},{28,8},{1,21},{... | collective-permute-start | bytes 196616 | tf_op jit(solution)/shard_map/ppermute | solution.py:18
  12.6 5.1 %collective-permute-start.5 = (bf16[128,256]{1,0:T(8,128)(2,1)S(1)}, bf16[128,256]{1,0:T(8,128)(2,1)S(1)}, u32[]{:S(2)}, u32[]{:S(2)}) collective-permute-start(bf16[128,256]{1,0:T(8,128)(2,1)S(1)} %get-tuple-element.22.own), channel_id=1, source_target_pairs={{0,28},{4,24},{8,20},{12,16},{16,12},{20,8},{24,4},{28,0},{1,29},{... | collective-permute-start | bytes 196616 | tf_op jit(solution)/shard_map/ppermute | solution.py:18
  14.6 4.4 %collective-permute-start.4 = (bf16[128,256]{1,0:T(8,128)(2,1)S(1)}, bf16[128,256]{1,0:T(8,128)(2,1)S(1)}, u32[]{:S(2)}, u32[]{:S(2)}) collective-permute-start(bf16[128,256]{1,0:T(8,128)(2,1)S(1)} %get-tuple-element.22.own), channel_id=1, source_target_pairs={{0,20},{4,16},{8,28},{12,24},{16,4},{20,0},{24,12},{28,8},{1,21},{... | collective-permute-start | bytes 196616 | tf_op jit(solution)/shard_map/ppermute | solution.py:18
  15.4 4.2 %collective-permute-start.7 = (bf16[128,256]{1,0:T(8,128)(2,1)S(1)}, bf16[128,256]{1,0:T(8,128)(2,1)S(1)}, u32[]{:S(2)}, u32[]{:S(2)}) collective-permute-start(bf16[128,256]{1,0:T(8,128)(2,1)S(1)} %get-tuple-element.22.own), channel_id=1, source_target_pairs={{0,12},{4,8},{8,4},{12,0},{16,28},{20,24},{24,20},{28,16},{1,13},{... | collective-permute-start | bytes 196616 | tf_op jit(solution)/shard_map/ppermute | solution.py:18
  15.6 3.5 %collective-permute-start.6 = (bf16[128,256]{1,0:T(8,128)(2,1)S(1)}, bf16[128,256]{1,0:T(8,128)(2,1)S(1)}, u32[]{:S(2)}, u32[]{:S(2)}) collective-permute-start(bf16[128,256]{1,0:T(8,128)(2,1)S(1)} %get-tuple-element.22.own), channel_id=1, source_target_pairs={{0,4},{4,0},{8,12},{12,8},{16,20},{20,16},{24,28},{28,24},{1,5},{5... | collective-permute-start | bytes 196616 | tf_op jit(solution)/shard_map/ppermute | solution.py:18
  19.0 1.8 %collective-permute-start.9 = (bf16[256,256]{1,0:T(8,128)(2,1)S(1)}, bf16[256,256]{1,0:T(8,128)(2,1)S(1)}, u32[]{:S(2)}, u32[]{:S(2)}) collective-permute-start(bf16[256,256]{1,0:T(8,128)(2,1)S(1)} %pad_maximum_fusion.early), channel_id=1, source_target_pairs={{0,4},{4,0},{8,12},{12,8},{16,20},{20,16},{24,28},{28,24},{1,5},{5... | collective-permute-start | bytes 393224 | tf_op jit(solution)/shard_map/ppermute | solution.py:18
  19.5 1.3 %collective-permute-start.8 = (bf16[128,256]{1,0:T(8,128)(2,1)S(1)}, bf16[128,256]{1,0:T(8,128)(2,1)S(1)}, u32[]{:S(2)}, u32[]{:S(2)}) collective-permute-start(bf16[128,256]{1,0:T(8,128)(2,1)S(1)} %collective-permute-done.7.late), channel_id=1, source_target_pairs={{0,4},{4,0},{8,12},{12,8},{16,20},{20,16},{24,28},{28,24},{1,5},{5... | collective-permute-start | bytes 196616 | tf_op jit(solution)/shard_map/ppermute | solution.py:18
  21.1 6.4 %collective-permute-start.10 = (bf16[256,256]{1,0:T(8,128)(2,1)S(1)}, bf16[256,256]{1,0:T(8,128)(2,1)S(1)}, u32[]{:S(2)}, u32[]{:S(2)}) collective-permute-start(bf16[256,256]{1,0:T(8,128)(2,1)S(1)} %shard_map.115), channel_id=1, source_target_pairs={{0,2},{1,3},{2,0},{3,1},{4,5},{5,4},{6,7},{7,6},{8,10},{9,11},{10,... | collective-permute-start | bytes 393224 | tf_op jit(solution)/shard_map/ppermute | solution.py:195
  27.5 5.2 %collective-permute-start.11 = (bf16[256,256]{1,0:T(8,128)(2,1)S(1)}, bf16[256,256]{1,0:T(8,128)(2,1)S(1)}, u32[]{:S(2)}, u32[]{:S(2)}) collective-permute-start(bf16[256,256]{1,0:T(8,128)(2,1)S(1)} %add_convert_fusion), channel_id=1, source_target_pairs={{0,1},{1,0},{2,3},{3,2},{4,7},{5,6},{6,5},{7,4},{8,9},{9,8},{10,11... | collective-permute-start | bytes 393224 | tf_op jit(solution)/shard_map/ppermute | solution.py:195

commit v6 on v5

--- a/solution.py
+++ b/solution.py
@@ -151,7 +151,7 @@
     chip_sums = kept + from_core.astype(jnp.float32)
     arrived = [
         exchange(chip_sums[j * block_rows : (j + 1) * block_rows].astype(jnp.bfloat16), "feat", n_feat, 2 * j + 1)
-        for j in reversed(range(1, n_chip))
+        for j in sorted(range(1, n_chip), key=lambda j: (j.bit_count(), -j))
     ]
     preact = chip_sums[:block_rows] + bias
     for got in arrived:

time: 33.6 us -> 33.5 us (level)
  no operation moved by 1% of the time
where the time goes in v6:
time: 33.5 us; the launch traced here: 33.3 us
  waiting for transfers between devices  14.1 us (42%)
  starting transfers between devices  13.3 us (40%)
  Pallas kernels  3.55 us (11%)
  other arithmetic  0.9 us (3%)
  local copies, waits for them, and re-layouts  0.74 us (2%)
  between operations  0.73 us (2%)
    ppermute x10, starting transfers between devices, exchange(): return lax.ppermute(value, axis, [(i, i ^ flip) for i in range(size)])  8.69 us
    ppermute x10, waiting for transfers between devices, exchange(): return lax.ppermute(value, axis, [(i, i ^ flip) for i in range(size)])  7.78 us
    ppermute x2, waiting for transfers between devices, body(): got = lax.ppermute(sent, ('feat', 'rep'), pairs)  6.3 us
    ppermute x2, starting transfers between devices, body(): got = lax.ppermute(sent, ('feat', 'rep'), pairs)  4.6 us
    pallas_call x1, Pallas kernels, body(): pl.pallas_call(functools.partial(load_and_project, given_flips), out_shap...  1.79 us
    pallas_call x1, Pallas kernels, body(): pl.pallas_call(functools.partial(project_loaded, kept_flips), out_shape=r...  1.18 us
    slice x1, local copies, waits for them, and re-layouts, body(): return (hidden[None], grads[:columns], grads[columns:])  0.72 us
    broadcast_in_dim x1, other arithmetic, body(): return (hidden[None], grads[:columns], grads[columns:])  0.67 us
  transfers between devices with their start and end apart: 12, of which 8 were waited for; matrix products, arithmetic and copies ran while one was open for 2% of the time, Pallas kernels for 4%

profile of v6, /device:TPU:0, one launch (start us, length us, event | category | flops | bytes accessed | tf_op | source)
XLA Modules:
  0.0 33.3 jit_solution(8100823803510350114)
XLA Ops:
  0.6 1.8 %shard_map.112 = (bf16[512,256]{1,0:T(8,128)(2,1)S(1)}, bf16[512,256]{1,0:T(8,128)(2,1)S(1)}, bf16[2048,128]{1,0:T(8,128)(2,1)S(1)}, bf16[8,3,128,128]{3,2,1,0:T(8,128)(2,1)S(1)}, bf16[256,256]{1,0:T(8,128)(2,1)S(1)}) custom-call(s32[1,8]{1,0:T(1,128)} %order_hbm.3, s32[3,1,8]{2,1,0:T(1,128)} %bitcast.6, s32[1,8]{1,0:T(1,128)} %tile_count_hbm.3, ...), custom_call_target="tpu_custom_call" | custom-call | flops 117440512 | bytes 917504 | tf_op jit(solution)/shard_map/pallas_call | solution.py:126
  2.4 0.5 %collective-permute-start = (bf16[512,256]{1,0:T(8,128)(2,1)S(1)}, bf16[512,256]{1,0:T(8,128)(2,1)S(1)}, u32[]{:S(2)}, u32[]{:S(2)}) collective-permute-start(bf16[512,256]{1,0:T(8,128)(2,1)S(1)} %get-tuple-element.18), channel_id=1, source_target_pairs={{0,4},{4,0},{8,12},{12,8},{16,20},{20,16},{24,28},{28,24},{1,5},{5... | collective-permute-start | bytes 786440 | tf_op jit(solution)/shard_map/ppermute | solution.py:18
  3.0 1.2 %shard_map.113 = (bf16[512,256]{1,0:T(8,128)(2,1)S(1)}, f32[512,256]{1,0:T(8,128)S(1)}) custom-call(s32[1,8]{1,0:T(1,128)} %order_hbm.3, s32[3,1,8]{2,1,0:T(1,128)} %bitcast.7, s32[1,8]{1,0:T(1,128)} %tile_count_hbm.3, bf16[2048,128]{1,0:T(8,128)(2,1)S(1)} %get-tuple-element.14.feats, bf16[8,3,128,128]{3,2,1,0:T(8,128)(2,1)S(1)} %get-tuple-element.15.tiles, ...), custom_call_target="tpu_custom_call" | custom-call | flops 117440512 | bytes 917504 | tf_op jit(solution)/shard_map/pallas_call | solution.py:140
  4.3 2.7 %collective-permute-start.1 = (bf16[128,256]{1,0:T(8,128)(2,1)S(1)}, bf16[128,256]{1,0:T(8,128)(2,1)S(1)}, u32[]{:S(2)}, u32[]{:S(2)}) collective-permute-start(bf16[128,256]{1,0:T(8,128)(2,1)S(1)} %get-tuple-element.31), channel_id=1, source_target_pairs={{0,20},{4,16},{8,28},{12,24},{16,4},{20,0},{24,12},{28,8},{1,21},{... | collective-permute-start | bytes 196616 | tf_op jit(solution)/shard_map/ppermute | solution.py:18
  7.0 1.4 %collective-permute-start.3 = (bf16[128,256]{1,0:T(8,128)(2,1)S(1)}, bf16[128,256]{1,0:T(8,128)(2,1)S(1)}, u32[]{:S(2)}, u32[]{:S(2)}) collective-permute-start(bf16[128,256]{1,0:T(8,128)(2,1)S(1)} %get-tuple-element.32), channel_id=1, source_target_pairs={{0,28},{4,24},{8,20},{12,16},{16,12},{20,8},{24,4},{28,0},{1,29},{... | collective-permute-start | bytes 196616 | tf_op jit(solution)/shard_map/ppermute | solution.py:18
  8.4 2.1 %collective-permute-done.1 = bf16[128,256]{1,0:T(8,128)(2,1)S(1)} collective-permute-done((bf16[128,256]{1,0:T(8,128)(2,1)S(1)}, bf16[128,256]{1,0:T(8,128)(2,1)S(1)}, u32[]{:S(2)}, u32[]{:S(2)}) %collective-permute-start.1) | collective-permute-done | bytes 65568 | tf_op jit(solution)/shard_map/ppermute | solution.py:18
  10.5 1.3 %collective-permute-done.3 = bf16[128,256]{1,0:T(8,128)(2,1)S(1)} collective-permute-done((bf16[128,256]{1,0:T(8,128)(2,1)S(1)}, bf16[128,256]{1,0:T(8,128)(2,1)S(1)}, u32[]{:S(2)}, u32[]{:S(2)}) %collective-permute-start.3) | collective-permute-done | bytes 65568 | tf_op jit(solution)/shard_map/ppermute | solution.py:18
  11.8 0.7 %collective-permute-done.2 = bf16[128,256]{1,0:T(8,128)(2,1)S(1)} collective-permute-done((bf16[128,256]{1,0:T(8,128)(2,1)S(1)}, bf16[128,256]{1,0:T(8,128)(2,1)S(1)}, u32[]{:S(2)}, u32[]{:S(2)}) %collective-permute-start.2) | collective-permute-done | bytes 65568 | tf_op jit(solution)/shard_map/ppermute | solution.py:18
  12.6 2.2 %collective-permute-start.5 = (bf16[128,256]{1,0:T(8,128)(2,1)S(1)}, bf16[128,256]{1,0:T(8,128)(2,1)S(1)}, u32[]{:S(2)}, u32[]{:S(2)}) collective-permute-start(bf16[128,256]{1,0:T(8,128)(2,1)S(1)} %get-tuple-element.22.own), channel_id=1, source_target_pairs={{0,28},{4,24},{8,20},{12,16},{16,12},{20,8},{24,4},{28,0},{1,29},{... | collective-permute-start | bytes 196616 | tf_op jit(solution)/shard_map/ppermute | solution.py:18
  14.7 0.4 %collective-permute-start.4 = (bf16[128,256]{1,0:T(8,128)(2,1)S(1)}, bf16[128,256]{1,0:T(8,128)(2,1)S(1)}, u32[]{:S(2)}, u32[]{:S(2)}) collective-permute-start(bf16[128,256]{1,0:T(8,128)(2,1)S(1)} %get-tuple-element.22.own), channel_id=1, source_target_pairs={{0,20},{4,16},{8,28},{12,24},{16,4},{20,0},{24,12},{28,8},{1,21},{... | collective-permute-start | bytes 196616 | tf_op jit(solution)/shard_map/ppermute | solution.py:18
  15.1 0.4 %collective-permute-start.7 = (bf16[128,256]{1,0:T(8,128)(2,1)S(1)}, bf16[128,256]{1,0:T(8,128)(2,1)S(1)}, u32[]{:S(2)}, u32[]{:S(2)}) collective-permute-start(bf16[128,256]{1,0:T(8,128)(2,1)S(1)} %get-tuple-element.22.own), channel_id=1, source_target_pairs={{0,12},{4,8},{8,4},{12,0},{16,28},{20,24},{24,20},{28,16},{1,13},{... | collective-permute-start | bytes 196616 | tf_op jit(solution)/shard_map/ppermute | solution.py:18
  15.6 0.4 %collective-permute-start.6 = (bf16[128,256]{1,0:T(8,128)(2,1)S(1)}, bf16[128,256]{1,0:T(8,128)(2,1)S(1)}, u32[]{:S(2)}, u32[]{:S(2)}) collective-permute-start(bf16[128,256]{1,0:T(8,128)(2,1)S(1)} %get-tuple-element.22.own), channel_id=1, source_target_pairs={{0,4},{4,0},{8,12},{12,8},{16,20},{20,16},{24,28},{28,24},{1,5},{5... | collective-permute-start | bytes 196616 | tf_op jit(solution)/shard_map/ppermute | solution.py:18
  16.0 1.6 %collective-permute-done.5 = bf16[128,256]{1,0:T(8,128)(2,1)S(1)} collective-permute-done((bf16[128,256]{1,0:T(8,128)(2,1)S(1)}, bf16[128,256]{1,0:T(8,128)(2,1)S(1)}, u32[]{:S(2)}, u32[]{:S(2)}) %collective-permute-start.5) | collective-permute-done | bytes 65568 | tf_op jit(solution)/shard_map/ppermute | solution.py:18
  17.6 1.5 %collective-permute-done.4 = bf16[128,256]{1,0:T(8,128)(2,1)S(1)} collective-permute-done((bf16[128,256]{1,0:T(8,128)(2,1)S(1)}, bf16[128,256]{1,0:T(8,128)(2,1)S(1)}, u32[]{:S(2)}, u32[]{:S(2)}) %collective-permute-start.4) | collective-permute-done | bytes 65568 | tf_op jit(solution)/shard_map/ppermute | solution.py:18
  19.4 0.3 collective-permute-start.8
  19.7 0.3 shard_map.114.total
  20.0 0.6 %collective-permute-done.8.others_late = bf16[128,256]{1,0:T(8,128)(2,1)S(1)} collective-permute-done((bf16[128,256]{1,0:T(8,128)(2,1)S(1)}, bf16[128,256]{1,0:T(8,128)(2,1)S(1)}, u32[]{:S(2)}, u32[]{:S(2)}) %collective-permute-start.8) | collective-permute-done | bytes 65568 | tf_op jit(solution)/shard_map/ppermute | solution.py:18
  20.6 0.3 shard_map.115
  20.9 2.6 %collective-permute-start.10 = (bf16[256,256]{1,0:T(8,128)(2,1)S(1)}, bf16[256,256]{1,0:T(8,128)(2,1)S(1)}, u32[]{:S(2)}, u32[]{:S(2)}) collective-permute-start(bf16[256,256]{1,0:T(8,128)(2,1)S(1)} %shard_map.115), channel_id=1, source_target_pairs={{0,2},{1,3},{2,0},{3,1},{4,5},{5,4},{6,7},{7,6},{8,10},{9,11},{10,... | collective-permute-start | bytes 393224 | tf_op jit(solution)/shard_map/ppermute | solution.py:195
  23.6 3.7 %collective-permute-done.10 = bf16[256,256]{1,0:T(8,128)(2,1)S(1)} collective-permute-done((bf16[256,256]{1,0:T(8,128)(2,1)S(1)}, bf16[256,256]{1,0:T(8,128)(2,1)S(1)}, u32[]{:S(2)}, u32[]{:S(2)}) %collective-permute-start.10) | collective-permute-done | bytes 131104 | tf_op jit(solution)/shard_map/ppermute | solution.py:195
  27.3 2.0 %collective-permute-start.11 = (bf16[256,256]{1,0:T(8,128)(2,1)S(1)}, bf16[256,256]{1,0:T(8,128)(2,1)S(1)}, u32[]{:S(2)}, u32[]{:S(2)}) collective-permute-start(bf16[256,256]{1,0:T(8,128)(2,1)S(1)} %add_convert_fusion), channel_id=1, source_target_pairs={{0,1},{1,0},{2,3},{3,2},{4,7},{5,6},{6,5},{7,4},{8,9},{9,8},{10,11... | collective-permute-start | bytes 393224 | tf_op jit(solution)/shard_map/ppermute | solution.py:195
  29.3 0.7 %fusion.5 = bf16[1,128,256]{2,1,0:T(8,128)(2,1)} fusion(f32[128,256]{1,0:T(8,128)S(1)} %get-tuple-element.19), kind=kLoop, calls=%fused_computation.12 | loop fusion | flops 163840 | bytes 196608 | tf_op jit(solution)/shard_map/broadcast_in_dim | solution.py:197
  30.0 2.6 %collective-permute-done.11 = bf16[256,256]{1,0:T(8,128)(2,1)S(1)} collective-permute-done((bf16[256,256]{1,0:T(8,128)(2,1)S(1)}, bf16[256,256]{1,0:T(8,128)(2,1)S(1)}, u32[]{:S(2)}, u32[]{:S(2)}) %collective-permute-start.11) | collective-permute-done | bytes 131104 | tf_op jit(solution)/shard_map/ppermute | solution.py:195
  32.6 0.7 %fusion.8 = (f32[128,256]{1,0:T(8,128)}, f32[128,256]{1,0:T(8,128)}) fusion(f32[256,256]{1,0:T(8,128)S(1)} %convert_add_fusion.1), kind=kLoop, calls=%fused_computation.14 | loop fusion | bytes 524288 | tf_op jit(solution)/shard_map/slice | solution.py:197
  (16 shorter events, 0.6 us)
Async XLA Ops:
  2.4 1.7 %collective-permute-start = (bf16[512,256]{1,0:T(8,128)(2,1)S(1)}, bf16[512,256]{1,0:T(8,128)(2,1)S(1)}, u32[]{:S(2)}, u32[]{:S(2)}) collective-permute-start(bf16[512,256]{1,0:T(8,128)(2,1)S(1)} %get-tuple-element.18), channel_id=1, source_target_pairs={{0,4},{4,0},{8,12},{12,8},{16,20},{20,16},{24,28},{28,24},{1,5},{5... | collective-permute-start | bytes 786440 | tf_op jit(solution)/shard_map/ppermute | solution.py:18
  4.2 8.2 %copy-start = (bf16[1,128,256]{2,1,0:T(8,128)(2,1)S(1)}, bf16[1,128,256]{2,1,0:T(8,128)(2,1)}, u32[]{:S(2)}) copy-start(bf16[1,128,256]{2,1,0:T(8,128)(2,1)} %param.17) | copy-start | bytes 196612
  4.3 6.3 %collective-permute-start.1 = (bf16[128,256]{1,0:T(8,128)(2,1)S(1)}, bf16[128,256]{1,0:T(8,128)(2,1)S(1)}, u32[]{:S(2)}, u32[]{:S(2)}) collective-permute-start(bf16[128,256]{1,0:T(8,128)(2,1)S(1)} %get-tuple-element.31), channel_id=1, source_target_pairs={{0,20},{4,16},{8,28},{12,24},{16,4},{20,0},{24,12},{28,8},{1,21},{... | collective-permute-start | bytes 196616 | tf_op jit(solution)/shard_map/ppermute | solution.py:18
  7.0 4.9 %collective-permute-start.3 = (bf16[128,256]{1,0:T(8,128)(2,1)S(1)}, bf16[128,256]{1,0:T(8,128)(2,1)S(1)}, u32[]{:S(2)}, u32[]{:S(2)}) collective-permute-start(bf16[128,256]{1,0:T(8,128)(2,1)S(1)} %get-tuple-element.32), channel_id=1, source_target_pairs={{0,28},{4,24},{8,20},{12,16},{16,12},{20,8},{24,4},{28,0},{1,29},{... | collective-permute-start | bytes 196616 | tf_op jit(solution)/shard_map/ppermute | solution.py:18
  8.3 4.1 %copy-start.1 = (f32[256]{0:T(256)S(1)}, f32[256]{0:T(256)}, u32[]{:S(2)}) copy-start(f32[256]{0:T(256)} %param.12) | copy-start | bytes 3076
  8.3 4.1 %collective-permute-start.2 = (bf16[128,256]{1,0:T(8,128)(2,1)S(1)}, bf16[128,256]{1,0:T(8,128)(2,1)S(1)}, u32[]{:S(2)}, u32[]{:S(2)}) collective-permute-start(bf16[128,256]{1,0:T(8,128)(2,1)S(1)} %get-tuple-element.33), channel_id=1, source_target_pairs={{0,12},{4,8},{8,4},{12,0},{16,28},{20,24},{24,20},{28,16},{1,13},{... | collective-permute-start | bytes 196616 | tf_op jit(solution)/shard_map/ppermute | solution.py:18
  12.6 5.1 %collective-permute-start.5 = (bf16[128,256]{1,0:T(8,128)(2,1)S(1)}, bf16[128,256]{1,0:T(8,128)(2,1)S(1)}, u32[]{:S(2)}, u32[]{:S(2)}) collective-permute-start(bf16[128,256]{1,0:T(8,128)(2,1)S(1)} %get-tuple-element.22.own), channel_id=1, source_target_pairs={{0,28},{4,24},{8,20},{12,16},{16,12},{20,8},{24,4},{28,0},{1,29},{... | collective-permute-start | bytes 196616 | tf_op jit(solution)/shard_map/ppermute | solution.py:18
  14.7 4.4 %collective-permute-start.4 = (bf16[128,256]{1,0:T(8,128)(2,1)S(1)}, bf16[128,256]{1,0:T(8,128)(2,1)S(1)}, u32[]{:S(2)}, u32[]{:S(2)}) collective-permute-start(bf16[128,256]{1,0:T(8,128)(2,1)S(1)} %get-tuple-element.22.own), channel_id=1, source_target_pairs={{0,20},{4,16},{8,28},{12,24},{16,4},{20,0},{24,12},{28,8},{1,21},{... | collective-permute-start | bytes 196616 | tf_op jit(solution)/shard_map/ppermute | solution.py:18
  15.1 4.2 %collective-permute-start.7 = (bf16[128,256]{1,0:T(8,128)(2,1)S(1)}, bf16[128,256]{1,0:T(8,128)(2,1)S(1)}, u32[]{:S(2)}, u32[]{:S(2)}) collective-permute-start(bf16[128,256]{1,0:T(8,128)(2,1)S(1)} %get-tuple-element.22.own), channel_id=1, source_target_pairs={{0,12},{4,8},{8,4},{12,0},{16,28},{20,24},{24,20},{28,16},{1,13},{... | collective-permute-start | bytes 196616 | tf_op jit(solution)/shard_map/ppermute | solution.py:18
  15.6 3.6 %collective-permute-start.6 = (bf16[128,256]{1,0:T(8,128)(2,1)S(1)}, bf16[128,256]{1,0:T(8,128)(2,1)S(1)}, u32[]{:S(2)}, u32[]{:S(2)}) collective-permute-start(bf16[128,256]{1,0:T(8,128)(2,1)S(1)} %get-tuple-element.22.own), channel_id=1, source_target_pairs={{0,4},{4,0},{8,12},{12,8},{16,20},{20,16},{24,28},{28,24},{1,5},{5... | collective-permute-start | bytes 196616 | tf_op jit(solution)/shard_map/ppermute | solution.py:18
  19.1 1.5 %collective-permute-start.9 = (bf16[256,256]{1,0:T(8,128)(2,1)S(1)}, bf16[256,256]{1,0:T(8,128)(2,1)S(1)}, u32[]{:S(2)}, u32[]{:S(2)}) collective-permute-start(bf16[256,256]{1,0:T(8,128)(2,1)S(1)} %pad_maximum_fusion.early), channel_id=1, source_target_pairs={{0,4},{4,0},{8,12},{12,8},{16,20},{20,16},{24,28},{28,24},{1,5},{5... | collective-permute-start | bytes 393224 | tf_op jit(solution)/shard_map/ppermute | solution.py:18
  19.4 1.3 %collective-permute-start.8 = (bf16[128,256]{1,0:T(8,128)(2,1)S(1)}, bf16[128,256]{1,0:T(8,128)(2,1)S(1)}, u32[]{:S(2)}, u32[]{:S(2)}) collective-permute-start(bf16[128,256]{1,0:T(8,128)(2,1)S(1)} %collective-permute-done.7.late), channel_id=1, source_target_pairs={{0,4},{4,0},{8,12},{12,8},{16,20},{20,16},{24,28},{28,24},{1,5},{5... | collective-permute-start | bytes 196616 | tf_op jit(solution)/shard_map/ppermute | solution.py:18
  20.9 6.4 %collective-permute-start.10 = (bf16[256,256]{1,0:T(8,128)(2,1)S(1)}, bf16[256,256]{1,0:T(8,128)(2,1)S(1)}, u32[]{:S(2)}, u32[]{:S(2)}) collective-permute-start(bf16[256,256]{1,0:T(8,128)(2,1)S(1)} %shard_map.115), channel_id=1, source_target_pairs={{0,2},{1,3},{2,0},{3,1},{4,5},{5,4},{6,7},{7,6},{8,10},{9,11},{10,... | collective-permute-start | bytes 393224 | tf_op jit(solution)/shard_map/ppermute | solution.py:195
  27.3 5.2 %collective-permute-start.11 = (bf16[256,256]{1,0:T(8,128)(2,1)S(1)}, bf16[256,256]{1,0:T(8,128)(2,1)S(1)}, u32[]{:S(2)}, u32[]{:S(2)}) collective-permute-start(bf16[256,256]{1,0:T(8,128)(2,1)S(1)} %add_convert_fusion), channel_id=1, source_target_pairs={{0,1},{1,0},{2,3},{3,2},{4,7},{5,6},{6,5},{7,4},{8,9},{9,8},{10,11... | collective-permute-start | bytes 393224 | tf_op jit(solution)/shard_map/ppermute | solution.py:195

commit v7 on v6

--- a/solution.py
+++ b/solution.py
@@ -101,7 +101,8 @@
     def swap_cores(value):
         return exchange(value, "feat", n_feat, 1)
 
-    kept_flips = (0,) + tuple(2 * j + 1 for j in range(1, n_chip))
+    chips = [0, 1] + list(range(n_chip - 1, 1, -1))
+    kept_flips = (0,) + tuple(2 * chip + 1 for chip in chips[1:])
     given_flips = tuple(flip ^ 1 for flip in kept_flips)
     tiles_of_slot = jnp.transpose(tile_src, (2, 0, 1))
 
@@ -150,8 +151,8 @@
     from_core = swap_cores(given)
     chip_sums = kept + from_core.astype(jnp.float32)
     arrived = [
-        exchange(chip_sums[j * block_rows : (j + 1) * block_rows].astype(jnp.bfloat16), "feat", n_feat, 2 * j + 1)
-        for j in sorted(range(1, n_chip), key=lambda j: (j.bit_count(), -j))
+        exchange(chip_sums[j * block_rows : (j + 1) * block_rows].astype(jnp.bfloat16), "feat", n_feat, kept_flips[j])
+        for j in sorted(range(1, n_chip), key=lambda j: (chips[j].bit_count(), -chips[j]))
     ]
     preact = chip_sums[:block_rows] + bias
     for got in arrived:
@@ -163,7 +164,7 @@
     preact, output_grad = lax.optimization_barrier((preact, output_grad))
     hidden = jax.nn.silu(preact).astype(jnp.bfloat16)
 
-    received = [exchange(output_grad, "feat", n_feat, 2 * j + 1) for j in range(1, n_chip)]
+    received = [exchange(output_grad, "feat", n_feat, kept_flips[j]) for j in range(1, n_chip)]
     partner = swap_cores(output_grad)
     early = jnp.concatenate(received[1:], axis=0)
     early, partner = lax.optimization_barrier((early, partner))

time: 33.5 us -> 33.3 us (level)
  transfers between devices with their start and end apart: 12 -> 12, of which waited for: 8 -> 9; matrix products, arithmetic and copies ran while one was open for 2% -> 2% of each run, Pallas kernels for 4% -> 4%
where the time goes in v7:
time: 33.3 us; the launch traced here: 33.1 us
  waiting for transfers between devices  13.9 us (42%)
  starting transfers between devices  13.3 us (40%)
  Pallas kernels  3.55 us (11%)
  other arithmetic  0.9 us (3%)
  local copies, waits for them, and re-layouts  0.74 us (2%)
  between operations  0.73 us (2%)
    ppermute x10, starting transfers between devices, exchange(): return lax.ppermute(value, axis, [(i, i ^ flip) for i in range(size)])  8.86 us
    ppermute x10, waiting for transfers between devices, exchange(): return lax.ppermute(value, axis, [(i, i ^ flip) for i in range(size)])  7.57 us
    ppermute x2, waiting for transfers between devices, body(): got = lax.ppermute(sent, ('feat', 'rep'), pairs)  6.28 us
    ppermute x2, starting transfers between devices, body(): got = lax.ppermute(sent, ('feat', 'rep'), pairs)  4.48 us
    pallas_call x1, Pallas kernels, body(): pl.pallas_call(functools.partial(load_and_project, given_flips), out_shap...  1.79 us
    pallas_call x1, Pallas kernels, body(): pl.pallas_call(functools.partial(project_loaded, kept_flips), out_shape=r...  1.18 us
    slice x1, local copies, waits for them, and re-layouts, body(): return (hidden[None], grads[:columns], grads[columns:])  0.72 us
    broadcast_in_dim x1, other arithmetic, body(): return (hidden[None], grads[:columns], grads[columns:])  0.67 us
  transfers between devices with their start and end apart: 12, of which 9 were waited for; matrix products, arithmetic and copies ran while one was open for 2% of the time, Pallas kernels for 4%

profile of v7, /device:TPU:0, one launch (start us, length us, event | category | flops | bytes accessed | tf_op | source)
XLA Modules:
  0.0 33.1 jit_solution(6251505355036691232)
XLA Ops:
  0.6 1.8 %shard_map.112 = (bf16[512,256]{1,0:T(8,128)(2,1)S(1)}, bf16[512,256]{1,0:T(8,128)(2,1)S(1)}, bf16[2048,128]{1,0:T(8,128)(2,1)S(1)}, bf16[8,3,128,128]{3,2,1,0:T(8,128)(2,1)S(1)}, bf16[256,256]{1,0:T(8,128)(2,1)S(1)}) custom-call(s32[1,8]{1,0:T(1,128)} %order_hbm.3, s32[3,1,8]{2,1,0:T(1,128)} %bitcast.6, s32[1,8]{1,0:T(1,128)} %tile_count_hbm.3, ...), custom_call_target="tpu_custom_call" | custom-call | flops 117440512 | bytes 917504 | tf_op jit(solution)/shard_map/pallas_call | solution.py:127
  2.4 0.5 %collective-permute-start = (bf16[512,256]{1,0:T(8,128)(2,1)S(1)}, bf16[512,256]{1,0:T(8,128)(2,1)S(1)}, u32[]{:S(2)}, u32[]{:S(2)}) collective-permute-start(bf16[512,256]{1,0:T(8,128)(2,1)S(1)} %get-tuple-element.18), channel_id=1, source_target_pairs={{0,4},{4,0},{8,12},{12,8},{16,20},{20,16},{24,28},{28,24},{1,5},{5... | collective-permute-start | bytes 786440 | tf_op jit(solution)/shard_map/ppermute | solution.py:18
  3.0 1.2 %shard_map.113 = (bf16[512,256]{1,0:T(8,128)(2,1)S(1)}, f32[512,256]{1,0:T(8,128)S(1)}) custom-call(s32[1,8]{1,0:T(1,128)} %order_hbm.3, s32[3,1,8]{2,1,0:T(1,128)} %bitcast.7, s32[1,8]{1,0:T(1,128)} %tile_count_hbm.3, bf16[2048,128]{1,0:T(8,128)(2,1)S(1)} %get-tuple-element.14.feats, bf16[8,3,128,128]{3,2,1,0:T(8,128)(2,1)S(1)} %get-tuple-element.15.tiles, ...), custom_call_target="tpu_custom_call" | custom-call | flops 117440512 | bytes 917504 | tf_op jit(solution)/shard_map/pallas_call | solution.py:141
  4.3 2.7 %collective-permute-start.1 = (bf16[128,256]{1,0:T(8,128)(2,1)S(1)}, bf16[128,256]{1,0:T(8,128)(2,1)S(1)}, u32[]{:S(2)}, u32[]{:S(2)}) collective-permute-start(bf16[128,256]{1,0:T(8,128)(2,1)S(1)} %get-tuple-element.31), channel_id=1, source_target_pairs={{0,20},{4,16},{8,28},{12,24},{16,4},{20,0},{24,12},{28,8},{1,21},{... | collective-permute-start | bytes 196616 | tf_op jit(solution)/shard_map/ppermute | solution.py:18
  7.0 1.4 %collective-permute-start.3 = (bf16[128,256]{1,0:T(8,128)(2,1)S(1)}, bf16[128,256]{1,0:T(8,128)(2,1)S(1)}, u32[]{:S(2)}, u32[]{:S(2)}) collective-permute-start(bf16[128,256]{1,0:T(8,128)(2,1)S(1)} %get-tuple-element.32), channel_id=1, source_target_pairs={{0,28},{4,24},{8,20},{12,16},{16,12},{20,8},{24,4},{28,0},{1,29},{... | collective-permute-start | bytes 196616 | tf_op jit(solution)/shard_map/ppermute | solution.py:18
  8.4 2.1 %collective-permute-done.1 = bf16[128,256]{1,0:T(8,128)(2,1)S(1)} collective-permute-done((bf16[128,256]{1,0:T(8,128)(2,1)S(1)}, bf16[128,256]{1,0:T(8,128)(2,1)S(1)}, u32[]{:S(2)}, u32[]{:S(2)}) %collective-permute-start.1) | collective-permute-done | bytes 65568 | tf_op jit(solution)/shard_map/ppermute | solution.py:18
  10.5 1.3 %collective-permute-done.3 = bf16[128,256]{1,0:T(8,128)(2,1)S(1)} collective-permute-done((bf16[128,256]{1,0:T(8,128)(2,1)S(1)}, bf16[128,256]{1,0:T(8,128)(2,1)S(1)}, u32[]{:S(2)}, u32[]{:S(2)}) %collective-permute-start.3) | collective-permute-done | bytes 65568 | tf_op jit(solution)/shard_map/ppermute | solution.py:18
  11.8 0.7 %collective-permute-done.2 = bf16[128,256]{1,0:T(8,128)(2,1)S(1)} collective-permute-done((bf16[128,256]{1,0:T(8,128)(2,1)S(1)}, bf16[128,256]{1,0:T(8,128)(2,1)S(1)}, u32[]{:S(2)}, u32[]{:S(2)}) %collective-permute-start.2) | collective-permute-done | bytes 65568 | tf_op jit(solution)/shard_map/ppermute | solution.py:18
  12.6 1.3 %collective-permute-start.5 = (bf16[128,256]{1,0:T(8,128)(2,1)S(1)}, bf16[128,256]{1,0:T(8,128)(2,1)S(1)}, u32[]{:S(2)}, u32[]{:S(2)}) collective-permute-start(bf16[128,256]{1,0:T(8,128)(2,1)S(1)} %get-tuple-element.22.own), channel_id=1, source_target_pairs={{0,20},{4,16},{8,28},{12,24},{16,4},{20,0},{24,12},{28,8},{1,21},{... | collective-permute-start | bytes 196616 | tf_op jit(solution)/shard_map/ppermute | solution.py:18
  13.9 1.3 %collective-permute-start.4 = (bf16[128,256]{1,0:T(8,128)(2,1)S(1)}, bf16[128,256]{1,0:T(8,128)(2,1)S(1)}, u32[]{:S(2)}, u32[]{:S(2)}) collective-permute-start(bf16[128,256]{1,0:T(8,128)(2,1)S(1)} %get-tuple-element.22.own), channel_id=1, source_target_pairs={{0,28},{4,24},{8,20},{12,16},{16,12},{20,8},{24,4},{28,0},{1,29},{... | collective-permute-start | bytes 196616 | tf_op jit(solution)/shard_map/ppermute | solution.py:18
  15.1 0.4 %collective-permute-start.7 = (bf16[128,256]{1,0:T(8,128)(2,1)S(1)}, bf16[128,256]{1,0:T(8,128)(2,1)S(1)}, u32[]{:S(2)}, u32[]{:S(2)}) collective-permute-start(bf16[128,256]{1,0:T(8,128)(2,1)S(1)} %get-tuple-element.22.own), channel_id=1, source_target_pairs={{0,12},{4,8},{8,4},{12,0},{16,28},{20,24},{24,20},{28,16},{1,13},{... | collective-permute-start | bytes 196616 | tf_op jit(solution)/shard_map/ppermute | solution.py:18
  15.6 0.4 %collective-permute-start.6 = (bf16[128,256]{1,0:T(8,128)(2,1)S(1)}, bf16[128,256]{1,0:T(8,128)(2,1)S(1)}, u32[]{:S(2)}, u32[]{:S(2)}) collective-permute-start(bf16[128,256]{1,0:T(8,128)(2,1)S(1)} %get-tuple-element.22.own), channel_id=1, source_target_pairs={{0,4},{4,0},{8,12},{12,8},{16,20},{20,16},{24,28},{28,24},{1,5},{5... | collective-permute-start | bytes 196616 | tf_op jit(solution)/shard_map/ppermute | solution.py:18
  16.0 0.7 %collective-permute-done.5 = bf16[128,256]{1,0:T(8,128)(2,1)S(1)} collective-permute-done((bf16[128,256]{1,0:T(8,128)(2,1)S(1)}, bf16[128,256]{1,0:T(8,128)(2,1)S(1)}, u32[]{:S(2)}, u32[]{:S(2)}) %collective-permute-start.5) | collective-permute-done | bytes 65568 | tf_op jit(solution)/shard_map/ppermute | solution.py:18
  16.7 1.9 %collective-permute-done.4 = bf16[128,256]{1,0:T(8,128)(2,1)S(1)} collective-permute-done((bf16[128,256]{1,0:T(8,128)(2,1)S(1)}, bf16[128,256]{1,0:T(8,128)(2,1)S(1)}, u32[]{:S(2)}, u32[]{:S(2)}) %collective-permute-start.4) | collective-permute-done | bytes 65568 | tf_op jit(solution)/shard_map/ppermute | solution.py:18
  18.6 0.6 %collective-permute-start.9 = (bf16[256,256]{1,0:T(8,128)(2,1)S(1)}, bf16[256,256]{1,0:T(8,128)(2,1)S(1)}, u32[]{:S(2)}, u32[]{:S(2)}) collective-permute-start(bf16[256,256]{1,0:T(8,128)(2,1)S(1)} %pad_maximum_fusion.early), channel_id=1, source_target_pairs={{0,4},{4,0},{8,12},{12,8},{16,20},{20,16},{24,28},{28,24},{1,5},{5... | collective-permute-start | bytes 393224 | tf_op jit(solution)/shard_map/ppermute | solution.py:18
  19.5 0.3 shard_map.114.total
  19.8 0.8 %collective-permute-done.8.others_late = bf16[128,256]{1,0:T(8,128)(2,1)S(1)} collective-permute-done((bf16[128,256]{1,0:T(8,128)(2,1)S(1)}, bf16[128,256]{1,0:T(8,128)(2,1)S(1)}, u32[]{:S(2)}, u32[]{:S(2)}) %collective-permute-start.8) | collective-permute-done | bytes 65568 | tf_op jit(solution)/shard_map/ppermute | solution.py:18
  20.6 0.3 shard_map.115
  20.9 2.6 %collective-permute-start.10 = (bf16[256,256]{1,0:T(8,128)(2,1)S(1)}, bf16[256,256]{1,0:T(8,128)(2,1)S(1)}, u32[]{:S(2)}, u32[]{:S(2)}) collective-permute-start(bf16[256,256]{1,0:T(8,128)(2,1)S(1)} %shard_map.115), channel_id=1, source_target_pairs={{0,2},{1,3},{2,0},{3,1},{4,5},{5,4},{6,7},{7,6},{8,10},{9,11},{10,... | collective-permute-start | bytes 393224 | tf_op jit(solution)/shard_map/ppermute | solution.py:196
  23.5 3.8 %collective-permute-done.10 = bf16[256,256]{1,0:T(8,128)(2,1)S(1)} collective-permute-done((bf16[256,256]{1,0:T(8,128)(2,1)S(1)}, bf16[256,256]{1,0:T(8,128)(2,1)S(1)}, u32[]{:S(2)}, u32[]{:S(2)}) %collective-permute-start.10) | collective-permute-done | bytes 131104 | tf_op jit(solution)/shard_map/ppermute | solution.py:196
  27.3 1.9 %collective-permute-start.11 = (bf16[256,256]{1,0:T(8,128)(2,1)S(1)}, bf16[256,256]{1,0:T(8,128)(2,1)S(1)}, u32[]{:S(2)}, u32[]{:S(2)}) collective-permute-start(bf16[256,256]{1,0:T(8,128)(2,1)S(1)} %add_convert_fusion), channel_id=1, source_target_pairs={{0,1},{1,0},{2,3},{3,2},{4,7},{5,6},{6,5},{7,4},{8,9},{9,8},{10,11... | collective-permute-start | bytes 393224 | tf_op jit(solution)/shard_map/ppermute | solution.py:196
  29.2 0.7 %fusion.5 = bf16[1,128,256]{2,1,0:T(8,128)(2,1)} fusion(f32[128,256]{1,0:T(8,128)S(1)} %get-tuple-element.19), kind=kLoop, calls=%fused_computation.12 | loop fusion | flops 163840 | bytes 196608 | tf_op jit(solution)/shard_map/broadcast_in_dim | solution.py:198
  29.9 2.5 %collective-permute-done.11 = bf16[256,256]{1,0:T(8,128)(2,1)S(1)} collective-permute-done((bf16[256,256]{1,0:T(8,128)(2,1)S(1)}, bf16[256,256]{1,0:T(8,128)(2,1)S(1)}, u32[]{:S(2)}, u32[]{:S(2)}) %collective-permute-start.11) | collective-permute-done | bytes 131104 | tf_op jit(solution)/shard_map/ppermute | solution.py:196
  32.4 0.7 %fusion.8 = (f32[128,256]{1,0:T(8,128)}, f32[128,256]{1,0:T(8,128)}) fusion(f32[256,256]{1,0:T(8,128)S(1)} %convert_add_fusion.1), kind=kLoop, calls=%fused_computation.14 | loop fusion | bytes 524288 | tf_op jit(solution)/shard_map/slice | solution.py:198
  (16 shorter events, 0.6 us)
Async XLA Ops:
  2.4 1.7 %collective-permute-start = (bf16[512,256]{1,0:T(8,128)(2,1)S(1)}, bf16[512,256]{1,0:T(8,128)(2,1)S(1)}, u32[]{:S(2)}, u32[]{:S(2)}) collective-permute-start(bf16[512,256]{1,0:T(8,128)(2,1)S(1)} %get-tuple-element.18), channel_id=1, source_target_pairs={{0,4},{4,0},{8,12},{12,8},{16,20},{20,16},{24,28},{28,24},{1,5},{5... | collective-permute-start | bytes 786440 | tf_op jit(solution)/shard_map/ppermute | solution.py:18
  4.2 8.2 %copy-start = (bf16[1,128,256]{2,1,0:T(8,128)(2,1)S(1)}, bf16[1,128,256]{2,1,0:T(8,128)(2,1)}, u32[]{:S(2)}) copy-start(bf16[1,128,256]{2,1,0:T(8,128)(2,1)} %param.17) | copy-start | bytes 196612
  4.3 6.3 %collective-permute-start.1 = (bf16[128,256]{1,0:T(8,128)(2,1)S(1)}, bf16[128,256]{1,0:T(8,128)(2,1)S(1)}, u32[]{:S(2)}, u32[]{:S(2)}) collective-permute-start(bf16[128,256]{1,0:T(8,128)(2,1)S(1)} %get-tuple-element.31), channel_id=1, source_target_pairs={{0,20},{4,16},{8,28},{12,24},{16,4},{20,0},{24,12},{28,8},{1,21},{... | collective-permute-start | bytes 196616 | tf_op jit(solution)/shard_map/ppermute | solution.py:18
  7.0 4.9 %collective-permute-start.3 = (bf16[128,256]{1,0:T(8,128)(2,1)S(1)}, bf16[128,256]{1,0:T(8,128)(2,1)S(1)}, u32[]{:S(2)}, u32[]{:S(2)}) collective-permute-start(bf16[128,256]{1,0:T(8,128)(2,1)S(1)} %get-tuple-element.32), channel_id=1, source_target_pairs={{0,28},{4,24},{8,20},{12,16},{16,12},{20,8},{24,4},{28,0},{1,29},{... | collective-permute-start | bytes 196616 | tf_op jit(solution)/shard_map/ppermute | solution.py:18
  8.3 4.1 %copy-start.1 = (f32[256]{0:T(256)S(1)}, f32[256]{0:T(256)}, u32[]{:S(2)}) copy-start(f32[256]{0:T(256)} %param.12) | copy-start | bytes 3076
  8.3 4.1 %collective-permute-start.2 = (bf16[128,256]{1,0:T(8,128)(2,1)S(1)}, bf16[128,256]{1,0:T(8,128)(2,1)S(1)}, u32[]{:S(2)}, u32[]{:S(2)}) collective-permute-start(bf16[128,256]{1,0:T(8,128)(2,1)S(1)} %get-tuple-element.33), channel_id=1, source_target_pairs={{0,12},{4,8},{8,4},{12,0},{16,28},{20,24},{24,20},{28,16},{1,13},{... | collective-permute-start | bytes 196616 | tf_op jit(solution)/shard_map/ppermute | solution.py:18
  12.6 4.2 %collective-permute-start.5 = (bf16[128,256]{1,0:T(8,128)(2,1)S(1)}, bf16[128,256]{1,0:T(8,128)(2,1)S(1)}, u32[]{:S(2)}, u32[]{:S(2)}) collective-permute-start(bf16[128,256]{1,0:T(8,128)(2,1)S(1)} %get-tuple-element.22.own), channel_id=1, source_target_pairs={{0,20},{4,16},{8,28},{12,24},{16,4},{20,0},{24,12},{28,8},{1,21},{... | collective-permute-start | bytes 196616 | tf_op jit(solution)/shard_map/ppermute | solution.py:18
  13.9 4.7 %collective-permute-start.4 = (bf16[128,256]{1,0:T(8,128)(2,1)S(1)}, bf16[128,256]{1,0:T(8,128)(2,1)S(1)}, u32[]{:S(2)}, u32[]{:S(2)}) collective-permute-start(bf16[128,256]{1,0:T(8,128)(2,1)S(1)} %get-tuple-element.22.own), channel_id=1, source_target_pairs={{0,28},{4,24},{8,20},{12,16},{16,12},{20,8},{24,4},{28,0},{1,29},{... | collective-permute-start | bytes 196616 | tf_op jit(solution)/shard_map/ppermute | solution.py:18
  15.1 4.2 %collective-permute-start.7 = (bf16[128,256]{1,0:T(8,128)(2,1)S(1)}, bf16[128,256]{1,0:T(8,128)(2,1)S(1)}, u32[]{:S(2)}, u32[]{:S(2)}) collective-permute-start(bf16[128,256]{1,0:T(8,128)(2,1)S(1)} %get-tuple-element.22.own), channel_id=1, source_target_pairs={{0,12},{4,8},{8,4},{12,0},{16,28},{20,24},{24,20},{28,16},{1,13},{... | collective-permute-start | bytes 196616 | tf_op jit(solution)/shard_map/ppermute | solution.py:18
  15.6 3.1 %collective-permute-start.6 = (bf16[128,256]{1,0:T(8,128)(2,1)S(1)}, bf16[128,256]{1,0:T(8,128)(2,1)S(1)}, u32[]{:S(2)}, u32[]{:S(2)}) collective-permute-start(bf16[128,256]{1,0:T(8,128)(2,1)S(1)} %get-tuple-element.22.own), channel_id=1, source_target_pairs={{0,4},{4,0},{8,12},{12,8},{16,20},{20,16},{24,28},{28,24},{1,5},{5... | collective-permute-start | bytes 196616 | tf_op jit(solution)/shard_map/ppermute | solution.py:18
  18.6 2.0 %collective-permute-start.9 = (bf16[256,256]{1,0:T(8,128)(2,1)S(1)}, bf16[256,256]{1,0:T(8,128)(2,1)S(1)}, u32[]{:S(2)}, u32[]{:S(2)}) collective-permute-start(bf16[256,256]{1,0:T(8,128)(2,1)S(1)} %pad_maximum_fusion.early), channel_id=1, source_target_pairs={{0,4},{4,0},{8,12},{12,8},{16,20},{20,16},{24,28},{28,24},{1,5},{5... | collective-permute-start | bytes 393224 | tf_op jit(solution)/shard_map/ppermute | solution.py:18
  19.3 1.3 %collective-permute-start.8 = (bf16[128,256]{1,0:T(8,128)(2,1)S(1)}, bf16[128,256]{1,0:T(8,128)(2,1)S(1)}, u32[]{:S(2)}, u32[]{:S(2)}) collective-permute-start(bf16[128,256]{1,0:T(8,128)(2,1)S(1)} %collective-permute-done.7.late), channel_id=1, source_target_pairs={{0,4},{4,0},{8,12},{12,8},{16,20},{20,16},{24,28},{28,24},{1,5},{5... | collective-permute-start | bytes 196616 | tf_op jit(solution)/shard_map/ppermute | solution.py:18
  20.9 6.4 %collective-permute-start.10 = (bf16[256,256]{1,0:T(8,128)(2,1)S(1)}, bf16[256,256]{1,0:T(8,128)(2,1)S(1)}, u32[]{:S(2)}, u32[]{:S(2)}) collective-permute-start(bf16[256,256]{1,0:T(8,128)(2,1)S(1)} %shard_map.115), channel_id=1, source_target_pairs={{0,2},{1,3},{2,0},{3,1},{4,5},{5,4},{6,7},{7,6},{8,10},{9,11},{10,... | collective-permute-start | bytes 393224 | tf_op jit(solution)/shard_map/ppermute | solution.py:196
  27.3 5.0 %collective-permute-start.11 = (bf16[256,256]{1,0:T(8,128)(2,1)S(1)}, bf16[256,256]{1,0:T(8,128)(2,1)S(1)}, u32[]{:S(2)}, u32[]{:S(2)}) collective-permute-start(bf16[256,256]{1,0:T(8,128)(2,1)S(1)} %add_convert_fusion), channel_id=1, source_target_pairs={{0,1},{1,0},{2,3},{3,2},{4,7},{5,6},{6,5},{7,4},{8,9},{9,8},{10,11... | collective-permute-start | bytes 393224 | tf_op jit(solution)/shard_map/ppermute | solution.py:196

commit v8 on v7

--- a/solution.py
+++ b/solution.py
@@ -18,15 +18,19 @@
     return lax.ppermute(value, axis, [(i, i ^ flip) for i in range(size)])
 
 
-def copy_all(pairs, sems):
+def start_all(pairs, sems):
     copies = [pltpu.make_async_copy(source, target, sems.at[i]) for i, (source, target) in enumerate(pairs)]
     for copy in copies:
         copy.start()
-    for copy in copies:
+    return copies
+
+
+def copy_all(pairs, sems):
+    for copy in start_all(pairs, sems):
         copy.wait()
 
 
-def project_blocks(flips, order, tile_src, tile_count, feats, tiles, weights, rows_out, sums_out):
+def project_blocks(flips, order, tile_src, tile_count, feats, tiles, weights, rows_out, sums_out, tiles_copy=None):
     block_rows = tiles.shape[2]
     tile_slots = tiles.shape[1]
     me = lax.axis_index("feat")
@@ -34,17 +38,27 @@
     def block_of(index):
         return feats[pl.ds(pl.multiple_of(index * block_rows, block_rows), block_rows), :]
 
+    columns = feats.shape[1]
+    for j, flip in enumerate(flips):
+        rows_out[pl.ds(j * block_rows, block_rows), pl.ds(0, columns)] = block_of(order[0, me ^ flip])
+    if tiles_copy is not None:
+        own = jnp.dot(rows_out[:, pl.ds(0, columns)], weights[pl.ds(0, columns), :], preferred_element_type=jnp.float32)
+        tiles_copy.wait()
     for j, flip in enumerate(flips):
         block = order[0, me ^ flip]
-        mean = jnp.zeros((block_rows, feats.shape[1]), jnp.float32)
+        mean = jnp.zeros((block_rows, columns), jnp.float32)
         for k in range(tile_slots):
             tile = tiles[block, k]
             used = jnp.where(k < tile_count[0, block], tile, jnp.zeros_like(tile))
             mean += jnp.dot(used, block_of(tile_src[k, 0, block]), preferred_element_type=jnp.float32)
-        rows_out[pl.ds(j * block_rows, block_rows), :] = jnp.concatenate(
-            [block_of(block), mean.astype(jnp.bfloat16)], axis=1
+        rows_out[pl.ds(j * block_rows, block_rows), pl.ds(columns, columns)] = mean.astype(jnp.bfloat16)
+    if tiles_copy is not None:
+        sums = own + jnp.dot(
+            rows_out[:, pl.ds(columns, columns)], weights[pl.ds(columns, columns), :], preferred_element_type=jnp.float32
         )
-    sums_out[...] = jnp.dot(rows_out[...], weights[...], preferred_element_type=jnp.float32).astype(sums_out.dtype)
+    else:
+        sums = jnp.dot(rows_out[...], weights[...], preferred_element_type=jnp.float32)
+    sums_out[...] = sums.astype(sums_out.dtype)
 
 
 def load_and_project(
@@ -52,19 +66,21 @@
     rows_out, sums_out, feats, tiles, weights, order, tile_src, tile_count, sems,
 ):
     columns = feats.shape[1]
-    copy_all(
+    copies = start_all(
         (
             (order_hbm, order),
             (tile_src_hbm, tile_src),
             (tile_count_hbm, tile_count),
             (feats_hbm.at[0], feats),
-            (tiles_hbm.at[0], tiles),
             (w_self, weights.at[pl.ds(0, columns)]),
             (w_neigh, weights.at[pl.ds(columns, columns)]),
+            (tiles_hbm.at[0], tiles),
         ),
         sems,
     )
-    project_blocks(flips, order, tile_src, tile_count, feats, tiles, weights, rows_out, sums_out)
+    for copy in copies[:-1]:
+        copy.wait()
+    project_blocks(flips, order, tile_src, tile_count, feats, tiles, weights, rows_out, sums_out, copies[-1])
 
 
 def project_loaded(

time: 33.3 us -> 33.4 us (level)
  no operation moved by 1% of the time
where the time goes in v8:
time: 33.4 us; the launch traced here: 33.2 us
  waiting for transfers between devices  13.7 us (41%)
  starting transfers between devices  13.5 us (40%)
  Pallas kernels  3.63 us (11%)
  other arithmetic  0.9 us (3%)
  local copies, waits for them, and re-layouts  0.74 us (2%)
  between operations  0.73 us (2%)
    ppermute x10, starting transfers between devices, exchange(): return lax.ppermute(value, axis, [(i, i ^ flip) for i in range(size)])  8.85 us
    ppermute x10, waiting for transfers between devices, exchange(): return lax.ppermute(value, axis, [(i, i ^ flip) for i in range(size)])  7.54 us
    ppermute x2, waiting for transfers between devices, body(): got = lax.ppermute(sent, ('feat', 'rep'), pairs)  6.13 us
    ppermute x2, starting transfers between devices, body(): got = lax.ppermute(sent, ('feat', 'rep'), pairs)  4.65 us
    pallas_call x1, Pallas kernels, body(): pl.pallas_call(functools.partial(load_and_project, given_flips), out_shap...  1.86 us
    pallas_call x1, Pallas kernels, body(): pl.pallas_call(functools.partial(project_loaded, kept_flips), out_shape=r...  1.18 us
    slice x1, local copies, waits for them, and re-layouts, body(): return (hidden[None], grads[:columns], grads[columns:])  0.72 us
    broadcast_in_dim x1, other arithmetic, body(): return (hidden[None], grads[:columns], grads[columns:])  0.67 us
  transfers between devices with their start and end apart: 12, of which 9 were waited for; matrix products, arithmetic and copies ran while one was open for 2% of the time, Pallas kernels for 4%

profile of v8, /device:TPU:0, one launch (start us, length us, event | category | flops | bytes accessed | tf_op | source)
XLA Modules:
  0.0 33.2 jit_solution(17274975411285664947)
XLA Ops:
  0.6 1.9 %shard_map.112 = (bf16[512,256]{1,0:T(8,128)(2,1)S(1)}, bf16[512,256]{1,0:T(8,128)(2,1)S(1)}, bf16[2048,128]{1,0:T(8,128)(2,1)S(1)}, bf16[8,3,128,128]{3,2,1,0:T(8,128)(2,1)S(1)}, bf16[256,256]{1,0:T(8,128)(2,1)S(1)}) custom-call(s32[1,8]{1,0:T(1,128)} %order_hbm.3, s32[3,1,8]{2,1,0:T(1,128)} %bitcast.6, s32[1,8]{1,0:T(1,128)} %tile_count_hbm.3, ...), custom_call_target="tpu_custom_call" | custom-call | flops 117440512 | bytes 917504 | tf_op jit(solution)/shard_map/pallas_call | solution.py:143
  2.5 0.5 %collective-permute-start = (bf16[512,256]{1,0:T(8,128)(2,1)S(1)}, bf16[512,256]{1,0:T(8,128)(2,1)S(1)}, u32[]{:S(2)}, u32[]{:S(2)}) collective-permute-start(bf16[512,256]{1,0:T(8,128)(2,1)S(1)} %get-tuple-element.18), channel_id=1, source_target_pairs={{0,4},{4,0},{8,12},{12,8},{16,20},{20,16},{24,28},{28,24},{1,5},{5... | collective-permute-start | bytes 786440 | tf_op jit(solution)/shard_map/ppermute | solution.py:18
  3.0 1.2 %shard_map.113 = (bf16[512,256]{1,0:T(8,128)(2,1)S(1)}, f32[512,256]{1,0:T(8,128)S(1)}) custom-call(s32[1,8]{1,0:T(1,128)} %order_hbm.3, s32[3,1,8]{2,1,0:T(1,128)} %bitcast.7, s32[1,8]{1,0:T(1,128)} %tile_count_hbm.3, bf16[2048,128]{1,0:T(8,128)(2,1)S(1)} %get-tuple-element.14.feats, bf16[8,3,128,128]{3,2,1,0:T(8,128)(2,1)S(1)} %get-tuple-element.15.tiles, ...), custom_call_target="tpu_custom_call" | custom-call | flops 117440512 | bytes 917504 | tf_op jit(solution)/shard_map/pallas_call | solution.py:157
  4.3 2.7 %collective-permute-start.1 = (bf16[128,256]{1,0:T(8,128)(2,1)S(1)}, bf16[128,256]{1,0:T(8,128)(2,1)S(1)}, u32[]{:S(2)}, u32[]{:S(2)}) collective-permute-start(bf16[128,256]{1,0:T(8,128)(2,1)S(1)} %get-tuple-element.31), channel_id=1, source_target_pairs={{0,20},{4,16},{8,28},{12,24},{16,4},{20,0},{24,12},{28,8},{1,21},{... | collective-permute-start | bytes 196616 | tf_op jit(solution)/shard_map/ppermute | solution.py:18
  7.0 1.4 %collective-permute-start.3 = (bf16[128,256]{1,0:T(8,128)(2,1)S(1)}, bf16[128,256]{1,0:T(8,128)(2,1)S(1)}, u32[]{:S(2)}, u32[]{:S(2)}) collective-permute-start(bf16[128,256]{1,0:T(8,128)(2,1)S(1)} %get-tuple-element.32), channel_id=1, source_target_pairs={{0,28},{4,24},{8,20},{12,16},{16,12},{20,8},{24,4},{28,0},{1,29},{... | collective-permute-start | bytes 196616 | tf_op jit(solution)/shard_map/ppermute | solution.py:18
  8.5 2.1 %collective-permute-done.1 = bf16[128,256]{1,0:T(8,128)(2,1)S(1)} collective-permute-done((bf16[128,256]{1,0:T(8,128)(2,1)S(1)}, bf16[128,256]{1,0:T(8,128)(2,1)S(1)}, u32[]{:S(2)}, u32[]{:S(2)}) %collective-permute-start.1) | collective-permute-done | bytes 65568 | tf_op jit(solution)/shard_map/ppermute | solution.py:18
  10.6 1.3 %collective-permute-done.3 = bf16[128,256]{1,0:T(8,128)(2,1)S(1)} collective-permute-done((bf16[128,256]{1,0:T(8,128)(2,1)S(1)}, bf16[128,256]{1,0:T(8,128)(2,1)S(1)}, u32[]{:S(2)}, u32[]{:S(2)}) %collective-permute-start.3) | collective-permute-done | bytes 65568 | tf_op jit(solution)/shard_map/ppermute | solution.py:18
  11.9 0.6 %collective-permute-done.2 = bf16[128,256]{1,0:T(8,128)(2,1)S(1)} collective-permute-done((bf16[128,256]{1,0:T(8,128)(2,1)S(1)}, bf16[128,256]{1,0:T(8,128)(2,1)S(1)}, u32[]{:S(2)}, u32[]{:S(2)}) %collective-permute-start.2) | collective-permute-done | bytes 65568 | tf_op jit(solution)/shard_map/ppermute | solution.py:18
  12.6 1.3 %collective-permute-start.5 = (bf16[128,256]{1,0:T(8,128)(2,1)S(1)}, bf16[128,256]{1,0:T(8,128)(2,1)S(1)}, u32[]{:S(2)}, u32[]{:S(2)}) collective-permute-start(bf16[128,256]{1,0:T(8,128)(2,1)S(1)} %get-tuple-element.22.own), channel_id=1, source_target_pairs={{0,20},{4,16},{8,28},{12,24},{16,4},{20,0},{24,12},{28,8},{1,21},{... | collective-permute-start | bytes 196616 | tf_op jit(solution)/shard_map/ppermute | solution.py:18
  13.9 1.3 %collective-permute-start.4 = (bf16[128,256]{1,0:T(8,128)(2,1)S(1)}, bf16[128,256]{1,0:T(8,128)(2,1)S(1)}, u32[]{:S(2)}, u32[]{:S(2)}) collective-permute-start(bf16[128,256]{1,0:T(8,128)(2,1)S(1)} %get-tuple-element.22.own), channel_id=1, source_target_pairs={{0,28},{4,24},{8,20},{12,16},{16,12},{20,8},{24,4},{28,0},{1,29},{... | collective-permute-start | bytes 196616 | tf_op jit(solution)/shard_map/ppermute | solution.py:18
  15.2 0.4 %collective-permute-start.7 = (bf16[128,256]{1,0:T(8,128)(2,1)S(1)}, bf16[128,256]{1,0:T(8,128)(2,1)S(1)}, u32[]{:S(2)}, u32[]{:S(2)}) collective-permute-start(bf16[128,256]{1,0:T(8,128)(2,1)S(1)} %get-tuple-element.22.own), channel_id=1, source_target_pairs={{0,12},{4,8},{8,4},{12,0},{16,28},{20,24},{24,20},{28,16},{1,13},{... | collective-permute-start | bytes 196616 | tf_op jit(solution)/shard_map/ppermute | solution.py:18
  15.6 0.4 %collective-permute-start.6 = (bf16[128,256]{1,0:T(8,128)(2,1)S(1)}, bf16[128,256]{1,0:T(8,128)(2,1)S(1)}, u32[]{:S(2)}, u32[]{:S(2)}) collective-permute-start(bf16[128,256]{1,0:T(8,128)(2,1)S(1)} %get-tuple-element.22.own), channel_id=1, source_target_pairs={{0,4},{4,0},{8,12},{12,8},{16,20},{20,16},{24,28},{28,24},{1,5},{5... | collective-permute-start | bytes 196616 | tf_op jit(solution)/shard_map/ppermute | solution.py:18
  16.0 0.7 %collective-permute-done.5 = bf16[128,256]{1,0:T(8,128)(2,1)S(1)} collective-permute-done((bf16[128,256]{1,0:T(8,128)(2,1)S(1)}, bf16[128,256]{1,0:T(8,128)(2,1)S(1)}, u32[]{:S(2)}, u32[]{:S(2)}) %collective-permute-start.5) | collective-permute-done | bytes 65568 | tf_op jit(solution)/shard_map/ppermute | solution.py:18
  16.8 1.9 %collective-permute-done.4 = bf16[128,256]{1,0:T(8,128)(2,1)S(1)} collective-permute-done((bf16[128,256]{1,0:T(8,128)(2,1)S(1)}, bf16[128,256]{1,0:T(8,128)(2,1)S(1)}, u32[]{:S(2)}, u32[]{:S(2)}) %collective-permute-start.4) | collective-permute-done | bytes 65568 | tf_op jit(solution)/shard_map/ppermute | solution.py:18
  18.7 0.6 %collective-permute-start.9 = (bf16[256,256]{1,0:T(8,128)(2,1)S(1)}, bf16[256,256]{1,0:T(8,128)(2,1)S(1)}, u32[]{:S(2)}, u32[]{:S(2)}) collective-permute-start(bf16[256,256]{1,0:T(8,128)(2,1)S(1)} %pad_maximum_fusion.early), channel_id=1, source_target_pairs={{0,4},{4,0},{8,12},{12,8},{16,20},{20,16},{24,28},{28,24},{1,5},{5... | collective-permute-start | bytes 393224 | tf_op jit(solution)/shard_map/ppermute | solution.py:18
  19.5 0.3 shard_map.114.total
  19.8 0.8 %collective-permute-done.8.others_late = bf16[128,256]{1,0:T(8,128)(2,1)S(1)} collective-permute-done((bf16[128,256]{1,0:T(8,128)(2,1)S(1)}, bf16[128,256]{1,0:T(8,128)(2,1)S(1)}, u32[]{:S(2)}, u32[]{:S(2)}) %collective-permute-start.8) | collective-permute-done | bytes 65568 | tf_op jit(solution)/shard_map/ppermute | solution.py:18
  20.6 0.3 shard_map.115
  20.9 2.7 %collective-permute-start.10 = (bf16[256,256]{1,0:T(8,128)(2,1)S(1)}, bf16[256,256]{1,0:T(8,128)(2,1)S(1)}, u32[]{:S(2)}, u32[]{:S(2)}) collective-permute-start(bf16[256,256]{1,0:T(8,128)(2,1)S(1)} %shard_map.115), channel_id=1, source_target_pairs={{0,2},{1,3},{2,0},{3,1},{4,5},{5,4},{6,7},{7,6},{8,10},{9,11},{10,... | collective-permute-start | bytes 393224 | tf_op jit(solution)/shard_map/ppermute | solution.py:212
  23.6 3.7 %collective-permute-done.10 = bf16[256,256]{1,0:T(8,128)(2,1)S(1)} collective-permute-done((bf16[256,256]{1,0:T(8,128)(2,1)S(1)}, bf16[256,256]{1,0:T(8,128)(2,1)S(1)}, u32[]{:S(2)}, u32[]{:S(2)}) %collective-permute-start.10) | collective-permute-done | bytes 131104 | tf_op jit(solution)/shard_map/ppermute | solution.py:212
  27.3 1.9 %collective-permute-start.11 = (bf16[256,256]{1,0:T(8,128)(2,1)S(1)}, bf16[256,256]{1,0:T(8,128)(2,1)S(1)}, u32[]{:S(2)}, u32[]{:S(2)}) collective-permute-start(bf16[256,256]{1,0:T(8,128)(2,1)S(1)} %add_convert_fusion), channel_id=1, source_target_pairs={{0,1},{1,0},{2,3},{3,2},{4,7},{5,6},{6,5},{7,4},{8,9},{9,8},{10,11... | collective-permute-start | bytes 393224 | tf_op jit(solution)/shard_map/ppermute | solution.py:212
  29.3 0.7 %fusion.5 = bf16[1,128,256]{2,1,0:T(8,128)(2,1)} fusion(f32[128,256]{1,0:T(8,128)S(1)} %get-tuple-element.19), kind=kLoop, calls=%fused_computation.12 | loop fusion | flops 163840 | bytes 196608 | tf_op jit(solution)/shard_map/broadcast_in_dim | solution.py:214
  30.0 2.5 %collective-permute-done.11 = bf16[256,256]{1,0:T(8,128)(2,1)S(1)} collective-permute-done((bf16[256,256]{1,0:T(8,128)(2,1)S(1)}, bf16[256,256]{1,0:T(8,128)(2,1)S(1)}, u32[]{:S(2)}, u32[]{:S(2)}) %collective-permute-start.11) | collective-permute-done | bytes 131104 | tf_op jit(solution)/shard_map/ppermute | solution.py:212
  32.5 0.7 %fusion.8 = (f32[128,256]{1,0:T(8,128)}, f32[128,256]{1,0:T(8,128)}) fusion(f32[256,256]{1,0:T(8,128)S(1)} %convert_add_fusion.1), kind=kLoop, calls=%fused_computation.14 | loop fusion | bytes 524288 | tf_op jit(solution)/shard_map/slice | solution.py:214
  (16 shorter events, 0.6 us)
Async XLA Ops:
  2.5 1.7 %collective-permute-start = (bf16[512,256]{1,0:T(8,128)(2,1)S(1)}, bf16[512,256]{1,0:T(8,128)(2,1)S(1)}, u32[]{:S(2)}, u32[]{:S(2)}) collective-permute-start(bf16[512,256]{1,0:T(8,128)(2,1)S(1)} %get-tuple-element.18), channel_id=1, source_target_pairs={{0,4},{4,0},{8,12},{12,8},{16,20},{20,16},{24,28},{28,24},{1,5},{5... | collective-permute-start | bytes 786440 | tf_op jit(solution)/shard_map/ppermute | solution.py:18
  4.3 8.2 %copy-start = (bf16[1,128,256]{2,1,0:T(8,128)(2,1)S(1)}, bf16[1,128,256]{2,1,0:T(8,128)(2,1)}, u32[]{:S(2)}) copy-start(bf16[1,128,256]{2,1,0:T(8,128)(2,1)} %param.17) | copy-start | bytes 196612
  4.3 6.3 %collective-permute-start.1 = (bf16[128,256]{1,0:T(8,128)(2,1)S(1)}, bf16[128,256]{1,0:T(8,128)(2,1)S(1)}, u32[]{:S(2)}, u32[]{:S(2)}) collective-permute-start(bf16[128,256]{1,0:T(8,128)(2,1)S(1)} %get-tuple-element.31), channel_id=1, source_target_pairs={{0,20},{4,16},{8,28},{12,24},{16,4},{20,0},{24,12},{28,8},{1,21},{... | collective-permute-start | bytes 196616 | tf_op jit(solution)/shard_map/ppermute | solution.py:18
  7.0 4.9 %collective-permute-start.3 = (bf16[128,256]{1,0:T(8,128)(2,1)S(1)}, bf16[128,256]{1,0:T(8,128)(2,1)S(1)}, u32[]{:S(2)}, u32[]{:S(2)}) collective-permute-start(bf16[128,256]{1,0:T(8,128)(2,1)S(1)} %get-tuple-element.32), channel_id=1, source_target_pairs={{0,28},{4,24},{8,20},{12,16},{16,12},{20,8},{24,4},{28,0},{1,29},{... | collective-permute-start | bytes 196616 | tf_op jit(solution)/shard_map/ppermute | solution.py:18
  8.4 4.1 %copy-start.1 = (f32[256]{0:T(256)S(1)}, f32[256]{0:T(256)}, u32[]{:S(2)}) copy-start(f32[256]{0:T(256)} %param.12) | copy-start | bytes 3076
  8.4 4.1 %collective-permute-start.2 = (bf16[128,256]{1,0:T(8,128)(2,1)S(1)}, bf16[128,256]{1,0:T(8,128)(2,1)S(1)}, u32[]{:S(2)}, u32[]{:S(2)}) collective-permute-start(bf16[128,256]{1,0:T(8,128)(2,1)S(1)} %get-tuple-element.33), channel_id=1, source_target_pairs={{0,12},{4,8},{8,4},{12,0},{16,28},{20,24},{24,20},{28,16},{1,13},{... | collective-permute-start | bytes 196616 | tf_op jit(solution)/shard_map/ppermute | solution.py:18
  12.6 4.2 %collective-permute-start.5 = (bf16[128,256]{1,0:T(8,128)(2,1)S(1)}, bf16[128,256]{1,0:T(8,128)(2,1)S(1)}, u32[]{:S(2)}, u32[]{:S(2)}) collective-permute-start(bf16[128,256]{1,0:T(8,128)(2,1)S(1)} %get-tuple-element.22.own), channel_id=1, source_target_pairs={{0,20},{4,16},{8,28},{12,24},{16,4},{20,0},{24,12},{28,8},{1,21},{... | collective-permute-start | bytes 196616 | tf_op jit(solution)/shard_map/ppermute | solution.py:18
  13.9 4.7 %collective-permute-start.4 = (bf16[128,256]{1,0:T(8,128)(2,1)S(1)}, bf16[128,256]{1,0:T(8,128)(2,1)S(1)}, u32[]{:S(2)}, u32[]{:S(2)}) collective-permute-start(bf16[128,256]{1,0:T(8,128)(2,1)S(1)} %get-tuple-element.22.own), channel_id=1, source_target_pairs={{0,28},{4,24},{8,20},{12,16},{16,12},{20,8},{24,4},{28,0},{1,29},{... | collective-permute-start | bytes 196616 | tf_op jit(solution)/shard_map/ppermute | solution.py:18
  15.2 4.2 %collective-permute-start.7 = (bf16[128,256]{1,0:T(8,128)(2,1)S(1)}, bf16[128,256]{1,0:T(8,128)(2,1)S(1)}, u32[]{:S(2)}, u32[]{:S(2)}) collective-permute-start(bf16[128,256]{1,0:T(8,128)(2,1)S(1)} %get-tuple-element.22.own), channel_id=1, source_target_pairs={{0,12},{4,8},{8,4},{12,0},{16,28},{20,24},{24,20},{28,16},{1,13},{... | collective-permute-start | bytes 196616 | tf_op jit(solution)/shard_map/ppermute | solution.py:18
  15.6 3.1 %collective-permute-start.6 = (bf16[128,256]{1,0:T(8,128)(2,1)S(1)}, bf16[128,256]{1,0:T(8,128)(2,1)S(1)}, u32[]{:S(2)}, u32[]{:S(2)}) collective-permute-start(bf16[128,256]{1,0:T(8,128)(2,1)S(1)} %get-tuple-element.22.own), channel_id=1, source_target_pairs={{0,4},{4,0},{8,12},{12,8},{16,20},{20,16},{24,28},{28,24},{1,5},{5... | collective-permute-start | bytes 196616 | tf_op jit(solution)/shard_map/ppermute | solution.py:18
  18.7 1.9 %collective-permute-start.9 = (bf16[256,256]{1,0:T(8,128)(2,1)S(1)}, bf16[256,256]{1,0:T(8,128)(2,1)S(1)}, u32[]{:S(2)}, u32[]{:S(2)}) collective-permute-start(bf16[256,256]{1,0:T(8,128)(2,1)S(1)} %pad_maximum_fusion.early), channel_id=1, source_target_pairs={{0,4},{4,0},{8,12},{12,8},{16,20},{20,16},{24,28},{28,24},{1,5},{5... | collective-permute-start | bytes 393224 | tf_op jit(solution)/shard_map/ppermute | solution.py:18
  19.4 1.3 %collective-permute-start.8 = (bf16[128,256]{1,0:T(8,128)(2,1)S(1)}, bf16[128,256]{1,0:T(8,128)(2,1)S(1)}, u32[]{:S(2)}, u32[]{:S(2)}) collective-permute-start(bf16[128,256]{1,0:T(8,128)(2,1)S(1)} %collective-permute-done.7.late), channel_id=1, source_target_pairs={{0,4},{4,0},{8,12},{12,8},{16,20},{20,16},{24,28},{28,24},{1,5},{5... | collective-permute-start | bytes 196616 | tf_op jit(solution)/shard_map/ppermute | solution.py:18
  20.9 6.4 %collective-permute-start.10 = (bf16[256,256]{1,0:T(8,128)(2,1)S(1)}, bf16[256,256]{1,0:T(8,128)(2,1)S(1)}, u32[]{:S(2)}, u32[]{:S(2)}) collective-permute-start(bf16[256,256]{1,0:T(8,128)(2,1)S(1)} %shard_map.115), channel_id=1, source_target_pairs={{0,2},{1,3},{2,0},{3,1},{4,5},{5,4},{6,7},{7,6},{8,10},{9,11},{10,... | collective-permute-start | bytes 393224 | tf_op jit(solution)/shard_map/ppermute | solution.py:212
  27.3 5.1 %collective-permute-start.11 = (bf16[256,256]{1,0:T(8,128)(2,1)S(1)}, bf16[256,256]{1,0:T(8,128)(2,1)S(1)}, u32[]{:S(2)}, u32[]{:S(2)}) collective-permute-start(bf16[256,256]{1,0:T(8,128)(2,1)S(1)} %add_convert_fusion), channel_id=1, source_target_pairs={{0,1},{1,0},{2,3},{3,2},{4,7},{5,6},{6,5},{7,4},{8,9},{9,8},{10,11... | collective-permute-start | bytes 393224 | tf_op jit(solution)/shard_map/ppermute | solution.py:212
